TPU v7x, 256 devices: a whole 4x4x8 slice. The times are simulated.
256 devices in a mesh: expert: 32 (over x, z), dp: 8 (over y, core).
Axes of the slice: x: 4, y: 4, z: 8, core: 2. Of those that a mesh axis runs over, the one named last changes fastest.
Arguments:
- tokens: bfloat16 [8192, 2048], P('expert'), may hold values from -6 to 6
- cotangent: bfloat16 [8192, 2048], P('expert'), may hold values from -6 to 6
- expert_route: int32 [8192, 1], P('expert'), may hold values from 0 to 31; in each aligned block of 256 rows (0 to 255, 256 to 511, ...) at most 16 rows name the same one
- w_gate: bfloat16 [32, 2048, 7168], P('expert', None, 'dp'), may hold values from -0.125 to 0.125
- w_up: bfloat16 [32, 2048, 7168], P('expert', None, 'dp'), may hold values from -0.125 to 0.125
- w_down: bfloat16 [32, 7168, 2048], P('expert', 'dp'), may hold values from -0.0625 to 0.0625
- sign_seeds: int32 [32], P('expert'), may hold values from 0 to 65535
Outputs:
- tangent_grad: bfloat16 [8192, 2048], P('expert')
- curvature: float32 [32, 7168], P('expert', 'dp')
Inputs may be any that keep to these rules, and one draw needn't show every extreme that they name: `expert_route`: among the tokens of one index of expert no expert is named more than 16 times, and in some index one expert is named exactly 16 times; every expert is named by some token.
All inputs are finite; a program needn't handle non-finite values.
Results may differ from a plain program's by a relative error of at most 0.005.
Values may be sent and summed in bfloat16 or wider, within the bound.
No kernel may reach another device: no remote copies, remote signals or barrier semaphores. Data moves between devices by JAX's collectives and lax.ppermute only.
A program may use at most 64 MiB of HBM per device.

v0:
```python
import math

import jax
import jax.numpy as jnp
from jax import lax
from jax.sharding import PartitionSpec as P


def mix_bits(row_index, col_index, seed_value):
    mixed = (
        row_index * jnp.int32(73856093)
        + col_index * jnp.int32(19349663)
        + seed_value * jnp.int32(83492791)
    )
    mixed = mixed ^ mixed >> 15
    mixed = mixed * jnp.int32(735632791)
    mixed = mixed ^ mixed >> 13
    mixed = mixed * jnp.int32(1274126177)
    mixed = mixed ^ mixed >> 16
    return mixed >> 5 & 1


def sign_table(row_index, col_index, seed_value, model_width):
    bits = mix_bits(row_index, col_index, seed_value)
    scale = jnp.asarray(1.0 / math.sqrt(model_width), jnp.bfloat16)
    return jnp.where(bits == 1, scale, -scale)


def silu_slopes(pre_act):
    sigmoid_pre = jax.nn.sigmoid(pre_act)
    slope_one = sigmoid_pre * (1.0 + pre_act * (1.0 - sigmoid_pre))
    slope_two = sigmoid_pre * (1.0 - sigmoid_pre) * (2.0 + pre_act * (1.0 - 2.0 * sigmoid_pre))
    return (slope_one, slope_two)


def expert_rows(rows_x, rows_cot, gate_mat, up_mat, down_mat, sign_values):
    contract = (((1,), (1,)), ((), ()))
    gate_pre = jnp.dot(rows_x, gate_mat, preferred_element_type=jnp.float32)
    up_pre = jnp.dot(rows_x, up_mat, preferred_element_type=jnp.float32)
    gate_tangent = jnp.dot(rows_x, sign_values, preferred_element_type=jnp.float32)
    hidden_grad = lax.dot_general(rows_cot, down_mat, contract, preferred_element_type=jnp.float32)
    slope_one, slope_two = silu_slopes(gate_pre)
    grad_gate = (hidden_grad * up_pre * slope_one).astype(jnp.bfloat16)
    tangent_gate = hidden_grad * up_pre * slope_two * gate_tangent
    tangent_up = (hidden_grad * slope_one * gate_tangent).astype(jnp.bfloat16)
    curvature = jnp.sum(gate_tangent * tangent_gate, axis=0)
    tangent_grads = lax.dot_general(
        tangent_gate.astype(jnp.bfloat16), gate_mat, contract, preferred_element_type=jnp.float32
    )
    tangent_grads = tangent_grads + lax.dot_general(
        tangent_up, up_mat, contract, preferred_element_type=jnp.float32
    )
    tangent_grads = tangent_grads + lax.dot_general(
        grad_gate, sign_values, contract, preferred_element_type=jnp.float32
    )
    return (tangent_grads, curvature)


def dispatch_matrix(route_flat, expert_count, slot_count):
    expert_ids = jnp.arange(expert_count, dtype=jnp.int32)
    onehot = (route_flat[:, None] == expert_ids[None, :]).astype(jnp.int32)
    slot_place = jnp.sum(jnp.cumsum(onehot, axis=0) * onehot, axis=1) - 1
    target = route_flat * slot_count + slot_place
    slot_ids = jnp.arange(expert_count * slot_count, dtype=jnp.int32)
    return (slot_ids[:, None] == target[None, :]).astype(jnp.bfloat16)


def body(tokens, cotangent, expert_route, w_gate, w_up, w_down, sign_seeds):
    expert_count = lax.axis_size("expert")
    tok_count = tokens.shape[0]
    model_width = tokens.shape[1]
    hidden_cols = w_gate.shape[2]
    slot_count = max(2, 2 * tok_count // expert_count)
    offset = lax.axis_index("dp") * hidden_cols
    row_index = jnp.arange(model_width, dtype=jnp.int32)[:, None]
    col_index = offset + jnp.arange(hidden_cols, dtype=jnp.int32)[None, :]
    sign_values = sign_table(row_index, col_index, sign_seeds[0], model_width)
    own_dispatch = dispatch_matrix(expert_route[:, 0], expert_count, slot_count)
    send_x = (
        jnp.dot(own_dispatch, tokens, preferred_element_type=jnp.float32)
        .astype(jnp.bfloat16)
        .reshape(expert_count, slot_count, model_width)
    )
    send_cot = (
        jnp.dot(own_dispatch, cotangent, preferred_element_type=jnp.float32)
        .astype(jnp.bfloat16)
        .reshape(expert_count, slot_count, model_width)
    )
    received_x, received_cot = (
        lax.all_to_all(send_x, "expert", split_axis=0, concat_axis=0, tiled=True),
        lax.all_to_all(send_cot, "expert", split_axis=0, concat_axis=0, tiled=True),
    )
    tangent_grads, curvature = expert_rows(
        received_x.reshape(-1, model_width),
        received_cot.reshape(-1, model_width),
        w_gate[0],
        w_up[0],
        w_down[0],
        sign_values,
    )
    partial_value = tangent_grads.reshape(expert_count, slot_count, model_width)
    contract = (((0,), (0,)), ((), ()))
    summed = lax.psum(partial_value, "dp")
    own_rows = summed.astype(jnp.bfloat16)
    returned = lax.all_to_all(own_rows, "expert", split_axis=0, concat_axis=0, tiled=True)
    combined = lax.dot_general(
        own_dispatch,
        returned.reshape(expert_count * slot_count, model_width),
        contract,
        preferred_element_type=jnp.float32,
    )
    result = combined.astype(jnp.bfloat16)
    return (result, curvature[None, :])


def solution(mesh):
    in_specs = (
        P("expert", None),
        P("expert", None),
        P("expert", None),
        P("expert", None, "dp"),
        P("expert", None, "dp"),
        P("expert", "dp", None),
        P("expert"),
    )
    out_specs = (P("expert", None), P("expert", "dp"))
    return jax.shard_map(body, mesh=mesh, in_specs=in_specs, out_specs=out_specs, check_vma=False)
```

profile of v0, /device:TPU:1, one launch (start us, length us, event | category | flops | bytes accessed | tf_op | source)
XLA Modules:
  0.0 261.5 jit_solution(6124889449063517323)
XLA Ops:
  0.6 0.0 copy-start
  0.6 0.8 fusion.33
  1.4 0.6 reduce-window.6
  2.0 0.2 slice_reduce_fusion
  2.2 0.8 fusion.32
  3.0 0.7 add_add_fusion.1
  3.7 0.0 copy-done
  3.7 2.0 convolution_convert_fusion
  5.7 11.9 %all-to-all-start.1 = ((bf16[32,16,2048]{2,1,0:T(8,128)(2,1)}), bf16[32,16,2048]{2,1,0:T(8,128)(2,1)S(1)}, u32[]{:S(2)}, u32[]{:S(2)}) async-start(bf16[32,16,2048]{2,1,0:T(8,128)(2,1)} %bitcast.6), calls=%async_computation.1 | async-start | bytes 4194304 | tf_op jit(solution)/shard_map/all_to_all | solution.py:90
  17.6 3.3 %convolution_convert_fusion.1 = bf16[512,2048]{1,0:T(8,128)(2,1)} fusion(bf16[256,2048]{1,0:T(8,128)(2,1)} %param.8, s32[256]{0:T(256)S(1)} %add_add_fusion.1), kind=kOutput, calls=%fused_computation.21 | convolution fusion | flops 538050560 | bytes 3146752 | tf_op jit(solution)/shard_map/dot_general | solution.py:85
  20.9 45.6 %all-to-all-done.1 = bf16[32,16,2048]{2,1,0:T(8,128)(2,1)S(1)} async-done(((bf16[32,16,2048]{2,1,0:T(8,128)(2,1)}), bf16[32,16,2048]{2,1,0:T(8,128)(2,1)S(1)}, u32[]{:S(2)}, u32[]{:S(2)}) %all-to-all-start.1) | async-done | bytes 2097184 | tf_op jit(solution)/shard_map/all_to_all | solution.py:90
  66.5 7.3 %all-to-all-start = ((bf16[32,16,2048]{2,1,0:T(8,128)(2,1)}), bf16[32,16,2048]{2,1,0:T(8,128)(2,1)}, u32[]{:S(2)}, u32[]{:S(2)}) async-start(bf16[32,16,2048]{2,1,0:T(8,128)(2,1)} %bitcast.3), calls=%async_computation | async-start | bytes 4194304 | tf_op jit(solution)/shard_map/all_to_all | solution.py:91
  74.5 5.6 %fusion.8 = f32[512,896]{1,0:T(8,128)} fusion(bf16[512,2048]{1,0:T(8,128)(2,1)S(1)} %bitcast.48, bf16[1,2048,896]{2,1,0:T(8,128)(2,1)} %param.10), kind=kOutput, calls=%fused_computation.12 | convolution fusion | flops 1879048192 | bytes 7602176 | tf_op jit(solution)/shard_map/dot_general | solution.py:38
  80.1 42.1 %all-to-all-done = bf16[32,16,2048]{2,1,0:T(8,128)(2,1)} async-done(((bf16[32,16,2048]{2,1,0:T(8,128)(2,1)}), bf16[32,16,2048]{2,1,0:T(8,128)(2,1)}, u32[]{:S(2)}, u32[]{:S(2)}) %all-to-all-start) | async-done | bytes 2097184 | tf_op jit(solution)/shard_map/all_to_all | solution.py:91
  122.2 0.0 copy-start.1
  122.2 5.2 %fusion.14 = f32[512,896]{1,0:T(8,128)S(1)} fusion(bf16[512,2048]{1,0:T(8,128)(2,1)} %bitcast.4, bf16[1,896,2048]{2,1,0:T(8,128)(2,1)} %param.12), kind=kOutput, calls=%fused_computation.18 | convolution fusion | flops 1879048192 | bytes 7602176 | tf_op jit(solution)/shard_map/dot_general | solution.py:41
  127.4 0.0 copy-done.1
  127.4 0.0 copy-start.3
  127.4 2.3 fusion.24
  129.8 0.0 copy-done.3
  129.8 5.0 %multiply_reduce_fusion = (f32[896]{0:T(1024)S(1)}, f32[512,896]{1,0:T(8,128)S(1)}) fusion(f32[512,896]{1,0:T(8,128)S(1)} %fusion.24, f32[512,896]{1,0:T(8,128)S(1)} %copy-done.3, bf16[512,2048]{1,0:T(8,128)(2,1)S(1)} %bitcast.50, s32[]{:T(128)} %bitcast.10, s32[896]{0:T(1024)S(1)} %add_multiply_fusion, s32[2048]{0:T(1024)S(1)} %iota_multiply_fusion), kind=kOutput, calls=%fused_computation.30 | convolution fusion | flops 1911159936 | bytes 7617540 | tf_op jit(solution)/shard_map/dot_general | solution.py:40
  134.8 0.0 copy-start.2
  134.9 2.8 %fusion.10 = f32[512,2048]{1,0:T(8,128)S(1)} fusion(bf16[1,2048,896]{2,1,0:T(8,128)(2,1)S(1)} %copy-done.1, f32[512,896]{1,0:T(8,128)S(1)} %get-tuple-element.3, f32[512,896]{1,0:T(8,128)S(1)} %fusion.14, f32[512,896]{1,0:T(8,128)S(1)} %copy-done.3), kind=kOutput, calls=%fused_computation.14 | convolution fusion | flops 1883635712 | bytes 13369344 | tf_op jit(solution)/shard_map/dot_general | solution.py:50
  137.7 0.0 copy-done.2
  137.7 3.3 %fusion.6 = f32[512,2048]{1,0:T(8,128)S(1)} fusion(bf16[1,2048,896]{2,1,0:T(8,128)(2,1)S(1)} %copy-done.2, f32[512,896]{1,0:T(8,128)S(1)} %get-tuple-element.3, f32[512,896]{1,0:T(8,128)S(1)} %fusion.24, f32[512,896]{1,0:T(8,128)S(1)} %copy-done.3), kind=kOutput, calls=%fused_computation.10 | convolution fusion | flops 1885011968 | bytes 13369344 | tf_op jit(solution)/shard_map/dot_general | solution.py:47
  140.9 7.1 %add_add_fusion = f32[512,2048]{1,0:T(8,128)} fusion(f32[512,2048]{1,0:T(8,128)S(1)} %fusion.6, f32[512,2048]{1,0:T(8,128)S(1)} %fusion.10, s32[]{:T(128)} %bitcast.10, s32[896]{0:T(1024)S(1)} %add_multiply_fusion, s32[2048]{0:T(1024)S(1)} %iota_multiply_fusion, f32[512,896]{1,0:T(8,128)S(1)} %fusion.24, f32[512,896]{1,0:T(8,128)S(1)} %copy-done.3), kind=kOutput, calls=%fused_computation.9 | convolution fusion | flops 1910964224 | bytes 16264708 | tf_op jit(solution)/shard_map/dot_general | solution.py:53
  148.0 58.0 %all-reduce.1 = bf16[32,16,2048]{2,1,0:T(8,128)(2,1)} all-reduce(f32[32,16,2048]{2,1,0:T(8,128)} %bitcast.47), channel_id=1, replica_groups=mesh['expert'=32,'dp'=8] {'dp'}, use_global_device_ids=true, to_apply=%region_3.4 | all-reduce | flops 1048576 | bytes 6291456 | tf_op jit(solution)/shard_map/psum | solution.py:103
  206.0 5.8 %all-to-all-start.2 = ((bf16[32,16,2048]{2,1,0:T(8,128)(2,1)}), bf16[32,16,2048]{2,1,0:T(8,128)(2,1)S(1)}, u32[]{:S(2)}, u32[]{:S(2)}) async-start(bf16[32,16,2048]{2,1,0:T(8,128)(2,1)} %all-reduce.1), calls=%async_computation.2 | async-start | bytes 4194304 | tf_op jit(solution)/shard_map/all_to_all | solution.py:105
  211.8 0.6 broadcast_in_dim.18
  212.4 47.3 %all-to-all-done.2 = bf16[32,16,2048]{2,1,0:T(8,128)(2,1)S(1)} async-done(((bf16[32,16,2048]{2,1,0:T(8,128)(2,1)}), bf16[32,16,2048]{2,1,0:T(8,128)(2,1)S(1)}, u32[]{:S(2)}, u32[]{:S(2)}) %all-to-all-start.2) | async-done | bytes 2097184 | tf_op jit(solution)/shard_map/all_to_all | solution.py:105
  259.7 1.7 convolution_convert_fusion.2
  (4 shorter events, 0.1 us)
Async XLA Ops:
  0.6 3.1 %copy-start = (bf16[256,2048]{1,0:T(8,128)(2,1)S(1)}, bf16[256,2048]{1,0:T(8,128)(2,1)}, u32[]{:S(2)}) copy-start(bf16[256,2048]{1,0:T(8,128)(2,1)} %param.7) | copy-start | bytes 3145732
  5.7 60.8 %all-to-all-start.1 = ((bf16[32,16,2048]{2,1,0:T(8,128)(2,1)}), bf16[32,16,2048]{2,1,0:T(8,128)(2,1)S(1)}, u32[]{:S(2)}, u32[]{:S(2)}) async-start(bf16[32,16,2048]{2,1,0:T(8,128)(2,1)} %bitcast.6), calls=%async_computation.1 | async-start | bytes 4194304 | tf_op jit(solution)/shard_map/all_to_all | solution.py:90
  66.5 55.8 %all-to-all-start = ((bf16[32,16,2048]{2,1,0:T(8,128)(2,1)}), bf16[32,16,2048]{2,1,0:T(8,128)(2,1)}, u32[]{:S(2)}, u32[]{:S(2)}) async-start(bf16[32,16,2048]{2,1,0:T(8,128)(2,1)} %bitcast.3), calls=%async_computation | async-start | bytes 4194304 | tf_op jit(solution)/shard_map/all_to_all | solution.py:91
  122.2 5.2 %copy-start.1 = (bf16[1,2048,896]{2,1,0:T(8,128)(2,1)S(1)}, bf16[1,2048,896]{2,1,0:T(8,128)(2,1)}, u32[]{:S(2)}) copy-start(bf16[1,2048,896]{2,1,0:T(8,128)(2,1)} %param.11) | copy-start | bytes 11010052
  127.4 2.4 copy-start.3
  134.8 2.8 %copy-start.2 = (bf16[1,2048,896]{2,1,0:T(8,128)(2,1)S(1)}, bf16[1,2048,896]{2,1,0:T(8,128)(2,1)}, u32[]{:S(2)}) copy-start(bf16[1,2048,896]{2,1,0:T(8,128)(2,1)} %param.10) | copy-start | bytes 11010052
  206.0 53.8 %all-to-all-start.2 = ((bf16[32,16,2048]{2,1,0:T(8,128)(2,1)}), bf16[32,16,2048]{2,1,0:T(8,128)(2,1)S(1)}, u32[]{:S(2)}, u32[]{:S(2)}) async-start(bf16[32,16,2048]{2,1,0:T(8,128)(2,1)} %all-reduce.1), calls=%async_computation.2 | async-start | bytes 4194304 | tf_op jit(solution)/shard_map/all_to_all | solution.py:105
where the time goes:
time: 264 us; the launch traced here: 261 us
  waiting for transfers between devices  135 us (51%)
  blocking collectives  58 us (22%)
  matrix products  38.3 us (15%)
  starting transfers between devices  25 us (9%)
  other arithmetic  2.85 us (1%)
    psum x1, blocking collectives, body(): summed = lax.psum(partial_value, 'dp')  58 us
    all_to_all x1, waiting for transfers between devices, body(): lax.all_to_all(own_rows, 'expert', split_axis=0, concat_axis=0, tiled=True)  47.3 us
    all_to_all x1, waiting for transfers between devices, body(): lax.all_to_all(send_x, 'expert', split_axis=0, concat_axis=0, tiled=True)  45.6 us
    all_to_all x1, waiting for transfers between devices, body(): lax.all_to_all(send_cot, 'expert', split_axis=0, concat_axis=0, tiled=True)  42.1 us
    all_to_all x1, starting transfers between devices, body(): lax.all_to_all(send_x, 'expert', split_axis=0, concat_axis=0, tiled=True)  11.9 us
    all_to_all x1, starting transfers between devices, body(): lax.all_to_all(send_cot, 'expert', split_axis=0, concat_axis=0, tiled=True)  7.31 us
    dot_general x1, matrix products, expert_rows(): lax.dot_general(grad_gate, sign_values, contract, preferred_element_type=...  7.05 us
    all_to_all x1, starting transfers between devices, body(): lax.all_to_all(own_rows, 'expert', split_axis=0, concat_axis=0, tiled=True)  5.84 us
  transfers between devices with their start and end apart: 3, of which 3 were waited for; matrix products, arithmetic and copies ran while one was open for 4% of the time, Pallas kernels for 0%

commit v1 on v0

v1 whole, which is shorter than its diff:
```python
import math

import jax
import jax.numpy as jnp
from jax import lax
from jax.sharding import Mesh, PartitionSpec as P

EXPERT = ("x", "z")
SWAP = [(0, 1), (1, 0)]


def mix_bits(row_index, col_index, seed_value):
    mixed = (
        row_index * jnp.int32(73856093)
        + col_index * jnp.int32(19349663)
        + seed_value * jnp.int32(83492791)
    )
    mixed = mixed ^ mixed >> 15
    mixed = mixed * jnp.int32(735632791)
    mixed = mixed ^ mixed >> 13
    mixed = mixed * jnp.int32(1274126177)
    mixed = mixed ^ mixed >> 16
    return mixed >> 5 & 1


def sign_table(row_index, col_index, seed_value, model_width):
    bits = mix_bits(row_index, col_index, seed_value)
    scale = jnp.asarray(1.0 / math.sqrt(model_width), jnp.bfloat16)
    return jnp.where(bits == 1, scale, -scale)


def silu_slopes(pre_act):
    sigmoid_pre = jax.nn.sigmoid(pre_act)
    slope_one = sigmoid_pre * (1.0 + pre_act * (1.0 - sigmoid_pre))
    slope_two = sigmoid_pre * (1.0 - sigmoid_pre) * (2.0 + pre_act * (1.0 - 2.0 * sigmoid_pre))
    return (slope_one, slope_two)


def expert_rows(rows_x, rows_cot, gate_mat, up_mat, down_mat, sign_values):
    contract = (((1,), (1,)), ((), ()))
    gate_pre = jnp.dot(rows_x, gate_mat, preferred_element_type=jnp.float32)
    up_pre = jnp.dot(rows_x, up_mat, preferred_element_type=jnp.float32)
    gate_tangent = jnp.dot(rows_x, sign_values, preferred_element_type=jnp.float32)
    hidden_grad = lax.dot_general(rows_cot, down_mat, contract, preferred_element_type=jnp.float32)
    slope_one, slope_two = silu_slopes(gate_pre)
    grad_gate = (hidden_grad * up_pre * slope_one).astype(jnp.bfloat16)
    tangent_gate = hidden_grad * up_pre * slope_two * gate_tangent
    tangent_up = (hidden_grad * slope_one * gate_tangent).astype(jnp.bfloat16)
    curvature = jnp.sum(gate_tangent * tangent_gate, axis=0)
    tangent_grads = lax.dot_general(
        tangent_gate.astype(jnp.bfloat16), gate_mat, contract, preferred_element_type=jnp.float32
    )
    tangent_grads = tangent_grads + lax.dot_general(
        tangent_up, up_mat, contract, preferred_element_type=jnp.float32
    )
    tangent_grads = tangent_grads + lax.dot_general(
        grad_gate, sign_values, contract, preferred_element_type=jnp.float32
    )
    return (tangent_grads, curvature)


def dispatch_matrix(route_flat, expert_count, slot_count):
    tok_count = route_flat.shape[0]
    place = jnp.arange(tok_count, dtype=jnp.int32)
    earlier = (route_flat[:, None] == route_flat[None, :]) & (place[:, None] < place[None, :])
    slot_place = jnp.sum(earlier.astype(jnp.int32), axis=0)
    target = route_flat * slot_count + slot_place
    slot_ids = jnp.arange(expert_count * slot_count, dtype=jnp.int32)
    return (slot_ids[:, None] == target[None, :]).astype(jnp.bfloat16)


def join_cores(own, core):
    other = lax.ppermute(own, "c", SWAP)
    count = own.shape[0]
    both = jnp.zeros((2 * count,) + own.shape[1:], own.dtype)
    both = lax.dynamic_update_slice_in_dim(both, own, core * count, 0)
    return lax.dynamic_update_slice_in_dim(both, other, (1 - core) * count, 0)


def gather_y(own):
    count = lax.axis_size("y")
    return lax.all_to_all(
        jnp.broadcast_to(own[None], (count,) + own.shape), "y", split_axis=0, concat_axis=0, tiled=True
    )


def body(tokens, cotangent, expert_route, w_gate, w_up, w_down, sign_seeds):
    expert_count = lax.axis_size(EXPERT)
    ys, cores = lax.axis_size("y"), lax.axis_size("c")
    y, core = lax.axis_index("y"), lax.axis_index("c")
    tok_count, model_width = tokens.shape
    hidden_cols = w_gate.shape[2]
    slot_count = max(2, 2 * tok_count // expert_count)
    rows = expert_count * slot_count
    width = model_width // (ys * cores)
    offset = (y * cores + core) * hidden_cols
    row_index = jnp.arange(model_width, dtype=jnp.int32)[:, None]
    col_index = offset + jnp.arange(hidden_cols, dtype=jnp.int32)[None, :]
    sign_values = sign_table(row_index, col_index, sign_seeds[0], model_width)
    dispatch = dispatch_matrix(expert_route[:, 0], expert_count, slot_count)

    start = (core * ys + y) * width
    piece = jnp.concatenate(
        [lax.dynamic_slice_in_dim(a, start, width, 1) for a in (tokens, cotangent)], axis=1
    )
    send = jnp.dot(dispatch, piece, preferred_element_type=jnp.float32).astype(jnp.bfloat16)
    received = lax.all_to_all(
        send.reshape(expert_count, slot_count, 2 * width), EXPERT, split_axis=0, concat_axis=0, tiled=True
    ).reshape(rows, 2 * width)
    blocks = join_cores(gather_y(received), core)
    rows_x = blocks[:, :, :width].transpose(1, 0, 2).reshape(rows, model_width)
    rows_cot = blocks[:, :, width:].transpose(1, 0, 2).reshape(rows, model_width)
    tangent_grads, curvature = expert_rows(
        rows_x, rows_cot, w_gate[0], w_up[0], w_down[0], sign_values
    )

    halves = tangent_grads.reshape(rows, cores, model_width // cores)
    keep = lax.dynamic_slice_in_dim(halves, core, 1, 1)[:, 0]
    give = lax.dynamic_slice_in_dim(halves, 1 - core, 1, 1)[:, 0].astype(jnp.bfloat16)
    pair = keep + lax.ppermute(give, "c", SWAP).astype(jnp.float32)
    parts = pair.astype(jnp.bfloat16).reshape(rows, ys, width).transpose(1, 0, 2)
    parts = lax.all_to_all(parts, "y", split_axis=0, concat_axis=0, tiled=True)
    own_rows = jnp.sum(parts.astype(jnp.float32), axis=0).astype(jnp.bfloat16)
    returned = lax.all_to_all(
        own_rows.reshape(expert_count, slot_count, width), EXPERT, split_axis=0, concat_axis=0, tiled=True
    ).reshape(rows, width)
    combined = lax.dot_general(
        dispatch, returned, (((0,), (0,)), ((), ())), preferred_element_type=jnp.float32
    ).astype(jnp.bfloat16)
    result = join_cores(gather_y(combined), core)
    result = result.transpose(1, 0, 2).reshape(tok_count, model_width)
    return (result, curvature[None, :])


def solution(mesh):
    chips = Mesh(mesh.devices.reshape(4, 8, 4, 2), ("x", "z", "y", "c"))
    expert, dp = EXPERT, ("y", "c")
    in_specs = (
        P(expert, None),
        P(expert, None),
        P(expert, None),
        P(expert, None, dp),
        P(expert, None, dp),
        P(expert, dp, None),
        P(expert),
    )
    out_specs = (P(expert, None), P(expert, dp))
    return jax.shard_map(body, mesh=chips, in_specs=in_specs, out_specs=out_specs, check_vma=False)
```

time: 264 us -> 164 us (0.62)
  waiting for transfers between devices: 135 us -> 2.94 us
  blocking collectives: 58 us -> 96 us
  local copies, waits for them, and re-layouts: 0.79 us -> 24 us
  starting transfers between devices: 25 us -> 10.2 us
  matrix products: 38.3 us -> 26 us
    all_to_all x3 -> x0, waiting for transfers between devices: 135 us -> none  [the longest x1 47.3 us: body(): lax.all_to_all(own_rows, 'expert', split_axis=0, concat_axis=0, tiled=True)]
    all_to_all x0 -> x5, blocking collectives: none -> 96 us  [the longest x2 35.9 us: gather_y(): lax.all_to_all(jnp.broadcast_to(own[None], (count,) + own.shape), 'y', sp...]
    psum x1 -> x0, blocking collectives: 58 us -> none  [body(): summed = lax.psum(partial_value, 'dp')]
    all_to_all x3 -> x0, starting transfers between devices: 25 us -> none  [the longest x1 11.9 us: body(): lax.all_to_all(send_x, 'expert', split_axis=0, concat_axis=0, tiled=True)]
    ppermute x0 -> x3, starting transfers between devices: none -> 10.2 us  [the longest x2 9.51 us: join_cores(): other = lax.ppermute(own, 'c', SWAP)]
    dynamic_slice x0 -> x3, local copies, waits for them, and re-layouts: none -> 9.05 us  [the longest x1 4.08 us: body(): lax.dynamic_slice_in_dim(halves, 1 - core, 1, 1)[:, 0].astype(jnp.bfloat16)]
    reshape x0 -> x2, local copies, waits for them, and re-layouts: none -> 6.66 us  [the longest x1 6.59 us: body(): halves = tangent_grads.reshape(rows, cores, model_width // cores)]
    dot_general x3 -> x2, matrix products: 7.05 us -> 0.65 us  [the longest x1 0.35 us: body(): lax.dot_general(dispatch, returned, (((0,), (0,)), ((), ())), preferred_e...]
  transfers between devices with their start and end apart: 3 -> 3, of which waited for: 3 -> 2; matrix products, arithmetic and copies ran while one was open for 4% -> 4% of each run, Pallas kernels for 0% -> 0%
where the time goes in v1:
time: 164 us; the launch traced here: 163 us
  blocking collectives  96 us (59%)
  matrix products  26 us (16%)
  local copies, waits for them, and re-layouts  24 us (15%)
  starting transfers between devices  10.2 us (6%)
  waiting for transfers between devices  2.94 us (2%)
  other arithmetic  2.53 us (2%)
    all_to_all x2, blocking collectives, gather_y(): lax.all_to_all(jnp.broadcast_to(own[None], (count,) + own.shape), 'y', sp...  35.9 us
    all_to_all x1, blocking collectives, body(): lax.all_to_all(send.reshape(expert_count, slot_count, 2 * width), EXPERT,...  26 us
    all_to_all x1, blocking collectives, body(): parts = lax.all_to_all(parts, 'y', split_axis=0, concat_axis=0, tiled=True)  17.2 us
    all_to_all x1, blocking collectives, body(): lax.all_to_all(own_rows.reshape(expert_count, slot_count, width), EXPERT,...  16.9 us
    ppermute x2, starting transfers between devices, join_cores(): other = lax.ppermute(own, 'c', SWAP)  9.51 us
    dot_general x1, matrix products, expert_rows(): lax.dot_general(grad_gate, sign_values, contract, preferred_element_type=...  7.13 us
    reshape x1, local copies, waits for them, and re-layouts, body(): halves = tangent_grads.reshape(rows, cores, model_width // cores)  6.59 us
    dot_general x1, matrix products, expert_rows(): jnp.dot(rows_x, sign_values, preferred_element_type=jnp.float32)  4.92 us
  transfers between devices with their start and end apart: 3, of which 2 were waited for; matrix products, arithmetic and copies ran while one was open for 4% of the time, Pallas kernels for 0%

profile of v1, /device:TPU:1, one launch (start us, length us, event | category | flops | bytes accessed | tf_op | source)
XLA Modules:
  0.0 163.2 jit_solution(14594088380348367000)
XLA Ops:
  0.6 0.9 convert_reduce_fusion
  1.5 0.7 multiply_add_fusion
  2.2 1.0 constant_dynamic-slice_fusion.2
  3.2 0.3 convolution_convert_fusion
  3.5 26.0 %all_to_all.25 = bf16[32,16,512]{2,1,0:T(8,128)(2,1)S(1)} all-to-all(bf16[32,16,512]{2,1,0:T(8,128)(2,1)S(1)} %bitcast.60), channel_id=1, replica_groups=mesh['x'=4,'z'=8,'y'=4,'c'=2] {'x','z'}, dimensions={0} | all-to-all | bytes 1048576 | tf_op jit(solution)/shard_map/all_to_all | solution.py:107
  29.5 0.2 copy.16
  29.7 0.2 broadcast_in_dim.39
  29.8 26.6 %all_to_all.26 = bf16[4,512,512]{1,2,0:T(8,128)(2,1)S(1)} all-to-all(bf16[4,512,512]{1,2,0:T(8,128)(2,1)S(1)} %broadcast_in_dim.39), channel_id=1, replica_groups=mesh['x'=4,'z'=8,'y'=4,'c'=2] {'y'}, dimensions={0} | all-to-all | bytes 4194304 | tf_op jit(solution)/shard_map/all_to_all | solution.py:82
  56.4 4.7 %collective-permute-start = (bf16[4,512,512]{1,2,0:T(8,128)(2,1)S(1)}, bf16[4,512,512]{1,2,0:T(8,128)(2,1)}, u32[]{:S(2)}, u32[]{:S(2)}) collective-permute-start(bf16[4,512,512]{1,2,0:T(8,128)(2,1)S(1)} %all_to_all.26), channel_id=1, source_target_pairs={{0,1},{1,0},{2,3},{3,2},{4,5},{5,4},{6,7},{7,6},{8,9},{9,8},{10,11... | collective-permute-start | bytes 6291464 | tf_op jit(solution)/shard_map/ppermute | solution.py:73
  61.8 0.4 broadcast_in_dim.37
  62.2 0.2 constant_dynamic-update-slice_fusion.1
  62.4 2.7 %collective-permute-done = bf16[4,512,512]{1,2,0:T(8,128)(2,1)} collective-permute-done((bf16[4,512,512]{1,2,0:T(8,128)(2,1)S(1)}, bf16[4,512,512]{1,2,0:T(8,128)(2,1)}, u32[]{:S(2)}, u32[]{:S(2)}) %collective-permute-start) | collective-permute-done | bytes 2097184 | tf_op jit(solution)/shard_map/ppermute | solution.py:73
  65.0 1.8 %constant_dynamic-update-slice_fusion = bf16[8,512,512]{1,2,0:T(8,128)(2,1)S(1)} fusion(bf16[8,512,512]{1,2,0:T(8,128)(2,1)S(1)} %constant_dynamic-update-slice_fusion.1, bf16[4,512,512]{1,2,0:T(8,128)(2,1)} %collective-permute-done, s32[]{:T(128)S(6)} %select_n.24), kind=kLoop, calls=%fused_computation.56 | loop fusion | bytes 4194308 | tf_op jit(solution)/shard_map/dynamic_update_slice | solution.py:77
  66.9 0.0 copy-start.1
  66.9 0.4 fusion.58
  67.2 1.7 %copy-done.1 = bf16[1,896,2048]{2,1,0:T(8,128)(2,1)S(1)} copy-done((bf16[1,896,2048]{2,1,0:T(8,128)(2,1)S(1)}, bf16[1,896,2048]{2,1,0:T(8,128)(2,1)}, u32[]{:S(2)}) %copy-start.1) | copy-done | bytes 3670040
  68.9 0.0 copy-start.2
  68.9 2.4 %fusion.14 = f32[512,896]{1,0:T(8,128)S(1)} fusion(bf16[512,2048]{0,1:T(8,128)(2,1)S(1)} %bitcast.56, bf16[1,896,2048]{2,1,0:T(8,128)(2,1)S(1)} %copy-done.1), kind=kOutput, calls=%fused_computation.18 | convolution fusion | flops 1879048192 | bytes 7602176 | tf_op jit(solution)/shard_map/dot_general | solution.py:44
  71.3 0.0 copy-done.2
  71.3 0.0 copy-start
  71.3 2.4 %fusion.8 = f32[512,896]{1,0:T(8,128)S(1)} fusion(bf16[512,2048]{0,1:T(8,128)(2,1)S(1)} %bitcast.49, bf16[1,2048,896]{2,1,0:T(8,128)(2,1)S(1)} %copy-done.2), kind=kOutput, calls=%fused_computation.12 | convolution fusion | flops 1879048192 | bytes 7602176 | tf_op jit(solution)/shard_map/dot_general | solution.py:41
  73.7 0.0 copy-done
  73.7 2.3 %fusion.25 = f32[512,896]{1,0:T(8,128)S(1)} fusion(f32[512,896]{1,0:T(8,128)S(1)} %fusion.14, bf16[512,2048]{0,1:T(8,128)(2,1)S(1)} %bitcast.50, bf16[1,2048,896]{2,1,0:T(8,128)(2,1)S(1)} %copy-done), kind=kOutput, calls=%fused_computation.35 | convolution fusion | flops 1879506944 | bytes 9437184 | tf_op jit(solution)/shard_map/dot_general | solution.py:42
  76.1 4.9 %multiply_reduce_fusion = (f32[896]{0:T(1024)S(1)}, f32[512,896]{1,0:T(8,128)S(1)}) fusion(f32[512,896]{1,0:T(8,128)S(1)} %fusion.25, f32[512,896]{1,0:T(8,128)S(1)} %fusion.8, bf16[512,2048]{0,1:T(8,128)(2,1)S(1)} %bitcast.51, s32[]{:T(128)} %bitcast.11, s32[896]{0:T(1024)S(1)} %add_multiply_fusion, s32[2048]{0:T(1024)S(1)} %iota_multiply_fusion), kind=kOutput, calls=%fused_computation.30 | convolution fusion | flops 1911159936 | bytes 7617540 | tf_op jit(solution)/shard_map/dot_general | solution.py:43
  81.0 3.0 %fusion.10 = f32[512,2048]{1,0:T(8,128)S(1)} fusion(bf16[1,2048,896]{2,1,0:T(8,128)(2,1)S(1)} %copy-done, f32[512,896]{1,0:T(8,128)S(1)} %get-tuple-element.5, f32[512,896]{1,0:T(8,128)S(1)} %fusion.14, f32[512,896]{1,0:T(8,128)S(1)} %fusion.8), kind=kOutput, calls=%fused_computation.14 | convolution fusion | flops 1883635712 | bytes 13369344 | tf_op jit(solution)/shard_map/dot_general | solution.py:53
  84.0 3.1 %fusion.6 = f32[512,2048]{1,0:T(8,128)S(1)} fusion(bf16[1,2048,896]{2,1,0:T(8,128)(2,1)S(1)} %copy-done.2, f32[512,896]{1,0:T(8,128)S(1)} %get-tuple-element.5, f32[512,896]{1,0:T(8,128)S(1)} %fusion.25, f32[512,896]{1,0:T(8,128)S(1)} %fusion.8), kind=kOutput, calls=%fused_computation.10 | convolution fusion | flops 1885011968 | bytes 13369344 | tf_op jit(solution)/shard_map/dot_general | solution.py:50
  87.1 7.1 %add_add_fusion = f32[512,2048]{1,0:T(8,128)} fusion(f32[512,2048]{1,0:T(8,128)S(1)} %fusion.6, f32[512,2048]{1,0:T(8,128)S(1)} %fusion.10, s32[]{:T(128)} %bitcast.11, s32[896]{0:T(1024)S(1)} %add_multiply_fusion, s32[2048]{0:T(1024)S(1)} %iota_multiply_fusion, f32[512,896]{1,0:T(8,128)S(1)} %fusion.25, f32[512,896]{1,0:T(8,128)S(1)} %fusion.8), kind=kOutput, calls=%fused_computation.9 | convolution fusion | flops 1910964224 | bytes 16264708 | tf_op jit(solution)/shard_map/dot_general | solution.py:56
  94.3 6.6 %reshape.57 = f32[512,2,1024]{2,1,0:T(2,128)} reshape(f32[512,2048]{1,0:T(8,128)} %add_add_fusion) | data formatting | bytes 8388608 | tf_op jit(solution)/shard_map/reshape | solution.py:117
  100.9 4.1 %constant_dynamic-slice_fusion = bf16[512,1,1024]{2,1,0:T(2,128)(2,1)S(1)} fusion(f32[512,2,1024]{2,1,0:T(2,128)} %reshape.57, s32[]{:T(128)S(6)} %select_n.27), kind=kLoop, calls=%fused_computation.54 | loop fusion | bytes 2097156 | tf_op jit(solution)/shard_map/dynamic_slice | solution.py:119
  104.9 0.4 copy.32
  105.3 0.7 collective-permute-start.1
  106.0 4.0 %constant_dynamic-slice_fusion.1 = f32[512,1,1024]{2,1,0:T(1,128)S(1)} fusion(f32[512,2,1024]{2,1,0:T(2,128)} %reshape.57, s32[]{:T(128)S(6)} %select_n.26), kind=kLoop, calls=%fused_computation.55 | loop fusion | bytes 4194308 | tf_op jit(solution)/shard_map/dynamic_slice | solution.py:118
  110.0 0.0 collective-permute-done.1
  110.0 0.7 fusion.16
  110.7 0.1 copy.33
  110.8 17.2 %all_to_all.27 = bf16[4,512,256]{2,1,0:T(8,128)(2,1)S(1)} all-to-all(bf16[4,512,256]{2,1,0:T(8,128)(2,1)S(1)} %bitcast.53), channel_id=1, replica_groups=mesh['x'=4,'z'=8,'y'=4,'c'=2] {'y'}, dimensions={0} | all-to-all | bytes 2097152 | tf_op jit(solution)/shard_map/all_to_all | solution.py:122
  128.0 0.3 reduce_sum.31
  128.3 16.9 %all_to_all.28 = bf16[32,16,256]{2,1,0:T(8,128)(2,1)S(1)} all-to-all(bf16[32,16,256]{2,1,0:T(8,128)(2,1)S(1)} %bitcast.58), channel_id=1, replica_groups=mesh['x'=4,'z'=8,'y'=4,'c'=2] {'x','z'}, dimensions={0} | all-to-all | bytes 524288 | tf_op jit(solution)/shard_map/all_to_all | solution.py:124
  145.2 0.3 convolution_convert_fusion.1
  145.6 9.3 %all_to_all.29 = bf16[4,256,256]{2,1,0:T(8,128)(2,1)S(1)} all-to-all(bf16[4,256,256]{2,1,0:T(8,128)(2,1)S(1)} %broadcast_in_dim.42), channel_id=1, replica_groups=mesh['x'=4,'z'=8,'y'=4,'c'=2] {'y'}, dimensions={0} | all-to-all | bytes 1048576 | tf_op jit(solution)/shard_map/all_to_all | solution.py:82
  154.9 4.8 %collective-permute-start.2 = (bf16[4,256,256]{2,1,0:T(8,128)(2,1)S(1)}, bf16[4,256,256]{2,1,0:T(8,128)(2,1)S(1)}, u32[]{:S(2)}, u32[]{:S(2)}) collective-permute-start(bf16[4,256,256]{2,1,0:T(8,128)(2,1)S(1)} %all_to_all.29), channel_id=1, source_target_pairs={{0,1},{1,0},{2,3},{3,2},{4,5},{5,4},{6,7},{7,6},{8,9},{9,8},{10,11... | collective-permute-start | bytes 1572872 | tf_op jit(solution)/shard_map/ppermute | solution.py:73
  159.8 0.6 broadcast_in_dim.43
  160.3 0.1 broadcast_in_dim.36
  160.4 0.6 copy_dynamic-update-slice_fusion.1
  161.0 0.3 collective-permute-done.2
  161.3 0.6 copy_dynamic-update-slice_fusion
  161.9 1.3 copy.24
  (3 shorter events, 0.0 us)
Async XLA Ops:
  56.4 8.6 %collective-permute-start = (bf16[4,512,512]{1,2,0:T(8,128)(2,1)S(1)}, bf16[4,512,512]{1,2,0:T(8,128)(2,1)}, u32[]{:S(2)}, u32[]{:S(2)}) collective-permute-start(bf16[4,512,512]{1,2,0:T(8,128)(2,1)S(1)} %all_to_all.26), channel_id=1, source_target_pairs={{0,1},{1,0},{2,3},{3,2},{4,5},{5,4},{6,7},{7,6},{8,9},{9,8},{10,11... | collective-permute-start | bytes 6291464 | tf_op jit(solution)/shard_map/ppermute | solution.py:73
  66.9 2.0 %copy-start.1 = (bf16[1,896,2048]{2,1,0:T(8,128)(2,1)S(1)}, bf16[1,896,2048]{2,1,0:T(8,128)(2,1)}, u32[]{:S(2)}) copy-start(bf16[1,896,2048]{2,1,0:T(8,128)(2,1)} %param.12) | copy-start | bytes 11010052
  68.9 2.4 %copy-start.2 = (bf16[1,2048,896]{2,1,0:T(8,128)(2,1)S(1)}, bf16[1,2048,896]{2,1,0:T(8,128)(2,1)}, u32[]{:S(2)}) copy-start(bf16[1,2048,896]{2,1,0:T(8,128)(2,1)} %param.10) | copy-start | bytes 11010052
  71.3 2.4 %copy-start = (bf16[1,2048,896]{2,1,0:T(8,128)(2,1)S(1)}, bf16[1,2048,896]{2,1,0:T(8,128)(2,1)}, u32[]{:S(2)}) copy-start(bf16[1,2048,896]{2,1,0:T(8,128)(2,1)} %param.11) | copy-start | bytes 11010052
  105.3 4.7 %collective-permute-start.1 = (bf16[512,1024]{1,0:T(8,128)(2,1)S(1)}, bf16[512,1024]{1,0:T(8,128)(2,1)S(1)}, u32[]{:S(2)}, u32[]{:S(2)}) collective-permute-start(bf16[512,1024]{1,0:T(8,128)(2,1)S(1)} %bitcast.57), channel_id=1, source_target_pairs={{0,1},{1,0},{2,3},{3,2},{4,5},{5,4},{6,7},{7,6},{8,9},{9,8},{10,11... | collective-permute-start | bytes 3145736 | tf_op jit(solution)/shard_map/ppermute | solution.py:120
  154.9 6.3 %collective-permute-start.2 = (bf16[4,256,256]{2,1,0:T(8,128)(2,1)S(1)}, bf16[4,256,256]{2,1,0:T(8,128)(2,1)S(1)}, u32[]{:S(2)}, u32[]{:S(2)}) collective-permute-start(bf16[4,256,256]{2,1,0:T(8,128)(2,1)S(1)} %all_to_all.29), channel_id=1, source_target_pairs={{0,1},{1,0},{2,3},{3,2},{4,5},{5,4},{6,7},{7,6},{8,9},{9,8},{10,11... | collective-permute-start | bytes 1572872 | tf_op jit(solution)/shard_map/ppermute | solution.py:73

commit v2 on v1

v2 whole, which is shorter than its diff:
```python
import functools
import math

import jax
import jax.numpy as jnp
from jax import lax
from jax.experimental import pallas as pl
from jax.experimental.pallas import tpu as pltpu
from jax.sharding import Mesh, PartitionSpec as P

EXPERT = ("x", "z")
SWAP = [(0, 1), (1, 0)]
SHIFTS = (1, -1, 2)
TILE = 256
VMEM = 56 * 1024 * 1024
BF16 = jnp.bfloat16
F32 = jnp.float32


def params():
    return pltpu.CompilerParams(vmem_limit_bytes=VMEM)


def cost(flops, moved, exps=0):
    return pl.CostEstimate(flops=flops, bytes_accessed=moved, transcendentals=exps)


def sign_kernel(info_ref, out_ref):
    rows, cols = out_ref.shape
    first = pl.program_id(0) * rows
    row = lax.broadcasted_iota(jnp.int32, (rows, 1), 0) + first
    col = lax.broadcasted_iota(jnp.int32, (1, cols), 1) + info_ref[0]
    mixed = row * jnp.int32(73856093) + (
        col * jnp.int32(19349663) + info_ref[1] * jnp.int32(83492791)
    )
    mixed = mixed ^ mixed >> 15
    mixed = mixed * jnp.int32(735632791)
    mixed = mixed ^ mixed >> 13
    mixed = mixed * jnp.int32(1274126177)
    mixed = mixed ^ mixed >> 16
    scale = jnp.asarray(1.0 / math.sqrt(2048), BF16).astype(F32)
    out_ref[...] = jnp.where((mixed & 32) != 0, scale, -scale).astype(BF16)


def sign_table(offset, seed, model_width, hidden_cols):
    info = jnp.stack([offset, seed])
    rows = 128
    return pl.pallas_call(
        sign_kernel,
        out_shape=jax.ShapeDtypeStruct((model_width, hidden_cols), BF16),
        grid=(model_width // rows,),
        in_specs=[pl.BlockSpec(memory_space=pltpu.SMEM)],
        out_specs=pl.BlockSpec((rows, hidden_cols), lambda i: (i, 0)),
        compiler_params=params(),
        cost_estimate=cost(30 * model_width * hidden_cols, 2 * model_width * hidden_cols),
        name="sign_table",
    )(info)


def place(scratch, half, blocks_ref, y, ys):
    width = blocks_ref.shape[2]
    for slot, shift in enumerate((0,) + SHIFTS):
        source = lax.rem(y - shift + ys, ys)
        column = pl.multiple_of(half + source * width, width)
        scratch[:, pl.ds(column, width)] = blocks_ref[slot]


def forward_kernel(ys, pos_ref, own_ref, other_ref, gate_ref, up_ref, sign_ref, a_ref, b_ref, c_ref, e_ref, xs):
    y, core = pos_ref[0], pos_ref[1]
    half = xs.shape[1] // 2

    @pl.when(pl.program_id(0) == 0)
    def _():
        place(xs, core * half, own_ref, y, ys)
        place(xs, (1 - core) * half, other_ref, y, ys)

    x = xs[...]
    pre = jnp.dot(x, gate_ref[0], preferred_element_type=F32)
    lin = jnp.dot(x, up_ref[0], preferred_element_type=F32)
    tangent = jnp.dot(x, sign_ref[...], preferred_element_type=F32)
    sig = jax.nn.sigmoid(pre)
    rest = 1.0 - sig
    slope = sig * (1.0 + pre * rest)
    bend = sig * rest * (2.0 + pre * (1.0 - 2.0 * sig))
    a_ref[...] = lin * slope
    b_ref[...] = slope * tangent
    third = lin * bend * tangent
    c_ref[...] = third
    e_ref[...] = third * tangent


def forward(pos, own, other, w_gate, w_up, signs):
    ys, rows, width = own.shape
    model, hidden = signs.shape
    whole = pl.BlockSpec((ys, rows, width), lambda j, p: (0, 0, 0))
    weight = pl.BlockSpec((1, model, TILE), lambda j, p: (0, 0, j))
    column = pl.BlockSpec((rows, TILE), lambda j, p: (0, j))
    return pl.pallas_call(
        functools.partial(forward_kernel, ys),
        out_shape=[jax.ShapeDtypeStruct((rows, hidden), F32)] * 4,
        grid_spec=pltpu.PrefetchScalarGridSpec(
            num_scalar_prefetch=1,
            grid=(pl.cdiv(hidden, TILE),),
            in_specs=[whole, whole, weight, weight, pl.BlockSpec((model, TILE), lambda j, p: (0, j))],
            out_specs=[column] * 4,
            scratch_shapes=[pltpu.VMEM((rows, model), BF16)],
        ),
        compiler_params=params(),
        cost_estimate=cost(6 * rows * model * hidden, 6 * model * hidden + 16 * rows * hidden, rows * hidden),
        name="forward",
    )(pos, own, other, w_gate, w_up, signs)


NT = (((1,), (1,)), ((), ()))


def first_half_kernel(ys, pos_ref, own_ref, down_ref, h_ref, cs):
    @pl.when(pl.program_id(0) == 0)
    def _():
        place(cs, 0, own_ref, pos_ref[0], ys)

    h_ref[...] = lax.dot_general(cs[...], down_ref[0], NT, preferred_element_type=F32)


def first_half(pos, own, w_down):
    ys, rows, width = own.shape
    hidden, model = w_down.shape[1:]
    half = model // 2
    return pl.pallas_call(
        functools.partial(first_half_kernel, ys),
        out_shape=jax.ShapeDtypeStruct((rows, hidden), F32),
        grid_spec=pltpu.PrefetchScalarGridSpec(
            num_scalar_prefetch=1,
            grid=(pl.cdiv(hidden, TILE),),
            in_specs=[
                pl.BlockSpec((ys, rows, width), lambda j, p: (0, 0, 0)),
                pl.BlockSpec((1, TILE, half), lambda j, p: (0, j, p[1])),
            ],
            out_specs=pl.BlockSpec((rows, TILE), lambda j, p: (0, j)),
            scratch_shapes=[pltpu.VMEM((rows, half), BF16)],
        ),
        compiler_params=params(),
        cost_estimate=cost(2 * rows * half * hidden, 2 * half * hidden + 4 * rows * hidden),
        name="first_half",
    )(pos, own, w_down)


def middle_kernel(ys, pos_ref, other_ref, down_ref, h_ref, a_ref, b_ref, c_ref, e_ref, tg_ref, tu_ref, gg_ref, cu_ref, cs):
    @pl.when(pl.program_id(0) == 0)
    def _():
        place(cs, 0, other_ref, pos_ref[0], ys)

    h = h_ref[...] + lax.dot_general(cs[...], down_ref[0], NT, preferred_element_type=F32)
    tg_ref[...] = (h * c_ref[...]).astype(BF16)
    tu_ref[...] = (h * b_ref[...]).astype(BF16)
    gg_ref[...] = (h * a_ref[...]).astype(BF16)
    cu_ref[...] = jnp.sum(h * e_ref[...], axis=0, keepdims=True)


def middle(pos, other, w_down, h, factors):
    ys, rows, width = other.shape
    hidden, model = w_down.shape[1:]
    half = model // 2
    column = pl.BlockSpec((rows, TILE), lambda j, p: (0, j))
    return pl.pallas_call(
        functools.partial(middle_kernel, ys),
        out_shape=[jax.ShapeDtypeStruct((rows, hidden), BF16)] * 3 + [jax.ShapeDtypeStruct((1, hidden), F32)],
        grid_spec=pltpu.PrefetchScalarGridSpec(
            num_scalar_prefetch=1,
            grid=(pl.cdiv(hidden, TILE),),
            in_specs=[
                pl.BlockSpec((ys, rows, width), lambda j, p: (0, 0, 0)),
                pl.BlockSpec((1, TILE, half), lambda j, p: (0, j, 1 - p[1])),
                column,
                column,
                column,
                column,
                column,
            ],
            out_specs=[column, column, column, pl.BlockSpec((1, TILE), lambda j, p: (0, j))],
            scratch_shapes=[pltpu.VMEM((rows, half), BF16)],
        ),
        compiler_params=params(),
        cost_estimate=cost(2 * rows * half * hidden, 2 * half * hidden + 26 * rows * hidden),
        name="middle",
    )(pos, other, w_down, h, *factors)


def backward_kernel(pos_ref, tg_ref, tu_ref, gg_ref, gate_ref, up_ref, sign_ref, out_ref):
    total = lax.dot_general(tg_ref[...], gate_ref[0], NT, preferred_element_type=F32)
    total += lax.dot_general(tu_ref[...], up_ref[0], NT, preferred_element_type=F32)
    total += lax.dot_general(gg_ref[...], sign_ref[...], NT, preferred_element_type=F32)
    out_ref[0] = total.astype(out_ref.dtype)


def backward(pos, grads, w_gate, w_up, signs, ys, dtype, flip, name):
    rows, hidden = grads[0].shape
    model = signs.shape[0]
    width = model // (2 * ys)

    def tile(i, p):
        shift = jnp.where(i == 1, 1, jnp.where(i == 2, ys - 1, jnp.where(i == 3, 2, 0)))
        core = 1 - p[1] if flip else p[1]
        return core * ys + lax.rem(p[0] + shift, ys)

    grad = pl.BlockSpec((rows, hidden), lambda i, p: (0, 0))
    weight = pl.BlockSpec((1, width, hidden), lambda i, p: (0, tile(i, p), 0))
    return pl.pallas_call(
        backward_kernel,
        out_shape=jax.ShapeDtypeStruct((ys, rows, width), dtype),
        grid_spec=pltpu.PrefetchScalarGridSpec(
            num_scalar_prefetch=1,
            grid=(ys,),
            in_specs=[grad] * 3 + [weight, weight, pl.BlockSpec((width, hidden), lambda i, p: (tile(i, p), 0))],
            out_specs=pl.BlockSpec((1, rows, width), lambda i, p: (i, 0, 0)),
        ),
        compiler_params=params(),
        cost_estimate=cost(3 * rows * model * hidden, 3 * model * hidden + 6 * rows * hidden),
        name=name,
    )(pos, *grads, w_gate, w_up, signs)


def assemble_kernel(ys, pos_ref, own_ref, other_ref, out_ref):
    y, core = pos_ref[0], pos_ref[1]
    half = out_ref.shape[1] // 2
    place(out_ref, core * half, own_ref, y, ys)
    place(out_ref, (1 - core) * half, other_ref, y, ys)


def assemble(pos, own, other):
    ys, rows, width = own.shape
    return pl.pallas_call(
        functools.partial(assemble_kernel, ys),
        out_shape=jax.ShapeDtypeStruct((rows, 2 * ys * width), own.dtype),
        in_specs=[pl.BlockSpec(memory_space=pltpu.SMEM)] + [pl.BlockSpec(memory_space=pltpu.VMEM)] * 2,
        out_specs=pl.BlockSpec(memory_space=pltpu.VMEM),
        compiler_params=params(),
        cost_estimate=cost(0, 8 * ys * rows * width),
        name="assemble",
    )(pos, own, other)


def shift_y(value, shift):
    count = lax.axis_size("y")
    return lax.ppermute(value, "y", [(i, (i + shift) % count) for i in range(count)])


def gather_y(own):
    return jnp.stack([own] + [shift_y(own, shift) for shift in SHIFTS])


def swap_cores(value):
    return lax.ppermute(value, "c", SWAP)


def exchange(value):
    return lax.all_to_all(value, EXPERT, split_axis=0, concat_axis=0, tiled=True)


def dispatch_matrix(route_flat, expert_count, slot_count):
    tok_count = route_flat.shape[0]
    token = jnp.arange(tok_count, dtype=jnp.int32)
    earlier = (route_flat[:, None] == route_flat[None, :]) & (token[:, None] < token[None, :])
    slot_place = jnp.sum(earlier.astype(jnp.int32), axis=0)
    target = route_flat * slot_count + slot_place
    slot_ids = jnp.arange(expert_count * slot_count, dtype=jnp.int32)
    return (slot_ids[:, None] == target[None, :]).astype(BF16)


def body(tokens, cotangent, expert_route, w_gate, w_up, w_down, sign_seeds):
    expert_count = lax.axis_size(EXPERT)
    ys, cores = lax.axis_size("y"), lax.axis_size("c")
    y, core = lax.axis_index("y"), lax.axis_index("c")
    tok_count, model_width = tokens.shape
    hidden_cols = w_gate.shape[2]
    slot_count = max(2, 2 * tok_count // expert_count)
    rows = expert_count * slot_count
    width = model_width // (ys * cores)
    pos = jnp.stack([y, core]).astype(jnp.int32)
    dispatch = dispatch_matrix(expert_route[:, 0], expert_count, slot_count)

    def send_rows(values):
        piece = lax.dynamic_slice_in_dim(values, (core * ys + y) * width, width, 1)
        send = jnp.dot(dispatch, piece, preferred_element_type=F32).astype(BF16)
        return exchange(send.reshape(expert_count, slot_count, width)).reshape(rows, width)

    x_rows, cotangent = lax.optimization_barrier((send_rows(tokens), cotangent))
    x_moved = [shift_y(x_rows, shift) for shift in SHIFTS]
    cot_rows = send_rows(cotangent)
    x_moved, cot_rows, seed = lax.optimization_barrier((x_moved, cot_rows, sign_seeds[0]))
    x_own = jnp.stack([x_rows] + x_moved)
    x_other = swap_cores(x_own)
    cot_moved = [shift_y(cot_rows, shift) for shift in SHIFTS]
    signs = sign_table((y * cores + core) * hidden_cols, seed, model_width, hidden_cols)
    factors = forward(pos, x_own, x_other, w_gate, w_up, signs)
    factors, cot_moved = lax.optimization_barrier((factors, cot_moved))
    cot_own = jnp.stack([cot_rows] + cot_moved)
    h = first_half(pos, cot_own, w_down)
    *grads, curvature = middle(pos, swap_cores(cot_own), w_down, h, factors)

    give = backward(pos, grads, w_gate, w_up, signs, ys, BF16, True, "backward_give")
    keep = backward(pos, grads, w_gate, w_up, signs, ys, F32, False, "backward_keep")
    pair = keep + swap_cores(give).astype(F32)
    total = pair[0]
    for slot, shift in enumerate(SHIFTS):
        total = total + shift_y(pair[slot + 1].astype(BF16), shift).astype(F32)
    returned = exchange(total.astype(BF16).reshape(expert_count, slot_count, width)).reshape(rows, width)
    combined = lax.dot_general(
        dispatch, returned, (((0,), (0,)), ((), ())), preferred_element_type=F32
    ).astype(BF16)
    result = gather_y(combined)
    return (assemble(pos, result, swap_cores(result)), curvature)


def solution(mesh):
    chips = Mesh(mesh.devices.reshape(4, 8, 4, 2), ("x", "z", "y", "c"))
    expert, dp = EXPERT, ("y", "c")
    in_specs = (
        P(expert, None),
        P(expert, None),
        P(expert, None),
        P(expert, None, dp),
        P(expert, None, dp),
        P(expert, dp, None),
        P(expert),
    )
    out_specs = (P(expert, None), P(expert, dp))
    return jax.shard_map(body, mesh=chips, in_specs=in_specs, out_specs=out_specs, check_vma=False)
```

time: 164 us -> 165 us (level)
  blocking collectives: 96 us -> 40 us
  Pallas kernels: 0 us -> 53.6 us
  waiting for transfers between devices: 2.94 us -> 28.6 us
  matrix products: 26 us -> 2.43 us
  local copies, waits for them, and re-layouts: 24 us -> 2.81 us
  starting transfers between devices: 10.2 us -> 30.4 us
  other arithmetic: 2.53 us -> 5.26 us
    all_to_all x5 -> x2, blocking collectives: 96 us -> 40 us  [exchange(): lax.all_to_all(value, EXPERT, split_axis=0, concat_axis=0, tiled=True)]
    pallas_call x0 -> x7, Pallas kernels: none -> 53.6 us  [the longest x2 16.7 us: backward(): pl.pallas_call(backward_kernel, out_shape=jax.ShapeDtypeStruct((ys, rows,...]
    ppermute x3 -> x16, waiting for transfers between devices: 2.94 us -> 28.6 us  [the longest x12 27 us: shift_y(): lax.ppermute(value, 'y', [(i, (i + shift) % count) for i in range(count)])]
    dot_general x8 -> x2, matrix products: 25.6 us -> 2.09 us  [send_rows(): send = jnp.dot(dispatch, piece, preferred_element_type=F32).astype(BF16)]
    ppermute x3 -> x16, starting transfers between devices: 10.2 us -> 24.1 us  [the longest x12 15.2 us: shift_y(): lax.ppermute(value, 'y', [(i, (i + shift) % count) for i in range(count)])]
    dynamic_slice x3 -> x0, local copies, waits for them, and re-layouts: 9.05 us -> none  [the longest x1 4.08 us: body(): lax.dynamic_slice_in_dim(halves, 1 - core, 1, 1)[:, 0].astype(jnp.bfloat16)]
    reshape x2 -> x0, local copies, waits for them, and re-layouts: 6.66 us -> none  [the longest x1 6.59 us: body(): halves = tangent_grads.reshape(rows, cores, model_width // cores)]
    all_to_all x0 -> x1, starting transfers between devices: none -> 6.29 us  [exchange(): lax.all_to_all(value, EXPERT, split_axis=0, concat_axis=0, tiled=True)]
  transfers between devices with their start and end apart: 3 -> 17, of which waited for: 2 -> 8; matrix products, arithmetic and copies ran while one was open for 4% -> 1% of each run, Pallas kernels for 0% -> 21%
where the time goes in v2:
time: 165 us
  Pallas kernels  53.6 us (32%)
  blocking collectives  40 us (24%)
  starting transfers between devices  30.4 us (18%)
  waiting for transfers between devices  28.6 us (17%)
  other arithmetic  5.26 us (3%)
  local copies, waits for them, and re-layouts  2.81 us (2%)
  matrix products  2.43 us (1%)
    all_to_all x2, blocking collectives, exchange(): lax.all_to_all(value, EXPERT, split_axis=0, concat_axis=0, tiled=True)  40 us
    ppermute x12, waiting for transfers between devices, shift_y(): lax.ppermute(value, 'y', [(i, (i + shift) % count) for i in range(count)])  27 us
    pallas_call x2, Pallas kernels, backward(): pl.pallas_call(backward_kernel, out_shape=jax.ShapeDtypeStruct((ys, rows,...  16.7 us
    ppermute x12, starting transfers between devices, shift_y(): lax.ppermute(value, 'y', [(i, (i + shift) % count) for i in range(count)])  15.2 us
    pallas_call x1, Pallas kernels, forward(): pl.pallas_call(functools.partial(forward_kernel, ys), out_shape=[jax.Shap...  12.9 us
    ppermute x4, starting transfers between devices, swap_cores(): return lax.ppermute(value, 'c', SWAP)  8.93 us
    pallas_call x1, Pallas kernels, sign_table(): pl.pallas_call(sign_kernel, out_shape=jax.ShapeDtypeStruct((model_width,...  8.16 us
    pallas_call x1, Pallas kernels, middle(): pl.pallas_call(functools.partial(middle_kernel, ys), out_shape=[jax.Shape...  7.89 us
  transfers between devices with their start and end apart: 17, of which 8 were waited for; matrix products, arithmetic and copies ran while one was open for 1% of the time, Pallas kernels for 21%

profile of v2, /device:TPU:1, one launch (start us, length us, event | category | flops | bytes accessed | tf_op | source)
XLA Modules:
  0.0 164.5 jit_solution(15312666273913526513)
XLA Ops:
  0.7 0.9 convert_reduce_fusion
  1.5 0.7 multiply_add_fusion
  2.2 0.2 convolution_convert_fusion.1
  2.5 21.4 %all_to_all.15 = bf16[32,16,256]{2,1,0:T(8,128)(2,1)S(1)} all-to-all(bf16[32,16,256]{2,1,0:T(8,128)(2,1)S(1)} %bitcast.41), channel_id=1, replica_groups=mesh['x'=4,'z'=8,'y'=4,'c'=2] {'x','z'}, dimensions={0} | all-to-all | bytes 524288 | tf_op jit(solution)/shard_map/all_to_all | solution.py:257
  23.8 1.8 %convolution_convert_fusion = bf16[512,256]{1,0:T(8,128)(2,1)} fusion(s32[256]{0:T(256)S(1)} %multiply_add_fusion, bf16[256,2048]{1,0:T(8,128)(2,1)} %param.8, s32[]{:T(128)S(6)} %select_n.4), kind=kOutput, calls=%fused_computation.1 | convolution fusion | flops 67371008 | bytes 394244 | tf_op jit(solution)/shard_map/dot_general | solution.py:284
  25.7 6.3 %all-to-all-start.1 = ((bf16[32,16,256]{2,1,0:T(8,128)(2,1)}), bf16[32,16,256]{2,1,0:T(8,128)(2,1)S(1)}, u32[]{:S(2)}, u32[]{:S(2)}) async-start(bf16[32,16,256]{2,1,0:T(8,128)(2,1)} %bitcast.5), calls=%async_computation.1 | async-start | bytes 524288 | tf_op jit(solution)/shard_map/all_to_all | solution.py:257
  32.0 3.0 %collective-permute-start.2 = (bf16[512,256]{1,0:T(8,128)(2,1)S(1)}, bf16[512,256]{1,0:T(8,128)(2,1)S(1)}, u32[]{:S(2)}, u32[]{:S(2)}) collective-permute-start(bf16[512,256]{1,0:T(8,128)(2,1)S(1)} %bitcast.47), channel_id=1, source_target_pairs={{0,4},{2,6},{4,0},{6,2},{1,5},{3,7},{5,1},{7,3},{8,12},{10,14},{12... | collective-permute-start | bytes 786440 | tf_op jit(solution)/shard_map/ppermute | solution.py:245
  35.0 0.8 collective-permute-start.1
  35.8 0.7 collective-permute-start
  36.4 3.1 %collective-permute-done.2 = bf16[512,256]{1,0:T(8,128)(2,1)S(1)} collective-permute-done((bf16[512,256]{1,0:T(8,128)(2,1)S(1)}, bf16[512,256]{1,0:T(8,128)(2,1)S(1)}, u32[]{:S(2)}, u32[]{:S(2)}) %collective-permute-start.2) | collective-permute-done | bytes 262176 | tf_op jit(solution)/shard_map/ppermute | solution.py:245
  39.5 7.2 %collective-permute-done.1 = bf16[512,256]{1,0:T(8,128)(2,1)S(1)} collective-permute-done((bf16[512,256]{1,0:T(8,128)(2,1)S(1)}, bf16[512,256]{1,0:T(8,128)(2,1)S(1)}, u32[]{:S(2)}, u32[]{:S(2)}) %collective-permute-start.1) | collective-permute-done | bytes 262176 | tf_op jit(solution)/shard_map/ppermute | solution.py:245
  46.7 0.1 pad_maximum_fusion.own_ref
  46.9 1.6 collective-permute-start.3
  49.2 0.6 pad_add_fusion.1.info_ref
  49.8 8.2 %sign_table.1.sign_ref = bf16[2048,896]{1,0:T(8,128)(2,1)} custom-call(s32[2]{0:T(128)} %pad_add_fusion.1.info_ref), custom_call_target="tpu_custom_call" | custom-call | flops 55050240 | bytes 3670016 | tf_op jit(solution)/shard_map/sign_table/pallas_call | solution.py:48
  58.0 0.7 pad_add_fusion.pos_ref
  58.6 2.5 %collective-permute-start.6 = (bf16[512,256]{1,0:T(8,128)(2,1)S(1)}, bf16[512,256]{1,0:T(8,128)(2,1)S(1)}, u32[]{:S(2)}, u32[]{:S(2)}) collective-permute-start(bf16[512,256]{1,0:T(8,128)(2,1)S(1)} %bitcast.43), channel_id=1, source_target_pairs={{0,4},{2,6},{4,0},{6,2},{1,5},{3,7},{5,1},{7,3},{8,12},{10,14},{12... | collective-permute-start | bytes 786440 | tf_op jit(solution)/shard_map/ppermute | solution.py:245
  61.2 0.9 collective-permute-start.5
  62.1 0.5 collective-permute-start.4
  62.6 1.0 copy-done.6
  63.6 12.9 %forward.1 = (f32[512,896]{1,0:T(8,128)}, f32[512,896]{1,0:T(8,128)}, f32[512,896]{1,0:T(8,128)}, f32[512,896]{1,0:T(8,128)}) custom-call(s32[2]{0:T(128)} %pad_add_fusion.pos_ref, bf16[4,512,256]{2,1,0:T(8,128)(2,1)} %copy-done.3, bf16[4,512,256]{2,1,0:T(8,128)(2,1)} %copy-done.6, bf16[1,2048,896]{2,1,0:T(8,128)(2,1)} %gate_ref.5, ...), custom_call_target="tpu_custom_call" | custom-call | flops 5637144576 | bytes 18350080 | tf_op jit(solution)/shard_map/forward/pallas_call | solution.py:98
  76.5 0.1 pad_maximum_fusion.1.own_ref
  76.6 1.0 collective-permute-start.7
  77.6 5.7 %first_half.1.h_ref = f32[512,896]{1,0:T(8,128)} custom-call(s32[2]{0:T(128)} %pad_add_fusion.pos_ref, bf16[4,512,256]{2,1,0:T(8,128)(2,1)} %copy-done.1, bf16[1,896,2048]{2,1,0:T(8,128)(2,1)} %down_ref.3), custom_call_target="tpu_custom_call" | custom-call | flops 939524096 | bytes 3670016 | tf_op jit(solution)/shard_map/first_half/pallas_call | solution.py:129
  83.3 1.0 copy-done.4
  84.3 7.9 %middle.1 = (bf16[512,896]{1,0:T(8,128)(2,1)}, bf16[512,896]{1,0:T(8,128)(2,1)}, bf16[512,896]{1,0:T(8,128)(2,1)}, f32[1,896]{1,0:T(1,128)}) custom-call(s32[2]{0:T(128)} %pad_add_fusion.pos_ref, bf16[4,512,256]{2,1,0:T(8,128)(2,1)} %copy-done.4, bf16[1,896,2048]{2,1,0:T(8,128)(2,1)} %down_ref.3, f32[512,896]{1,0:T(8,128)} %first_half.1.h_ref, ...), custom_call_target="tpu_custom_call" | custom-call | flops 939524096 | bytes 13762560 | tf_op jit(solution)/shard_map/middle/pallas_call | solution.py:165
  92.2 8.2 %backward_give.1 = bf16[4,512,256]{2,1,0:T(8,128)(2,1)} custom-call(s32[2]{0:T(128)} %pad_add_fusion.pos_ref, bf16[512,896]{1,0:T(8,128)(2,1)} %get-tuple-element.42.tg_ref, bf16[512,896]{1,0:T(8,128)(2,1)} %get-tuple-element.43.tu_ref, bf16[512,896]{1,0:T(8,128)(2,1)} %get-tuple-element.44.gg_ref, bf16[1,2048,896]{2,1,0:T(8,128)(2,1)} %gate_ref.5, ...), custom_call_target="tpu_custom_call" | custom-call | flops 2818572288 | bytes 8257536 | tf_op jit(solution)/shard_map/backward_give/pallas_call | solution.py:208
  100.4 0.9 collective-permute-start.8
  101.3 8.4 %backward_keep.1 = f32[4,512,256]{2,1,0:T(8,128)} custom-call(s32[2]{0:T(128)} %pad_add_fusion.pos_ref, bf16[512,896]{1,0:T(8,128)(2,1)} %get-tuple-element.42.tg_ref, bf16[512,896]{1,0:T(8,128)(2,1)} %get-tuple-element.43.tu_ref, bf16[512,896]{1,0:T(8,128)(2,1)} %get-tuple-element.44.gg_ref, bf16[1,2048,896]{2,1,0:T(8,128)(2,1)} %gate_ref.5, ...), custom_call_target="tpu_custom_call" | custom-call | flops 2818572288 | bytes 8257536 | tf_op jit(solution)/shard_map/backward_keep/pallas_call | solution.py:208
  109.7 1.9 %fusion.12 = (bf16[4,512,256]{2,1,0:T(8,128)(2,1)S(1)}, f32[4,512,256]{2,1,0:T(8,128)S(1)}) fusion(f32[4,512,256]{2,1,0:T(8,128)} %backward_keep.1, bf16[4,512,256]{2,1,0:T(8,128)(2,1)S(1)} %collective-permute-done.8), kind=kLoop, calls=%fused_computation.29 | loop fusion | flops 1572864 | bytes 6291456 | tf_op jit(solution)/shard_map/convert.2
  111.7 0.5 collective-permute-start.9
  112.2 2.9 %collective-permute-start.11 = (bf16[512,256]{1,0:T(8,128)(2,1)S(1)}, bf16[512,256]{1,0:T(8,128)(2,1)S(1)}, u32[]{:S(2)}, u32[]{:S(2)}) collective-permute-start(bf16[512,256]{1,0:T(8,128)(2,1)S(1)} %get-tuple-element.49), channel_id=1, source_target_pairs={{0,4},{2,6},{4,0},{6,2},{1,5},{3,7},{5,1},{7,3},{8,12},{10,14},{12... | collective-permute-start | bytes 786440 | tf_op jit(solution)/shard_map/ppermute | solution.py:245
  115.1 5.8 %collective-permute-done.9 = bf16[512,256]{1,0:T(8,128)(2,1)S(1)} collective-permute-done((bf16[512,256]{1,0:T(8,128)(2,1)S(1)}, bf16[512,256]{1,0:T(8,128)(2,1)S(1)}, u32[]{:S(2)}, u32[]{:S(2)}) %collective-permute-start.9) | collective-permute-done | bytes 262176 | tf_op jit(solution)/shard_map/ppermute | solution.py:245
  120.9 6.3 %collective-permute-done.11 = bf16[512,256]{1,0:T(8,128)(2,1)S(1)} collective-permute-done((bf16[512,256]{1,0:T(8,128)(2,1)S(1)}, bf16[512,256]{1,0:T(8,128)(2,1)S(1)}, u32[]{:S(2)}, u32[]{:S(2)}) %collective-permute-start.11) | collective-permute-done | bytes 262176 | tf_op jit(solution)/shard_map/ppermute | solution.py:245
  127.2 0.2 fusion.3
  127.3 18.7 %all_to_all.16 = bf16[32,16,256]{2,1,0:T(8,128)(2,1)S(1)} all-to-all(bf16[32,16,256]{2,1,0:T(8,128)(2,1)S(1)} %bitcast.42), channel_id=1, replica_groups=mesh['x'=4,'z'=8,'y'=4,'c'=2] {'x','z'}, dimensions={0} | all-to-all | bytes 524288 | tf_op jit(solution)/shard_map/all_to_all | solution.py:257
  146.0 0.3 convolution_convert_fusion.2
  146.4 0.9 collective-permute-start.14
  147.3 2.0 %collective-permute-start.13 = (bf16[256,256]{1,0:T(8,128)(2,1)S(1)}, bf16[256,256]{1,0:T(8,128)(2,1)S(1)}, u32[]{:S(2)}, u32[]{:S(2)}) collective-permute-start(bf16[256,256]{1,0:T(8,128)(2,1)S(1)} %convolution_convert_fusion.2), channel_id=1, source_target_pairs={{0,6},{2,0},{4,2},{6,4},{1,7},{3,1},{5,3},{7,5},{8,14},{10,8},{12,... | collective-permute-start | bytes 393224 | tf_op jit(solution)/shard_map/ppermute | solution.py:245
  149.3 0.4 collective-permute-start.12
  149.7 2.1 %collective-permute-done.14 = bf16[256,256]{1,0:T(8,128)(2,1)S(1)} collective-permute-done((bf16[256,256]{1,0:T(8,128)(2,1)S(1)}, bf16[256,256]{1,0:T(8,128)(2,1)S(1)}, u32[]{:S(2)}, u32[]{:S(2)}) %collective-permute-start.14) | collective-permute-done | bytes 131104 | tf_op jit(solution)/shard_map/ppermute | solution.py:245
  151.8 1.7 %collective-permute-done.13 = bf16[256,256]{1,0:T(8,128)(2,1)S(1)} collective-permute-done((bf16[256,256]{1,0:T(8,128)(2,1)S(1)}, bf16[256,256]{1,0:T(8,128)(2,1)S(1)}, u32[]{:S(2)}, u32[]{:S(2)}) %collective-permute-start.13) | collective-permute-done | bytes 131104 | tf_op jit(solution)/shard_map/ppermute | solution.py:245
  153.5 0.8 collective-permute-done.12
  154.3 0.1 pad_maximum_fusion.2.own_ref
  154.4 5.4 %collective-permute-start.15 = (bf16[4,256,256]{2,1,0:T(8,128)(2,1)S(1)}, bf16[4,256,256]{2,1,0:T(8,128)(2,1)S(1)}, u32[]{:S(2)}, u32[]{:S(2)}) collective-permute-start(bf16[4,256,256]{2,1,0:T(8,128)(2,1)S(1)} %pad_maximum_fusion.2.own_ref), channel_id=1, source_target_pairs={{0,1},{1,0},{2,3},{3,2},{4,5},{5,4},{6,7},{7,6},{8,9},{9,8},{10,11... | collective-permute-start | bytes 1572872 | tf_op jit(solution)/shard_map/ppermute | solution.py:253
  159.9 1.5 collective-permute-done.15.other_ref
  161.4 0.8 copy-done.5
  162.2 2.3 %assemble.1 = bf16[256,2048]{1,0:T(8,128)(2,1)} custom-call(s32[2]{0:T(128)} %pad_add_fusion.pos_ref, bf16[4,256,256]{2,1,0:T(8,128)(2,1)} %copy-done.2, bf16[4,256,256]{2,1,0:T(8,128)(2,1)} %copy-done.5), custom_call_target="tpu_custom_call" | custom-call | bytes 2097152 | tf_op jit(solution)/shard_map/assemble/pallas_call | solution.py:232
  (22 shorter events, 0.1 us)
Async XLA Ops:
  0.6 1.6 copy-start
  25.7 21.1 %all-to-all-start.1 = ((bf16[32,16,256]{2,1,0:T(8,128)(2,1)}), bf16[32,16,256]{2,1,0:T(8,128)(2,1)S(1)}, u32[]{:S(2)}, u32[]{:S(2)}) async-start(bf16[32,16,256]{2,1,0:T(8,128)(2,1)} %bitcast.5), calls=%async_computation.1 | async-start | bytes 524288 | tf_op jit(solution)/shard_map/all_to_all | solution.py:257
  32.0 7.6 %collective-permute-start.2 = (bf16[512,256]{1,0:T(8,128)(2,1)S(1)}, bf16[512,256]{1,0:T(8,128)(2,1)S(1)}, u32[]{:S(2)}, u32[]{:S(2)}) collective-permute-start(bf16[512,256]{1,0:T(8,128)(2,1)S(1)} %bitcast.47), channel_id=1, source_target_pairs={{0,4},{2,6},{4,0},{6,2},{1,5},{3,7},{5,1},{7,3},{8,12},{10,14},{12... | collective-permute-start | bytes 786440 | tf_op jit(solution)/shard_map/ppermute | solution.py:245
  35.0 11.8 %collective-permute-start.1 = (bf16[512,256]{1,0:T(8,128)(2,1)S(1)}, bf16[512,256]{1,0:T(8,128)(2,1)S(1)}, u32[]{:S(2)}, u32[]{:S(2)}) collective-permute-start(bf16[512,256]{1,0:T(8,128)(2,1)S(1)} %bitcast.48), channel_id=1, source_target_pairs={{0,6},{2,0},{4,2},{6,4},{1,7},{3,1},{5,3},{7,5},{8,14},{10,8},{12,... | collective-permute-start | bytes 786440 | tf_op jit(solution)/shard_map/ppermute | solution.py:245
  35.8 11.0 %collective-permute-start = (bf16[512,256]{1,0:T(8,128)(2,1)S(1)}, bf16[512,256]{1,0:T(8,128)(2,1)S(1)}, u32[]{:S(2)}, u32[]{:S(2)}) collective-permute-start(bf16[512,256]{1,0:T(8,128)(2,1)S(1)} %bitcast.49), channel_id=1, source_target_pairs={{0,2},{2,4},{4,6},{6,0},{1,3},{3,5},{5,7},{7,1},{8,10},{10,12},{12... | collective-permute-start | bytes 786440 | tf_op jit(solution)/shard_map/ppermute | solution.py:245
  46.9 15.8 %copy-start.3 = (bf16[4,512,256]{2,1,0:T(8,128)(2,1)}, bf16[4,512,256]{2,1,0:T(8,128)(2,1)S(1)}, u32[]{:S(2)}) copy-start(bf16[4,512,256]{2,1,0:T(8,128)(2,1)S(1)} %pad_maximum_fusion.own_ref) | copy-start | bytes 3145732
  46.9 15.7 %collective-permute-start.3 = (bf16[4,512,256]{2,1,0:T(8,128)(2,1)S(1)}, bf16[4,512,256]{2,1,0:T(8,128)(2,1)S(1)}, u32[]{:S(2)}, u32[]{:S(2)}) collective-permute-start(bf16[4,512,256]{2,1,0:T(8,128)(2,1)S(1)} %pad_maximum_fusion.own_ref), channel_id=1, source_target_pairs={{0,1},{1,0},{2,3},{3,2},{4,5},{5,4},{6,7},{7,6},{8,9},{9,8},{10,11... | collective-permute-start | bytes 3145736 | tf_op jit(solution)/shard_map/ppermute | solution.py:253
  58.6 17.8 %collective-permute-start.6 = (bf16[512,256]{1,0:T(8,128)(2,1)S(1)}, bf16[512,256]{1,0:T(8,128)(2,1)S(1)}, u32[]{:S(2)}, u32[]{:S(2)}) collective-permute-start(bf16[512,256]{1,0:T(8,128)(2,1)S(1)} %bitcast.43), channel_id=1, source_target_pairs={{0,4},{2,6},{4,0},{6,2},{1,5},{3,7},{5,1},{7,3},{8,12},{10,14},{12... | collective-permute-start | bytes 786440 | tf_op jit(solution)/shard_map/ppermute | solution.py:245
  61.2 15.3 %collective-permute-start.5 = (bf16[512,256]{1,0:T(8,128)(2,1)S(1)}, bf16[512,256]{1,0:T(8,128)(2,1)S(1)}, u32[]{:S(2)}, u32[]{:S(2)}) collective-permute-start(bf16[512,256]{1,0:T(8,128)(2,1)S(1)} %bitcast.44), channel_id=1, source_target_pairs={{0,6},{2,0},{4,2},{6,4},{1,7},{3,1},{5,3},{7,5},{8,14},{10,8},{12,... | collective-permute-start | bytes 786440 | tf_op jit(solution)/shard_map/ppermute | solution.py:245
  62.1 14.4 %collective-permute-start.4 = (bf16[512,256]{1,0:T(8,128)(2,1)S(1)}, bf16[512,256]{1,0:T(8,128)(2,1)S(1)}, u32[]{:S(2)}, u32[]{:S(2)}) collective-permute-start(bf16[512,256]{1,0:T(8,128)(2,1)S(1)} %bitcast.45), channel_id=1, source_target_pairs={{0,2},{2,4},{4,6},{6,0},{1,3},{3,5},{5,7},{7,1},{8,10},{10,12},{12... | collective-permute-start | bytes 786440 | tf_op jit(solution)/shard_map/ppermute | solution.py:245
  62.6 1.0 copy-start.6
  76.6 1.0 copy-start.1
  76.6 6.7 %collective-permute-start.7 = (bf16[4,512,256]{2,1,0:T(8,128)(2,1)S(1)}, bf16[4,512,256]{2,1,0:T(8,128)(2,1)S(1)}, u32[]{:S(2)}, u32[]{:S(2)}) collective-permute-start(bf16[4,512,256]{2,1,0:T(8,128)(2,1)S(1)} %pad_maximum_fusion.1.own_ref), channel_id=1, source_target_pairs={{0,1},{1,0},{2,3},{3,2},{4,5},{5,4},{6,7},{7,6},{8,9},{9,8},{10,11... | collective-permute-start | bytes 3145736 | tf_op jit(solution)/shard_map/ppermute | solution.py:253
  83.3 1.0 copy-start.4
  100.4 9.3 %collective-permute-start.8 = (bf16[4,512,256]{2,1,0:T(8,128)(2,1)}, bf16[4,512,256]{2,1,0:T(8,128)(2,1)S(1)}, u32[]{:S(2)}, u32[]{:S(2)}) collective-permute-start(bf16[4,512,256]{2,1,0:T(8,128)(2,1)} %backward_give.1), channel_id=1, source_target_pairs={{0,1},{1,0},{2,3},{3,2},{4,5},{5,4},{6,7},{7,6},{8,9},{9,8},{10,11... | collective-permute-start | bytes 3145736 | tf_op jit(solution)/shard_map/ppermute | solution.py:253
  111.7 9.2 %collective-permute-start.9 = (bf16[512,256]{1,0:T(8,128)(2,1)S(1)}, bf16[512,256]{1,0:T(8,128)(2,1)S(1)}, u32[]{:S(2)}, u32[]{:S(2)}) collective-permute-start(bf16[512,256]{1,0:T(8,128)(2,1)S(1)} %get-tuple-element.48), channel_id=1, source_target_pairs={{0,2},{2,4},{4,6},{6,0},{1,3},{3,5},{5,7},{7,1},{8,10},{10,12},{12... | collective-permute-start | bytes 786440 | tf_op jit(solution)/shard_map/ppermute | solution.py:245
  112.2 15.0 %collective-permute-start.11 = (bf16[512,256]{1,0:T(8,128)(2,1)S(1)}, bf16[512,256]{1,0:T(8,128)(2,1)S(1)}, u32[]{:S(2)}, u32[]{:S(2)}) collective-permute-start(bf16[512,256]{1,0:T(8,128)(2,1)S(1)} %get-tuple-element.49), channel_id=1, source_target_pairs={{0,4},{2,6},{4,0},{6,2},{1,5},{3,7},{5,1},{7,3},{8,12},{10,14},{12... | collective-permute-start | bytes 786440 | tf_op jit(solution)/shard_map/ppermute | solution.py:245
  115.1 12.1 %collective-permute-start.10 = (bf16[512,256]{1,0:T(8,128)(2,1)S(1)}, bf16[512,256]{1,0:T(8,128)(2,1)S(1)}, u32[]{:S(2)}, u32[]{:S(2)}) collective-permute-start(bf16[512,256]{1,0:T(8,128)(2,1)S(1)} %get-tuple-element.50), channel_id=1, source_target_pairs={{0,6},{2,0},{4,2},{6,4},{1,7},{3,1},{5,3},{7,5},{8,14},{10,8},{12,... | collective-permute-start | bytes 786440 | tf_op jit(solution)/shard_map/ppermute | solution.py:245
  146.4 5.4 %collective-permute-start.14 = (bf16[256,256]{1,0:T(8,128)(2,1)S(1)}, bf16[256,256]{1,0:T(8,128)(2,1)S(1)}, u32[]{:S(2)}, u32[]{:S(2)}) collective-permute-start(bf16[256,256]{1,0:T(8,128)(2,1)S(1)} %convolution_convert_fusion.2), channel_id=1, source_target_pairs={{0,4},{2,6},{4,0},{6,2},{1,5},{3,7},{5,1},{7,3},{8,12},{10,14},{12... | collective-permute-start | bytes 393224 | tf_op jit(solution)/shard_map/ppermute | solution.py:245
  147.3 6.2 %collective-permute-start.13 = (bf16[256,256]{1,0:T(8,128)(2,1)S(1)}, bf16[256,256]{1,0:T(8,128)(2,1)S(1)}, u32[]{:S(2)}, u32[]{:S(2)}) collective-permute-start(bf16[256,256]{1,0:T(8,128)(2,1)S(1)} %convolution_convert_fusion.2), channel_id=1, source_target_pairs={{0,6},{2,0},{4,2},{6,4},{1,7},{3,1},{5,3},{7,5},{8,14},{10,8},{12,... | collective-permute-start | bytes 393224 | tf_op jit(solution)/shard_map/ppermute | solution.py:245
  149.3 5.0 %collective-permute-start.12 = (bf16[256,256]{1,0:T(8,128)(2,1)S(1)}, bf16[256,256]{1,0:T(8,128)(2,1)S(1)}, u32[]{:S(2)}, u32[]{:S(2)}) collective-permute-start(bf16[256,256]{1,0:T(8,128)(2,1)S(1)} %convolution_convert_fusion.2), channel_id=1, source_target_pairs={{0,2},{2,4},{4,6},{6,0},{1,3},{3,5},{5,7},{7,1},{8,10},{10,12},{12... | collective-permute-start | bytes 393224 | tf_op jit(solution)/shard_map/ppermute | solution.py:245
  154.4 7.0 %copy-start.2 = (bf16[4,256,256]{2,1,0:T(8,128)(2,1)}, bf16[4,256,256]{2,1,0:T(8,128)(2,1)S(1)}, u32[]{:S(2)}) copy-start(bf16[4,256,256]{2,1,0:T(8,128)(2,1)S(1)} %pad_maximum_fusion.2.own_ref) | copy-start | bytes 1572868
  154.4 7.0 %collective-permute-start.15 = (bf16[4,256,256]{2,1,0:T(8,128)(2,1)S(1)}, bf16[4,256,256]{2,1,0:T(8,128)(2,1)S(1)}, u32[]{:S(2)}, u32[]{:S(2)}) collective-permute-start(bf16[4,256,256]{2,1,0:T(8,128)(2,1)S(1)} %pad_maximum_fusion.2.own_ref), channel_id=1, source_target_pairs={{0,1},{1,0},{2,3},{3,2},{4,5},{5,4},{6,7},{7,6},{8,9},{9,8},{10,11... | collective-permute-start | bytes 1572872 | tf_op jit(solution)/shard_map/ppermute | solution.py:253
  161.4 0.8 copy-start.5

commit v3 on v1

v3 whole, which is shorter than its diff:
```python
import math

import jax
import jax.numpy as jnp
from jax import lax
from jax.experimental import pallas as pl
from jax.experimental.pallas import tpu as pltpu
from jax.sharding import Mesh, PartitionSpec as P

EXPERT = ("x", "z")
SWAP = [(0, 1), (1, 0)]
BF16 = jnp.bfloat16
F32 = jnp.float32


def sign_kernel(info_ref, out_ref):
    rows, cols = out_ref.shape
    first = pl.program_id(0) * rows
    col = lax.broadcasted_iota(jnp.int32, (1, cols), 1) + info_ref[0]
    base = col * jnp.int32(19349663) + info_ref[1] * jnp.int32(83492791)
    scale = jnp.asarray(1.0 / math.sqrt(2048), BF16).astype(F32)
    step = 8
    for at in range(0, rows, step):
        row = lax.broadcasted_iota(jnp.int32, (step, 1), 0) + (first + at)
        mixed = row * jnp.int32(73856093) + base
        mixed = mixed ^ mixed >> 15
        mixed = mixed * jnp.int32(735632791)
        mixed = mixed ^ mixed >> 13
        mixed = mixed * jnp.int32(1274126177)
        mixed = mixed ^ mixed >> 16
        out_ref[at : at + step, :] = jnp.where((mixed & 32) != 0, scale, -scale).astype(BF16)


def sign_table(offset, seed, model_width, hidden_cols):
    rows = 512
    return pl.pallas_call(
        sign_kernel,
        out_shape=jax.ShapeDtypeStruct((model_width, hidden_cols), BF16),
        grid=(model_width // rows,),
        in_specs=[pl.BlockSpec(memory_space=pltpu.SMEM)],
        out_specs=pl.BlockSpec((rows, hidden_cols), lambda i: (i, 0)),
        compiler_params=pltpu.CompilerParams(vmem_limit_bytes=8 * 1024 * 1024),
        cost_estimate=pl.CostEstimate(flops=0, bytes_accessed=2 * model_width * hidden_cols, transcendentals=0),
        name="sign_table",
    )(jnp.stack([offset, seed]))


def dot(a, b, ca, cb):
    return lax.dot_general(a, b, (((ca,), (cb,)), ((), ())), preferred_element_type=F32)


def shift_y(value, shift):
    count = lax.axis_size("y")
    return lax.ppermute(value, "y", [(i, (i + shift) % count) for i in range(count)])


def turn(pieces, y):
    count = len(pieces)
    result = jnp.zeros((count,) + pieces[0].shape, pieces[0].dtype)
    for step, piece in enumerate(pieces):
        result = lax.dynamic_update_index_in_dim(result, piece, lax.rem(y + step, count), 0)
    return result


def swap_cores(value):
    return lax.ppermute(value, "c", SWAP)


def exchange(value):
    return lax.all_to_all(value, EXPERT, split_axis=0, concat_axis=0, tiled=True)


def half_of(value, core, axis):
    size = value.shape[axis] // 2
    return lax.dynamic_slice_in_dim(value, core * size, size, axis)


def forward_factors(pre, lin, tangent):
    sig = jax.nn.sigmoid(pre)
    rest = 1.0 - sig
    slope = sig * (1.0 + pre * rest)
    bend = sig * rest * (2.0 + pre * (1.0 - 2.0 * sig))
    third = lin * bend * tangent
    return (lin * slope, slope * tangent, third, third * tangent)


def dispatch_matrix(route_flat, expert_count, slot_count):
    tok_count = route_flat.shape[0]
    token = jnp.arange(tok_count, dtype=jnp.int32)
    earlier = (route_flat[:, None] == route_flat[None, :]) & (token[:, None] < token[None, :])
    slot_place = jnp.sum(earlier.astype(jnp.int32), axis=0)
    target = route_flat * slot_count + slot_place
    slot_ids = jnp.arange(expert_count * slot_count, dtype=jnp.int32)
    return (slot_ids[:, None] == target[None, :]).astype(BF16)


def body(tokens, cotangent, expert_route, w_gate, w_up, w_down, sign_seeds):
    expert_count = lax.axis_size(EXPERT)
    ys, cores = lax.axis_size("y"), lax.axis_size("c")
    y, core = lax.axis_index("y"), lax.axis_index("c")
    tok_count, model_width = tokens.shape
    hidden_cols = w_gate.shape[2]
    slot_count = max(2, 2 * tok_count // expert_count)
    rows = expert_count * slot_count
    width = model_width // (ys * cores)
    half = ys * width
    gate, up, down = w_gate[0], w_up[0], w_down[0]
    dispatch = dispatch_matrix(expert_route[:, 0], expert_count, slot_count)
    barrier = lax.optimization_barrier

    def packed(values):
        piece = lax.dynamic_slice_in_dim(values, (core * ys + y) * width, width, 1)
        send = jnp.dot(dispatch, piece, preferred_element_type=F32).astype(BF16)
        return send.reshape(expert_count, slot_count, width)

    def moved(piece):
        return [shift_y(piece, shift) for shift in (-1, 2, 1)]

    send_x, send_cot = barrier((packed(tokens), packed(cotangent)))
    x_piece, send_cot = barrier((exchange(send_x).reshape(rows, width).T, send_cot))
    x_moved = moved(x_piece)
    cot_piece = exchange(send_cot).reshape(rows, width).T
    x_moved, cot_piece, seed = barrier((x_moved, cot_piece, sign_seeds[0]))
    x_own = turn([x_piece] + x_moved, y).reshape(half, rows)
    x_other = swap_cores(x_own)
    cot_moved = moved(cot_piece)
    signs = sign_table((y * cores + core) * hidden_cols, seed, model_width, hidden_cols)
    mats = (gate, up, signs)
    firsts = barrier([dot(half_of(w, core, 0), x_own, 0, 0) for w in mats])
    factors = forward_factors(*[a + dot(half_of(w, 1 - core, 0), x_other, 0, 0) for a, w in zip(firsts, mats)])
    factors, cot_moved = barrier((factors, cot_moved))
    cot_own = turn([cot_piece] + cot_moved, y).reshape(half, rows)
    cot_other = swap_cores(cot_own)
    first = barrier(dot(half_of(down, core, 1), cot_own, 1, 0))
    h = first + dot(half_of(down, 1 - core, 1), cot_other, 1, 0)
    ggate, tup, tgate = [(h * f).astype(BF16) for f in factors[:3]]
    curvature = jnp.sum(h * factors[3], axis=1)

    def tangent_half(which):
        return (
            dot(half_of(gate, which, 0), tgate, 1, 0)
            + dot(half_of(up, which, 0), tup, 1, 0)
            + dot(half_of(signs, which, 0), ggate, 1, 0)
        )

    give = tangent_half(1 - core).astype(BF16)
    pair = tangent_half(core) + swap_cores(give).astype(F32)

    def part(shift):
        return lax.dynamic_slice_in_dim(pair, lax.rem(y + shift, ys) * width, width, 0)

    total = part(0)
    for shift in (2, 1, 3):
        total = total + shift_y(part(shift).astype(BF16), shift).astype(F32)
    back = total.astype(BF16).T.reshape(expert_count, slot_count, width)
    returned = exchange(back).reshape(rows, width)
    combined = dot(dispatch, returned, 0, 0).astype(BF16)
    own = jnp.stack([combined] + moved(combined))
    result = jnp.zeros((tok_count, model_width), BF16)
    for blocks, of_core in ((own, core), (swap_cores(own), 1 - core)):
        for step in range(ys):
            at = (of_core * ys + lax.rem(y + step, ys)) * width
            result = lax.dynamic_update_slice_in_dim(result, blocks[step], at, 1)
    return (result, curvature[None, :])


def solution(mesh):
    chips = Mesh(mesh.devices.reshape(4, 8, 4, 2), ("x", "z", "y", "c"))
    expert, dp = EXPERT, ("y", "c")
    in_specs = (
        P(expert, None),
        P(expert, None),
        P(expert, None),
        P(expert, None, dp),
        P(expert, None, dp),
        P(expert, dp, None),
        P(expert),
    )
    out_specs = (P(expert, None), P(expert, dp))
    return jax.shard_map(body, mesh=chips, in_specs=in_specs, out_specs=out_specs, check_vma=False)
```

time: 164 us -> 163 us (level)
  blocking collectives: 96 us -> 21.3 us
  waiting for transfers between devices: 2.94 us -> 39.2 us
  starting transfers between devices: 10.2 us -> 36 us
  matrix products: 26 us -> 42.1 us
  local copies, waits for them, and re-layouts: 24 us -> 14.4 us
  Pallas kernels: 0 us -> 3.73 us
    all_to_all x5 -> x1, blocking collectives: 96 us -> 21.3 us  [exchange(): lax.all_to_all(value, EXPERT, split_axis=0, concat_axis=0, tiled=True)]
    ppermute x3 -> x16, waiting for transfers between devices: 2.94 us -> 29.5 us  [the longest x12 28.6 us: shift_y(): lax.ppermute(value, 'y', [(i, (i + shift) % count) for i in range(count)])]
    dot_general x9 -> x17, matrix products: 26 us -> 42.1 us  [the longest x15 40 us: dot(): lax.dot_general(a, b, (((ca,), (cb,)), ((), ())), preferred_element_type=...]
    all_to_all x0 -> x2, starting transfers between devices: none -> 15.5 us  [exchange(): lax.all_to_all(value, EXPERT, split_axis=0, concat_axis=0, tiled=True)]
    ppermute x3 -> x16, starting transfers between devices: 10.2 us -> 20.5 us  [the longest x12 13.3 us: shift_y(): lax.ppermute(value, 'y', [(i, (i + shift) % count) for i in range(count)])]
    all_to_all x0 -> x2, waiting for transfers between devices: none -> 9.67 us  [exchange(): lax.all_to_all(value, EXPERT, split_axis=0, concat_axis=0, tiled=True)]
    dynamic_slice x3 -> x0, local copies, waits for them, and re-layouts: 9.05 us -> none  [the longest x1 4.08 us: body(): lax.dynamic_slice_in_dim(halves, 1 - core, 1, 1)[:, 0].astype(jnp.bfloat16)]
    reshape x2 -> x0, local copies, waits for them, and re-layouts: 6.66 us -> none  [the longest x1 6.59 us: body(): halves = tangent_grads.reshape(rows, cores, model_width // cores)]
  transfers between devices with their start and end apart: 3 -> 18, of which waited for: 2 -> 11; matrix products, arithmetic and copies ran while one was open for 4% -> 21% of each run, Pallas kernels for 0% -> 2%
where the time goes in v3:
time: 163 us; the launch traced here: 162 us
  matrix products  42.1 us (26%)
  waiting for transfers between devices  39.2 us (24%)
  starting transfers between devices  36 us (22%)
  blocking collectives  21.3 us (13%)
  local copies, waits for them, and re-layouts  14.4 us (9%)
  Pallas kernels  3.73 us (2%)
  other arithmetic  3.58 us (2%)
  between operations  1.83 us (1%)
    dot_general x15, matrix products, dot(): lax.dot_general(a, b, (((ca,), (cb,)), ((), ())), preferred_element_type=...  40 us
    ppermute x12, waiting for transfers between devices, shift_y(): lax.ppermute(value, 'y', [(i, (i + shift) % count) for i in range(count)])  28.6 us
    all_to_all x1, blocking collectives, exchange(): lax.all_to_all(value, EXPERT, split_axis=0, concat_axis=0, tiled=True)  21.3 us
    all_to_all x2, starting transfers between devices, exchange(): lax.all_to_all(value, EXPERT, split_axis=0, concat_axis=0, tiled=True)  15.5 us
    ppermute x12, starting transfers between devices, shift_y(): lax.ppermute(value, 'y', [(i, (i + shift) % count) for i in range(count)])  13.3 us
    all_to_all x2, waiting for transfers between devices, exchange(): lax.all_to_all(value, EXPERT, split_axis=0, concat_axis=0, tiled=True)  9.67 us
    unnamed x46, local copies, waits for them, and re-layouts  8.26 us
    ppermute x4, starting transfers between devices, swap_cores(): return lax.ppermute(value, 'c', SWAP)  7.16 us
  transfers between devices with their start and end apart: 18, of which 11 were waited for; matrix products, arithmetic and copies ran while one was open for 21% of the time, Pallas kernels for 2%

profile of v3, /device:TPU:1, one launch (start us, length us, event | category | flops | bytes accessed | tf_op | source)
XLA Modules:
  0.0 162.1 jit_solution(13287786620277397535)
XLA Ops:
  0.7 0.9 convert_reduce_fusion
  2.5 1.9 %convolution_convert_fusion = bf16[512,256]{1,0:T(8,128)(2,1)} fusion(s32[256]{0:T(256)S(1)} %multiply_add_fusion, bf16[256,2048]{1,0:T(8,128)(2,1)} %param.8, s32[]{:T(128)S(6)} %select_n.76), kind=kOutput, calls=%fused_computation.56 | convolution fusion | flops 67371008 | bytes 394244 | tf_op jit(solution)/shard_map/dot_general | solution.py:113
  4.3 21.3 %all_to_all.15 = bf16[32,16,256]{2,1,0:T(8,128)(2,1)S(1)} all-to-all(bf16[32,16,256]{2,1,0:T(8,128)(2,1)S(1)} %bitcast.105), channel_id=1, replica_groups=mesh['x'=4,'z'=8,'y'=4,'c'=2] {'x','z'}, dimensions={0} | all-to-all | bytes 524288 | tf_op jit(solution)/shard_map/all_to_all | solution.py:70
  25.7 6.3 %all-to-all-start.1 = ((bf16[32,16,256]{2,1,0:T(8,128)(2,1)}), bf16[32,16,256]{2,1,0:T(8,128)(2,1)S(1)}, u32[]{:S(2)}, u32[]{:S(2)}) async-start(bf16[32,16,256]{2,1,0:T(8,128)(2,1)} %bitcast.4), calls=%async_computation.1 | async-start | bytes 524288 | tf_op jit(solution)/shard_map/all_to_all | solution.py:70
  32.0 2.8 %collective-permute-start = (bf16[256,512]{0,1:T(8,128)(2,1)S(1)}, bf16[256,512]{0,1:T(8,128)(2,1)S(1)}, u32[]{:S(2)}, u32[]{:S(2)}) collective-permute-start(bf16[256,512]{0,1:T(8,128)(2,1)S(1)} %bitcast.101), channel_id=1, source_target_pairs={{0,6},{2,0},{4,2},{6,4},{1,7},{3,1},{5,3},{7,5},{8,14},{10,8},{12,... | collective-permute-start | bytes 786440 | tf_op jit(solution)/shard_map/ppermute | solution.py:54
  36.6 1.1 broadcast.17.clone
  37.7 0.7 constant_dynamic-update-slice_fusion.10
  38.4 1.8 %collective-permute-done = bf16[256,512]{0,1:T(8,128)(2,1)S(1)} collective-permute-done((bf16[256,512]{0,1:T(8,128)(2,1)S(1)}, bf16[256,512]{0,1:T(8,128)(2,1)S(1)}, u32[]{:S(2)}, u32[]{:S(2)}) %collective-permute-start) | collective-permute-done | bytes 262176 | tf_op jit(solution)/shard_map/ppermute | solution.py:54
  40.2 1.9 %collective-permute-done.1 = bf16[256,512]{0,1:T(8,128)(2,1)S(1)} collective-permute-done((bf16[256,512]{0,1:T(8,128)(2,1)S(1)}, bf16[256,512]{0,1:T(8,128)(2,1)S(1)}, u32[]{:S(2)}, u32[]{:S(2)}) %collective-permute-start.1) | collective-permute-done | bytes 262176 | tf_op jit(solution)/shard_map/ppermute | solution.py:54
  42.1 8.1 %collective-permute-done.2 = bf16[256,512]{0,1:T(8,128)(2,1)S(1)} collective-permute-done((bf16[256,512]{0,1:T(8,128)(2,1)S(1)}, bf16[256,512]{0,1:T(8,128)(2,1)S(1)}, u32[]{:S(2)}, u32[]{:S(2)}) %collective-permute-start.2) | collective-permute-done | bytes 262176 | tf_op jit(solution)/shard_map/ppermute | solution.py:54
  50.6 0.7 constant_dynamic-update-slice_fusion.9
  51.3 0.7 constant_dynamic-update-slice_fusion.8
  53.3 3.7 %sign_table.1 = bf16[2048,896]{1,0:T(8,128)(2,1)S(1)} custom-call(s32[2]{0:T(128)S(1)} %pad_add_fusion.info_ref), custom_call_target="tpu_custom_call" | custom-call | bytes 3670016 | tf_op jit(solution)/shard_map/sign_table/pallas_call | solution.py:36
  57.1 1.8 %copy-done.1 = bf16[2048,896]{1,0:T(8,128)(2,1)} copy-done((bf16[2048,896]{1,0:T(8,128)(2,1)}, bf16[2048,896]{1,0:T(8,128)(2,1)S(1)}, u32[]{:S(2)}) %copy-start.1) | copy-done | bytes 3670040
  59.5 0.8 collective-permute-start.6
  60.3 4.2 %fusion.37 = f32[896,512]{1,0:T(8,128)} fusion(bf16[1024,512]{1,0:T(8,128)(2,1)} %bitcast.15, bf16[2048,896]{1,0:T(8,128)(2,1)} %copy-done.1, s32[]{:T(128)S(6)} %select_n.75), kind=kOutput, calls=%fused_computation.46 | convolution fusion | flops 939524096 | bytes 4718596 | tf_op jit(solution)/shard_map/dot_general | solution.py:49
  64.5 3.8 %fusion.17 = f32[896,512]{1,0:T(8,128)} fusion(bf16[1024,512]{1,0:T(8,128)(2,1)} %bitcast.15, bf16[1,2048,896]{2,1,0:T(8,128)(2,1)S(1)} %copy-done.15, s32[]{:T(128)S(6)} %select_n.75), kind=kOutput, calls=%fused_computation.21 | convolution fusion | flops 939524096 | bytes 4718596 | tf_op jit(solution)/shard_map/dot_general | solution.py:49
  68.3 3.7 %fusion.23 = f32[896,512]{1,0:T(8,128)} fusion(bf16[1024,512]{1,0:T(8,128)(2,1)} %bitcast.15, bf16[1,2048,896]{2,1,0:T(8,128)(2,1)S(1)} %copy-done.18, s32[]{:T(128)S(6)} %select_n.75), kind=kOutput, calls=%fused_computation.27 | convolution fusion | flops 939524096 | bytes 4718596 | tf_op jit(solution)/shard_map/dot_general | solution.py:49
  72.3 3.7 %fusion.49 = f32[896,512]{1,0:T(8,128)S(1)} fusion(f32[896,512]{1,0:T(8,128)} %fusion.23, bf16[1024,512]{1,0:T(8,128)(2,1)} %collective-permute-done.3, bf16[1,2048,896]{2,1,0:T(8,128)(2,1)} %param.10, s32[]{:T(128)S(6)} %select_n.81), kind=kOutput, calls=%fused_computation.54 | convolution fusion | flops 939982848 | bytes 6553604 | tf_op jit(solution)/shard_map/dot_general | solution.py:49
  76.3 2.5 %fusion.46 = f32[896,512]{1,0:T(8,128)S(1)} fusion(f32[896,512]{1,0:T(8,128)S(1)} %copy-done.21, bf16[1024,512]{1,0:T(8,128)(2,1)} %collective-permute-done.3, bf16[1,2048,896]{2,1,0:T(8,128)(2,1)S(1)} %copy-done.16, s32[]{:T(128)S(6)} %select_n.81), kind=kOutput, calls=%fused_computation.53 | convolution fusion | flops 939982848 | bytes 6553604 | tf_op jit(solution)/shard_map/dot_general | solution.py:49
  79.2 6.4 %fusion.87 = (f32[896,512]{1,0:T(8,128)}, f32[896,512]{1,0:T(8,128)}, f32[896,512]{1,0:T(8,128)}, f32[896,512]{1,0:T(8,128)}) fusion(f32[896,512]{1,0:T(8,128)S(1)} %fusion.46, f32[896,512]{1,0:T(8,128)S(1)} %fusion.49, f32[896,512]{1,0:T(8,128)S(1)} %copy-done.22, bf16[1024,512]{1,0:T(8,128)(2,1)} %collective-permute-done.3, ...), kind=kOutput, calls=%fused_computation.113 | convolution fusion | flops 948240384 | bytes 15728644 | tf_op jit(solution)/shard_map/dot_general | solution.py:49
  86.2 0.9 collective-permute-start.7
  87.1 3.1 %fusion.19 = f32[896,512]{1,0:T(8,128)S(1)} fusion(bf16[1024,512]{1,0:T(8,128)(2,1)S(1)} %bitcast.96, bf16[1,896,2048]{2,1,0:T(8,128)(2,1)} %param.12, s32[]{:T(128)S(6)} %select_n.75), kind=kOutput, calls=%fused_computation.23 | convolution fusion | flops 939524096 | bytes 4718596 | tf_op jit(solution)/shard_map/dot_general | solution.py:49
  90.8 1.6 multiply_reduce_fusion
  92.5 1.3 fusion.11
  93.8 1.4 copy-done.19
  95.1 1.3 fusion.7
  97.2 2.3 %add_convert_fusion = bf16[1024,512]{0,1:T(8,128)(2,1)} fusion(f32[1024,512]{0,1:T(8,128)S(1)} %fusion.7, f32[1024,512]{0,1:T(8,128)S(1)} %fusion.11, bf16[896,512]{1,0:T(8,128)(2,1)S(1)} %get-tuple-element.48, bf16[2048,896]{1,0:T(8,128)(2,1)S(1)} %copy-done.3, s32[]{:T(128)S(6)} %select_n.81), kind=kOutput, calls=%fused_computation.3 | convolution fusion | flops 941096960 | bytes 7995396 | tf_op jit(solution)/shard_map/dot_general | solution.py:49
  100.1 3.2 %fusion.15 = f32[1024,512]{0,1:T(8,128)S(1)} fusion(bf16[896,512]{1,0:T(8,128)(2,1)} %copy-done.14, bf16[1,2048,896]{2,1,0:T(8,128)(2,1)} %param.11, s32[]{:T(128)S(6)} %select_n.75), kind=kOutput, calls=%fused_computation.19 | convolution fusion | flops 939524096 | bytes 4849668 | tf_op jit(solution)/shard_map/dot_general | solution.py:49
  103.3 1.3 fusion.21
  105.3 1.4 convert_add_fusion
  106.7 1.3 copy-done.5
  108.2 1.8 %collective-permute-start.10 = (bf16[256,512]{0,1:T(8,128)(2,1)S(1)}, bf16[256,512]{0,1:T(8,128)(2,1)S(1)}, u32[]{:S(2)}, u32[]{:S(2)}) collective-permute-start(bf16[256,512]{0,1:T(8,128)(2,1)S(1)} %get-tuple-element.46), channel_id=1, source_target_pairs={{0,2},{2,4},{4,6},{6,0},{1,3},{3,5},{5,7},{7,1},{8,10},{10,12},{12... | collective-permute-start | bytes 786440 | tf_op jit(solution)/shard_map/ppermute | solution.py:54
  110.0 0.9 collective-permute-start.11
  110.9 2.6 %collective-permute-start.9 = (bf16[256,512]{0,1:T(8,128)(2,1)S(1)}, bf16[256,512]{0,1:T(8,128)(2,1)S(1)}, u32[]{:S(2)}, u32[]{:S(2)}) collective-permute-start(bf16[256,512]{0,1:T(8,128)(2,1)S(1)} %get-tuple-element.44), channel_id=1, source_target_pairs={{0,4},{2,6},{4,0},{6,2},{1,5},{3,7},{5,1},{7,3},{8,12},{10,14},{12... | collective-permute-start | bytes 786440 | tf_op jit(solution)/shard_map/ppermute | solution.py:54
  113.5 3.8 %collective-permute-done.10 = bf16[256,512]{0,1:T(8,128)(2,1)S(1)} collective-permute-done((bf16[256,512]{0,1:T(8,128)(2,1)S(1)}, bf16[256,512]{0,1:T(8,128)(2,1)S(1)}, u32[]{:S(2)}, u32[]{:S(2)}) %collective-permute-start.10) | collective-permute-done | bytes 262176 | tf_op jit(solution)/shard_map/ppermute | solution.py:54
  117.4 0.8 collective-permute-done.11
  118.2 6.1 %collective-permute-done.9 = bf16[256,512]{0,1:T(8,128)(2,1)S(1)} collective-permute-done((bf16[256,512]{0,1:T(8,128)(2,1)S(1)}, bf16[256,512]{0,1:T(8,128)(2,1)S(1)}, u32[]{:S(2)}, u32[]{:S(2)}) %collective-permute-start.9) | collective-permute-done | bytes 262176 | tf_op jit(solution)/shard_map/ppermute | solution.py:54
  124.4 1.9 %add_convert_fusion.1 = bf16[256,512]{0,1:T(8,128)(2,1)} fusion(bf16[256,512]{0,1:T(8,128)(2,1)S(1)} %collective-permute-done.11, bf16[256,512]{0,1:T(8,128)(2,1)S(1)} %collective-permute-done.10, bf16[256,512]{0,1:T(8,128)(2,1)S(1)} %collective-permute-done.9, f32[1024,512]{0,1:T(8,128)} %copy-done.5, s32[]{:T(128)S(6)} %select_n.82), kind=kLoop, calls=%fused_computation.60 | loop fusion | flops 917504 | bytes 1572868 | tf_op jit(solution)/shard_map/convert_element_type | solution.py:155
  126.2 9.2 %all-to-all-start.2 = ((bf16[32,16,256]{2,1,0:T(8,128)(2,1)}), bf16[32,16,256]{2,1,0:T(8,128)(2,1)S(1)}, u32[]{:S(2)}, u32[]{:S(2)}) async-start(bf16[32,16,256]{2,1,0:T(8,128)(2,1)} %bitcast.27), calls=%async_computation.2 | async-start | bytes 524288 | tf_op jit(solution)/shard_map/all_to_all | solution.py:70
  135.4 9.7 %all-to-all-done.2 = bf16[32,16,256]{2,1,0:T(8,128)(2,1)S(1)} async-done(((bf16[32,16,256]{2,1,0:T(8,128)(2,1)}), bf16[32,16,256]{2,1,0:T(8,128)(2,1)S(1)}, u32[]{:S(2)}, u32[]{:S(2)}) %all-to-all-start.2) | async-done | bytes 262176 | tf_op jit(solution)/shard_map/all_to_all | solution.py:70
  145.6 1.9 %collective-permute-start.12 = (bf16[256,256]{1,0:T(8,128)(2,1)S(1)}, bf16[256,256]{1,0:T(8,128)(2,1)S(1)}, u32[]{:S(2)}, u32[]{:S(2)}) collective-permute-start(bf16[256,256]{1,0:T(8,128)(2,1)S(1)} %get-tuple-element.52), channel_id=1, source_target_pairs={{0,6},{2,0},{4,2},{6,4},{1,7},{3,1},{5,3},{7,5},{8,14},{10,8},{12,... | collective-permute-start | bytes 393224 | tf_op jit(solution)/shard_map/ppermute | solution.py:54
  148.2 2.6 %collective-permute-done.12 = bf16[256,256]{1,0:T(8,128)(2,1)S(1)} collective-permute-done((bf16[256,256]{1,0:T(8,128)(2,1)S(1)}, bf16[256,256]{1,0:T(8,128)(2,1)S(1)}, u32[]{:S(2)}, u32[]{:S(2)}) %collective-permute-start.12) | collective-permute-done | bytes 131104 | tf_op jit(solution)/shard_map/ppermute | solution.py:54
  150.8 2.1 %collective-permute-done.13 = bf16[256,256]{1,0:T(8,128)(2,1)S(1)} collective-permute-done((bf16[256,256]{1,0:T(8,128)(2,1)S(1)}, bf16[256,256]{1,0:T(8,128)(2,1)S(1)}, u32[]{:S(2)}, u32[]{:S(2)}) %collective-permute-start.13) | collective-permute-done | bytes 131104 | tf_op jit(solution)/shard_map/ppermute | solution.py:54
  152.9 1.3 collective-permute-done.14
  154.3 5.2 %collective-permute-start.15 = (bf16[4,256,256]{2,1,0:T(8,128)(2,1)S(1)}, bf16[4,256,256]{2,1,0:T(8,128)(2,1)S(1)}, u32[]{:S(2)}, u32[]{:S(2)}) collective-permute-start(bf16[4,256,256]{2,1,0:T(8,128)(2,1)S(1)} %pad_maximum_fusion), channel_id=1, source_target_pairs={{0,1},{1,0},{2,3},{3,2},{4,5},{5,4},{6,7},{7,6},{8,9},{9,8},{10,11... | collective-permute-start | bytes 1572872 | tf_op jit(solution)/shard_map/ppermute | solution.py:66
  160.1 0.9 collective-permute-done.15
  161.1 1.0 copy-done.10
  (86 shorter events, 10.7 us)
Async XLA Ops:
  0.6 1.6 copy-start
  25.7 24.5 %all-to-all-start.1 = ((bf16[32,16,256]{2,1,0:T(8,128)(2,1)}), bf16[32,16,256]{2,1,0:T(8,128)(2,1)S(1)}, u32[]{:S(2)}, u32[]{:S(2)}) async-start(bf16[32,16,256]{2,1,0:T(8,128)(2,1)} %bitcast.4), calls=%async_computation.1 | async-start | bytes 524288 | tf_op jit(solution)/shard_map/all_to_all | solution.py:70
  32.0 8.2 %collective-permute-start = (bf16[256,512]{0,1:T(8,128)(2,1)S(1)}, bf16[256,512]{0,1:T(8,128)(2,1)S(1)}, u32[]{:S(2)}, u32[]{:S(2)}) collective-permute-start(bf16[256,512]{0,1:T(8,128)(2,1)S(1)} %bitcast.101), channel_id=1, source_target_pairs={{0,6},{2,0},{4,2},{6,4},{1,7},{3,1},{5,3},{7,5},{8,14},{10,8},{12,... | collective-permute-start | bytes 786440 | tf_op jit(solution)/shard_map/ppermute | solution.py:54
  34.8 7.3 %collective-permute-start.1 = (bf16[256,512]{0,1:T(8,128)(2,1)S(1)}, bf16[256,512]{0,1:T(8,128)(2,1)S(1)}, u32[]{:S(2)}, u32[]{:S(2)}) collective-permute-start(bf16[256,512]{0,1:T(8,128)(2,1)S(1)} %bitcast.102), channel_id=1, source_target_pairs={{0,4},{2,6},{4,0},{6,2},{1,5},{3,7},{5,1},{7,3},{8,12},{10,14},{12... | collective-permute-start | bytes 786440 | tf_op jit(solution)/shard_map/ppermute | solution.py:54
  35.1 15.0 %collective-permute-start.2 = (bf16[256,512]{0,1:T(8,128)(2,1)S(1)}, bf16[256,512]{0,1:T(8,128)(2,1)S(1)}, u32[]{:S(2)}, u32[]{:S(2)}) collective-permute-start(bf16[256,512]{0,1:T(8,128)(2,1)S(1)} %bitcast.103), channel_id=1, source_target_pairs={{0,2},{2,4},{4,6},{6,0},{1,3},{3,5},{5,7},{7,1},{8,10},{10,12},{12... | collective-permute-start | bytes 786440 | tf_op jit(solution)/shard_map/ppermute | solution.py:54
  52.8 19.5 %collective-permute-start.3 = (bf16[1024,512]{1,0:T(8,128)(2,1)}, bf16[1024,512]{1,0:T(8,128)(2,1)}, u32[]{:S(2)}, u32[]{:S(2)}) collective-permute-start(bf16[1024,512]{1,0:T(8,128)(2,1)} %bitcast.15), channel_id=1, source_target_pairs={{0,1},{1,0},{2,3},{3,2},{4,5},{5,4},{6,7},{7,6},{8,9},{9,8},{10,11... | collective-permute-start | bytes 3145736 | tf_op jit(solution)/shard_map/ppermute | solution.py:66
  57.1 1.8 %copy-start.1 = (bf16[2048,896]{1,0:T(8,128)(2,1)}, bf16[2048,896]{1,0:T(8,128)(2,1)S(1)}, u32[]{:S(2)}) copy-start(bf16[2048,896]{1,0:T(8,128)(2,1)S(1)} %sign_table.1) | copy-start | bytes 11010052
  58.9 5.6 %copy-start.15 = (bf16[1,2048,896]{2,1,0:T(8,128)(2,1)S(1)}, bf16[1,2048,896]{2,1,0:T(8,128)(2,1)}, u32[]{:S(2)}) copy-start(bf16[1,2048,896]{2,1,0:T(8,128)(2,1)} %param.11) | copy-start | bytes 11010052
  58.9 26.7 %collective-permute-start.4 = (bf16[256,512]{0,1:T(8,128)(2,1)S(1)}, bf16[256,512]{0,1:T(8,128)(2,1)S(1)}, u32[]{:S(2)}, u32[]{:S(2)}) collective-permute-start(bf16[256,512]{0,1:T(8,128)(2,1)S(1)} %bitcast.97), channel_id=1, source_target_pairs={{0,6},{2,0},{4,2},{6,4},{1,7},{3,1},{5,3},{7,5},{8,14},{10,8},{12,... | collective-permute-start | bytes 786440 | tf_op jit(solution)/shard_map/ppermute | solution.py:54
  59.2 26.4 %collective-permute-start.5 = (bf16[256,512]{0,1:T(8,128)(2,1)S(1)}, bf16[256,512]{0,1:T(8,128)(2,1)S(1)}, u32[]{:S(2)}, u32[]{:S(2)}) collective-permute-start(bf16[256,512]{0,1:T(8,128)(2,1)S(1)} %bitcast.98), channel_id=1, source_target_pairs={{0,4},{2,6},{4,0},{6,2},{1,5},{3,7},{5,1},{7,3},{8,12},{10,14},{12... | collective-permute-start | bytes 786440 | tf_op jit(solution)/shard_map/ppermute | solution.py:54
  59.5 26.0 %collective-permute-start.6 = (bf16[256,512]{0,1:T(8,128)(2,1)S(1)}, bf16[256,512]{0,1:T(8,128)(2,1)S(1)}, u32[]{:S(2)}, u32[]{:S(2)}) collective-permute-start(bf16[256,512]{0,1:T(8,128)(2,1)S(1)} %bitcast.99), channel_id=1, source_target_pairs={{0,2},{2,4},{4,6},{6,0},{1,3},{3,5},{5,7},{7,1},{8,10},{10,12},{12... | collective-permute-start | bytes 786440 | tf_op jit(solution)/shard_map/ppermute | solution.py:54
  64.5 3.8 %copy-start.18 = (bf16[1,2048,896]{2,1,0:T(8,128)(2,1)S(1)}, bf16[1,2048,896]{2,1,0:T(8,128)(2,1)}, u32[]{:S(2)}) copy-start(bf16[1,2048,896]{2,1,0:T(8,128)(2,1)} %param.10) | copy-start | bytes 11010052
  72.3 3.7 %copy-start.16 = (bf16[1,2048,896]{2,1,0:T(8,128)(2,1)S(1)}, bf16[1,2048,896]{2,1,0:T(8,128)(2,1)}, u32[]{:S(2)}) copy-start(bf16[1,2048,896]{2,1,0:T(8,128)(2,1)} %param.11) | copy-start | bytes 11010052
  72.3 4.0 %copy-start.21 = (f32[896,512]{1,0:T(8,128)S(1)}, f32[896,512]{1,0:T(8,128)}, u32[]{:S(2)}) copy-start(f32[896,512]{1,0:T(8,128)} %fusion.17) | copy-start | bytes 5505028
  76.3 2.5 %copy-start.2 = (bf16[2048,896]{1,0:T(8,128)(2,1)S(1)}, bf16[2048,896]{1,0:T(8,128)(2,1)}, u32[]{:S(2)}) copy-start(bf16[2048,896]{1,0:T(8,128)(2,1)} %copy-done.1) | copy-start | bytes 11010052
  76.3 2.9 %copy-start.22 = (f32[896,512]{1,0:T(8,128)S(1)}, f32[896,512]{1,0:T(8,128)}, u32[]{:S(2)}) copy-start(f32[896,512]{1,0:T(8,128)} %fusion.37) | copy-start | bytes 5505028
  86.1 4.1 %copy-start.11 = (bf16[1,896,2048]{2,1,0:T(8,128)(2,1)S(1)}, bf16[1,896,2048]{2,1,0:T(8,128)(2,1)}, u32[]{:S(2)}) copy-start(bf16[1,896,2048]{2,1,0:T(8,128)(2,1)} %param.12) | copy-start | bytes 11010052
  86.1 4.1 %copy-start.6 = (f32[896,512]{1,0:T(8,128)S(1)}, f32[896,512]{1,0:T(8,128)}, u32[]{:S(2)}) copy-start(f32[896,512]{1,0:T(8,128)} %get-tuple-element.39) | copy-start | bytes 5505028
  86.2 4.1 %copy-start.7 = (f32[896,512]{1,0:T(8,128)S(1)}, f32[896,512]{1,0:T(8,128)}, u32[]{:S(2)}) copy-start(f32[896,512]{1,0:T(8,128)} %get-tuple-element.36) | copy-start | bytes 5505028
  86.2 4.2 %copy-start.8 = (f32[896,512]{1,0:T(8,128)S(1)}, f32[896,512]{1,0:T(8,128)}, u32[]{:S(2)}) copy-start(f32[896,512]{1,0:T(8,128)} %get-tuple-element.38) | copy-start | bytes 5505028
  86.2 4.7 %copy-start.9 = (f32[896,512]{1,0:T(8,128)S(1)}, f32[896,512]{1,0:T(8,128)}, u32[]{:S(2)}) copy-start(f32[896,512]{1,0:T(8,128)} %get-tuple-element.37) | copy-start | bytes 5505028
  86.2 4.0 %collective-permute-start.7 = (bf16[1024,512]{1,0:T(8,128)(2,1)S(1)}, bf16[1024,512]{1,0:T(8,128)(2,1)S(1)}, u32[]{:S(2)}, u32[]{:S(2)}) collective-permute-start(bf16[1024,512]{1,0:T(8,128)(2,1)S(1)} %bitcast.95), channel_id=1, source_target_pairs={{0,1},{1,0},{2,3},{3,2},{4,5},{5,4},{6,7},{7,6},{8,9},{9,8},{10,11... | collective-permute-start | bytes 3145736 | tf_op jit(solution)/shard_map/ppermute | solution.py:66
  90.2 2.3 %copy-start.17 = (bf16[1,2048,896]{2,1,0:T(8,128)(2,1)S(1)}, bf16[1,2048,896]{2,1,0:T(8,128)(2,1)}, u32[]{:S(2)}) copy-start(bf16[1,2048,896]{2,1,0:T(8,128)(2,1)} %param.11) | copy-start | bytes 11010052
  92.4 1.4 copy-start.14
  92.4 1.4 copy-start.12
  92.4 2.7 %copy-start.19 = (bf16[1,2048,896]{2,1,0:T(8,128)(2,1)S(1)}, bf16[1,2048,896]{2,1,0:T(8,128)(2,1)}, u32[]{:S(2)}) copy-start(bf16[1,2048,896]{2,1,0:T(8,128)(2,1)} %param.10) | copy-start | bytes 11010052
  95.1 2.0 %copy-start.3 = (bf16[2048,896]{1,0:T(8,128)(2,1)S(1)}, bf16[2048,896]{1,0:T(8,128)(2,1)}, u32[]{:S(2)}) copy-start(bf16[2048,896]{1,0:T(8,128)(2,1)} %copy-done.1) | copy-start | bytes 11010052
  99.5 5.1 %collective-permute-start.8 = (bf16[1024,512]{0,1:T(8,128)(2,1)}, bf16[1024,512]{0,1:T(8,128)(2,1)S(1)}, u32[]{:S(2)}, u32[]{:S(2)}) collective-permute-start(bf16[1024,512]{0,1:T(8,128)(2,1)} %add_convert_fusion), channel_id=1, source_target_pairs={{0,1},{1,0},{2,3},{3,2},{4,5},{5,4},{6,7},{7,6},{8,9},{9,8},{10,11... | collective-permute-start | bytes 3145736 | tf_op jit(solution)/shard_map/ppermute | solution.py:66
  100.1 3.2 %copy-start.13 = (bf16[896,512]{1,0:T(8,128)(2,1)S(1)}, bf16[896,512]{1,0:T(8,128)(2,1)}, u32[]{:S(2)}) copy-start(bf16[896,512]{1,0:T(8,128)(2,1)} %copy-done.12) | copy-start | bytes 2752516
  100.1 3.2 %copy-start.20 = (bf16[1,2048,896]{2,1,0:T(8,128)(2,1)S(1)}, bf16[1,2048,896]{2,1,0:T(8,128)(2,1)}, u32[]{:S(2)}) copy-start(bf16[1,2048,896]{2,1,0:T(8,128)(2,1)} %param.10) | copy-start | bytes 11010052
  103.3 2.0 %copy-start.4 = (bf16[2048,896]{1,0:T(8,128)(2,1)S(1)}, bf16[2048,896]{1,0:T(8,128)(2,1)}, u32[]{:S(2)}) copy-start(bf16[2048,896]{1,0:T(8,128)(2,1)} %copy-done.1) | copy-start | bytes 11010052
  106.7 1.4 copy-start.5
  108.2 9.2 %collective-permute-start.10 = (bf16[256,512]{0,1:T(8,128)(2,1)S(1)}, bf16[256,512]{0,1:T(8,128)(2,1)S(1)}, u32[]{:S(2)}, u32[]{:S(2)}) collective-permute-start(bf16[256,512]{0,1:T(8,128)(2,1)S(1)} %get-tuple-element.46), channel_id=1, source_target_pairs={{0,2},{2,4},{4,6},{6,0},{1,3},{3,5},{5,7},{7,1},{8,10},{10,12},{12... | collective-permute-start | bytes 786440 | tf_op jit(solution)/shard_map/ppermute | solution.py:54
  110.0 8.2 %collective-permute-start.11 = (bf16[256,512]{0,1:T(8,128)(2,1)S(1)}, bf16[256,512]{0,1:T(8,128)(2,1)S(1)}, u32[]{:S(2)}, u32[]{:S(2)}) collective-permute-start(bf16[256,512]{0,1:T(8,128)(2,1)S(1)} %get-tuple-element.45), channel_id=1, source_target_pairs={{0,6},{2,0},{4,2},{6,4},{1,7},{3,1},{5,3},{7,5},{8,14},{10,8},{12,... | collective-permute-start | bytes 786440 | tf_op jit(solution)/shard_map/ppermute | solution.py:54
  110.9 13.5 %collective-permute-start.9 = (bf16[256,512]{0,1:T(8,128)(2,1)S(1)}, bf16[256,512]{0,1:T(8,128)(2,1)S(1)}, u32[]{:S(2)}, u32[]{:S(2)}) collective-permute-start(bf16[256,512]{0,1:T(8,128)(2,1)S(1)} %get-tuple-element.44), channel_id=1, source_target_pairs={{0,4},{2,6},{4,0},{6,2},{1,5},{3,7},{5,1},{7,3},{8,12},{10,14},{12... | collective-permute-start | bytes 786440 | tf_op jit(solution)/shard_map/ppermute | solution.py:54
  126.2 18.9 %all-to-all-start.2 = ((bf16[32,16,256]{2,1,0:T(8,128)(2,1)}), bf16[32,16,256]{2,1,0:T(8,128)(2,1)S(1)}, u32[]{:S(2)}, u32[]{:S(2)}) async-start(bf16[32,16,256]{2,1,0:T(8,128)(2,1)} %bitcast.27), calls=%async_computation.2 | async-start | bytes 524288 | tf_op jit(solution)/shard_map/all_to_all | solution.py:70
  145.6 5.2 %collective-permute-start.12 = (bf16[256,256]{1,0:T(8,128)(2,1)S(1)}, bf16[256,256]{1,0:T(8,128)(2,1)S(1)}, u32[]{:S(2)}, u32[]{:S(2)}) collective-permute-start(bf16[256,256]{1,0:T(8,128)(2,1)S(1)} %get-tuple-element.52), channel_id=1, source_target_pairs={{0,6},{2,0},{4,2},{6,4},{1,7},{3,1},{5,3},{7,5},{8,14},{10,8},{12,... | collective-permute-start | bytes 393224 | tf_op jit(solution)/shard_map/ppermute | solution.py:54
  147.5 5.4 %collective-permute-start.13 = (bf16[256,256]{1,0:T(8,128)(2,1)S(1)}, bf16[256,256]{1,0:T(8,128)(2,1)S(1)}, u32[]{:S(2)}, u32[]{:S(2)}) collective-permute-start(bf16[256,256]{1,0:T(8,128)(2,1)S(1)} %get-tuple-element.52), channel_id=1, source_target_pairs={{0,4},{2,6},{4,0},{6,2},{1,5},{3,7},{5,1},{7,3},{8,12},{10,14},{12... | collective-permute-start | bytes 393224 | tf_op jit(solution)/shard_map/ppermute | solution.py:54
  148.2 6.0 %collective-permute-start.14 = (bf16[256,256]{1,0:T(8,128)(2,1)S(1)}, bf16[256,256]{1,0:T(8,128)(2,1)S(1)}, u32[]{:S(2)}, u32[]{:S(2)}) collective-permute-start(bf16[256,256]{1,0:T(8,128)(2,1)S(1)} %get-tuple-element.52), channel_id=1, source_target_pairs={{0,2},{2,4},{4,6},{6,0},{1,3},{3,5},{5,7},{7,1},{8,10},{10,12},{12... | collective-permute-start | bytes 393224 | tf_op jit(solution)/shard_map/ppermute | solution.py:54
  154.3 6.7 %collective-permute-start.15 = (bf16[4,256,256]{2,1,0:T(8,128)(2,1)S(1)}, bf16[4,256,256]{2,1,0:T(8,128)(2,1)S(1)}, u32[]{:S(2)}, u32[]{:S(2)}) collective-permute-start(bf16[4,256,256]{2,1,0:T(8,128)(2,1)S(1)} %pad_maximum_fusion), channel_id=1, source_target_pairs={{0,1},{1,0},{2,3},{3,2},{4,5},{5,4},{6,7},{7,6},{8,9},{9,8},{10,11... | collective-permute-start | bytes 1572872 | tf_op jit(solution)/shard_map/ppermute | solution.py:66
  161.1 1.0 copy-start.10

commit v4 on v3

v4 whole, which is shorter than its diff:
```python
import functools
import math

import jax
import jax.numpy as jnp
from jax import lax
from jax.experimental import pallas as pl
from jax.experimental.pallas import tpu as pltpu
from jax.sharding import Mesh, PartitionSpec as P

EXPERT = ("x", "z")
SWAP = [(0, 1), (1, 0)]
BF16 = jnp.bfloat16
F32 = jnp.float32
VMEM = 63 * 1024 * 1024


ORDER = (2, 1, 3, 0)


def dispatch_kernel(route_ref, tokens_ref, cot_ref, dispatch_ref, send_ref, pieces, sems):
    count = route_ref.shape[1]
    slots, width = dispatch_ref.shape[0], send_ref.shape[1] // 2
    slot_count = slots // lax.axis_size(EXPERT)
    start = (lax.axis_index("c") * lax.axis_size("y") + lax.axis_index("y")) * width
    columns = pl.ds(pl.multiple_of(start, width), width)
    copies = [
        pltpu.make_async_copy(ref.at[:, columns], pieces.at[:, pl.ds(at * width, width)], sems.at[at])
        for at, ref in enumerate((tokens_ref, cot_ref))
    ]
    for copy in copies:
        copy.start()
    across = jnp.broadcast_to(route_ref[...], (count, count))
    down = across.T
    earlier = (down == across) & (
        lax.broadcasted_iota(jnp.int32, (count, count), 0) < lax.broadcasted_iota(jnp.int32, (count, count), 1)
    )
    place = jnp.sum(jnp.where(earlier, 1.0, 0.0), axis=0, keepdims=True).astype(jnp.int32)
    target = route_ref[...] * slot_count + place
    slot = lax.broadcasted_iota(jnp.int32, (slots, count), 0)
    dispatch = jnp.where(slot == target, 1.0, 0.0).astype(BF16)
    dispatch_ref[...] = dispatch
    for copy in copies:
        copy.wait()
    send_ref[...] = jnp.dot(dispatch, pieces[...], preferred_element_type=F32).astype(BF16)


def dispatch_rows(route, tokens, cotangent, slots, width):
    count = tokens.shape[0]
    vmem = pl.BlockSpec(memory_space=pltpu.VMEM)
    anywhere = pl.BlockSpec(memory_space=pl.ANY)
    return pl.pallas_call(
        dispatch_kernel,
        out_shape=[jax.ShapeDtypeStruct((slots, count), BF16), jax.ShapeDtypeStruct((slots, 2 * width), BF16)],
        in_specs=[vmem, anywhere, anywhere],
        out_specs=[vmem, vmem],
        scratch_shapes=[pltpu.VMEM((count, 2 * width), BF16), pltpu.SemaphoreType.DMA((2,))],
        compiler_params=pltpu.CompilerParams(vmem_limit_bytes=VMEM),
        name="dispatch",
    )(route.reshape(1, count), tokens, cotangent)


def stage_kernel(info_ref, gate_ref, up_ref, down_ref, gate_out, up_out, down_out, sign_out, *, block_of):
    rows, cols = sign_out.shape
    gate_out[...] = gate_ref[0]
    up_out[...] = up_ref[0]
    down_out[...] = down_ref[0]
    first = block_of(pl.program_id(0), info_ref) * rows
    col = lax.broadcasted_iota(jnp.int32, (1, cols), 1) + info_ref[2]
    base = col * jnp.int32(19349663) + info_ref[3] * jnp.int32(83492791)
    scale = jnp.asarray(1.0 / math.sqrt(2048), BF16).astype(F32)
    step = 8
    for at in range(0, rows, step):
        row = lax.broadcasted_iota(jnp.int32, (step, 1), 0) + (first + at)
        mixed = row * jnp.int32(73856093) + base
        mixed = mixed ^ mixed >> 15
        mixed = mixed * jnp.int32(735632791)
        mixed = mixed ^ mixed >> 13
        mixed = mixed * jnp.int32(1274126177)
        mixed = mixed ^ mixed >> 16
        sign_out[at : at + step, :] = jnp.where((mixed & 32) != 0, scale, -scale).astype(BF16)


def stage_weights(info, w_gate, w_up, w_down, ys, width):
    model, hidden = w_gate.shape[1:]

    def block_of(i, p):
        k = lax.rem(i, ys)
        shift = jnp.where(k == 0, ORDER[0], jnp.where(k == 1, ORDER[1], jnp.where(k == 2, ORDER[2], ORDER[3])))
        core_of = jnp.where(i < ys, p[1], 1 - p[1])
        return core_of * ys + lax.rem(p[0] + shift, ys)

    rows_in = pl.BlockSpec((1, width, hidden), lambda i, p: (0, block_of(i, p), 0))
    rows_out = pl.BlockSpec((width, hidden), lambda i, p: (i, 0))
    return pl.pallas_call(
        functools.partial(stage_kernel, block_of=block_of),
        out_shape=[
            jax.ShapeDtypeStruct((model, hidden), BF16),
            jax.ShapeDtypeStruct((model, hidden), BF16),
            jax.ShapeDtypeStruct((hidden, model), BF16),
            jax.ShapeDtypeStruct((model, hidden), BF16),
        ],
        grid_spec=pltpu.PrefetchScalarGridSpec(
            num_scalar_prefetch=1,
            grid=(2 * ys,),
            in_specs=[rows_in, rows_in, pl.BlockSpec((1, hidden, width), lambda i, p: (0, 0, block_of(i, p)))],
            out_specs=[rows_out, rows_out, pl.BlockSpec((hidden, width), lambda i, p: (0, i)), rows_out],
        ),
        compiler_params=pltpu.CompilerParams(vmem_limit_bytes=VMEM),
        cost_estimate=pl.CostEstimate(flops=0, bytes_accessed=14 * model * hidden, transcendentals=0),
        name="stage_weights",
    )(info, w_gate, w_up, w_down)


def dot(a, b, ca, cb):
    return lax.dot_general(a, b, (((ca,), (cb,)), ((), ())), preferred_element_type=F32)


def shift_y(value, shift):
    count = lax.axis_size("y")
    return lax.ppermute(value, "y", [(i, (i + shift) % count) for i in range(count)])


def swap_cores(value):
    return lax.ppermute(value, "c", SWAP)


def exchange(value):
    return lax.all_to_all(value, EXPERT, split_axis=0, concat_axis=0, tiled=True)


def forward_factors(pre, lin, tangent):
    sig = jax.nn.sigmoid(pre)
    rest = 1.0 - sig
    slope = sig * (1.0 + pre * rest)
    bend = sig * rest * (2.0 + pre * (1.0 - 2.0 * sig))
    third = lin * bend * tangent
    return (lin * slope, slope * tangent, third, third * tangent)


def body(tokens, cotangent, expert_route, w_gate, w_up, w_down, sign_seeds):
    expert_count = lax.axis_size(EXPERT)
    ys, cores = lax.axis_size("y"), lax.axis_size("c")
    y, core = lax.axis_index("y"), lax.axis_index("c")
    tok_count, model_width = tokens.shape
    hidden_cols = w_gate.shape[2]
    slot_count = max(2, 2 * tok_count // expert_count)
    rows = expert_count * slot_count
    width = model_width // (ys * cores)
    half = ys * width
    barrier = lax.optimization_barrier

    def to_experts(send):
        return exchange(send.reshape(expert_count, slot_count, -1)).reshape(rows, -1)

    def gather_y(piece):
        return [piece if step == 0 else shift_y(piece, ys - step) for step in ORDER]

    dispatch, send = dispatch_rows(expert_route, tokens, cotangent, rows, width)
    send, seed = barrier((send, sign_seeds[0]))
    info = jnp.stack([y, core, (y * cores + core) * hidden_cols, seed]).astype(jnp.int32)
    gate, up, down, signs = stage_weights(info, w_gate, w_up, w_down, ys, width)
    received, gate, up, down, signs = barrier((to_experts(send), gate, up, down, signs))
    x_pieces = gather_y(received[:, :width].T)
    x_pieces, cot_piece = barrier((x_pieces, received[:, width:].T))
    x_own = jnp.concatenate(x_pieces, axis=0)
    x = jnp.concatenate([x_own, swap_cores(x_own)], axis=0)
    cot_pieces = gather_y(cot_piece)
    factors = forward_factors(*[dot(w, x, 0, 0) for w in (gate, up, signs)])
    factors, cot_pieces = barrier((factors, cot_pieces))
    cot_own = jnp.concatenate(cot_pieces, axis=0)
    cot_other = swap_cores(cot_own)
    first = barrier(dot(down[:, :half], cot_own, 1, 0))
    h = first + dot(down[:, half:], cot_other, 1, 0)
    ggate, tup, tgate = [(h * f).astype(BF16) for f in factors[:3]]
    curvature = jnp.sum(h * factors[3], axis=1)

    def tangent(grads, start, stop):
        return sum(dot(w[start:stop], g, 1, 0) for w, g in zip((gate, up, signs), grads))

    def pairs(grads, start, stop):
        give = tangent(grads, half + start, half + stop).astype(BF16)
        return tangent(grads, start, stop) + swap_cores(give).astype(F32)

    grads = (tgate, tup, ggate)
    far, grads = barrier((pairs(grads, 0, width), grads))
    near = pairs(grads, width, half)
    total = near[(ys - 2) * width :] + shift_y(far.astype(BF16), ORDER[0]).astype(F32)
    for at in range(ys - 2):
        total = total + shift_y(near[at * width : (at + 1) * width].astype(BF16), ORDER[at + 1]).astype(F32)
    returned = to_experts(total.astype(BF16).T)
    combined = dot(dispatch, returned, 0, 0).astype(BF16)
    own = jnp.stack(gather_y(combined))
    result = jnp.zeros((tok_count, model_width), BF16)
    for blocks, of_core in ((own, core), (swap_cores(own), 1 - core)):
        for at, step in enumerate(ORDER):
            column = (of_core * ys + lax.rem(y + step, ys)) * width
            result = lax.dynamic_update_slice_in_dim(result, blocks[at], column, 1)
    return (result, curvature[None, :])


def solution(mesh):
    chips = Mesh(mesh.devices.reshape(4, 8, 4, 2), ("x", "z", "y", "c"))
    expert, dp = EXPERT, ("y", "c")
    in_specs = (
        P(expert, None),
        P(expert, None),
        P(expert, None),
        P(expert, None, dp),
        P(expert, None, dp),
        P(expert, dp, None),
        P(expert),
    )
    out_specs = (P(expert, None), P(expert, dp))
    return jax.shard_map(body, mesh=chips, in_specs=in_specs, out_specs=out_specs, check_vma=False)
```

time: 163 us -> 125 us (0.77)
  matrix products: 42.1 us -> 18.8 us
  waiting for transfers between devices: 39.2 us -> 27.2 us
  Pallas kernels: 3.73 us -> 15.5 us
  local copies, waits for them, and re-layouts: 14.4 us -> 4.1 us
  blocking collectives: 21.3 us -> 18.2 us
  other arithmetic: 3.58 us -> 0.98 us
  starting transfers between devices: 36 us -> 38.2 us
    dot_general x15 -> x18, matrix products: 40 us -> 18.8 us  [dot(): lax.dot_general(a, b, (((ca,), (cb,)), ((), ())), preferred_element_type=...]
    pallas_call x1 -> x2, Pallas kernels: 3.73 us -> 15.5 us  [the longest x1 12.7 us: stage_weights(): pl.pallas_call(functools.partial(stage_kernel, block_of=block_of), out_sh...]
    all_to_all x2 -> x1, waiting for transfers between devices: 9.67 us -> 0.31 us  [exchange(): lax.all_to_all(value, EXPERT, split_axis=0, concat_axis=0, tiled=True)]
    unnamed x46 -> x19, local copies, waits for them, and re-layouts: 8.26 us -> 2.96 us
    ppermute x12, waiting for transfers between devices: 28.6 us -> 24.3 us  [shift_y(): lax.ppermute(value, 'y', [(i, (i + shift) % count) for i in range(count)])]
    ppermute x12, starting transfers between devices: 13.3 us -> 17.7 us  [shift_y(): lax.ppermute(value, 'y', [(i, (i + shift) % count) for i in range(count)])]
    all_to_all x2 -> x1, starting transfers between devices: 15.5 us -> 11.9 us  [exchange(): lax.all_to_all(value, EXPERT, split_axis=0, concat_axis=0, tiled=True)]
    all_to_all x1, blocking collectives: 21.3 us -> 18.2 us  [exchange(): lax.all_to_all(value, EXPERT, split_axis=0, concat_axis=0, tiled=True)]
  transfers between devices with their start and end apart: 18 -> 18, of which waited for: 11 -> 14; matrix products, arithmetic and copies ran while one was open for 21% -> 11% of each run, Pallas kernels for 2% -> 10%
where the time goes in v4:
time: 125 us
  starting transfers between devices  38.2 us (31%)
  waiting for transfers between devices  27.2 us (22%)
  matrix products  18.8 us (15%)
  blocking collectives  18.2 us (15%)
  Pallas kernels  15.5 us (12%)
  local copies, waits for them, and re-layouts  4.1 us (3%)
  between operations  1.66 us (1%)
    ppermute x12, waiting for transfers between devices, shift_y(): lax.ppermute(value, 'y', [(i, (i + shift) % count) for i in range(count)])  24.3 us
    dot_general x18, matrix products, dot(): lax.dot_general(a, b, (((ca,), (cb,)), ((), ())), preferred_element_type=...  18.8 us
    all_to_all x1, blocking collectives, exchange(): lax.all_to_all(value, EXPERT, split_axis=0, concat_axis=0, tiled=True)  18.2 us
    ppermute x12, starting transfers between devices, shift_y(): lax.ppermute(value, 'y', [(i, (i + shift) % count) for i in range(count)])  17.7 us
    pallas_call x1, Pallas kernels, stage_weights(): pl.pallas_call(functools.partial(stage_kernel, block_of=block_of), out_sh...  12.7 us
    all_to_all x1, starting transfers between devices, exchange(): lax.all_to_all(value, EXPERT, split_axis=0, concat_axis=0, tiled=True)  11.9 us
    ppermute x5, starting transfers between devices, swap_cores(): return lax.ppermute(value, 'c', SWAP)  8.64 us
    unnamed x19, local copies, waits for them, and re-layouts  2.96 us
  transfers between devices with their start and end apart: 18, of which 14 were waited for; matrix products, arithmetic and copies ran while one was open for 11% of the time, Pallas kernels for 10%

profile of v4, /device:TPU:1, one launch (start us, length us, event | category | flops | bytes accessed | tf_op | source)
XLA Modules:
  0.0 124.7 jit_solution(4968197722834632891)
XLA Ops:
  0.6 2.8 %dispatch.1 = (bf16[512,256]{1,0:T(8,128)(2,1)}, bf16[512,512]{1,0:T(8,128)(2,1)}) custom-call(s32[1,256]{1,0:T(1,128)} %bitcast.66, bf16[256,2048]{1,0:T(8,128)(2,1)} %tokens_ref.1, bf16[256,2048]{1,0:T(8,128)(2,1)} %cot_ref.1), custom_call_target="tpu_custom_call" | custom-call | tf_op jit(solution)/shard_map/dispatch/pallas_call | solution.py:52
  3.4 11.9 %all-to-all-start = ((bf16[32,16,512]{2,1,0:T(8,128)(2,1)}), bf16[32,16,512]{2,1,0:T(8,128)(2,1)S(1)}, u32[]{:S(2)}, u32[]{:S(2)}) async-start(bf16[32,16,512]{2,1,0:T(8,128)(2,1)} %bitcast.62), calls=%async_computation | async-start | bytes 1048576 | tf_op jit(solution)/shard_map/all_to_all | solution.py:129
  15.9 0.6 pad_add_fusion.info_ref
  16.6 12.7 %stage_weights.1 = (bf16[2048,896]{1,0:T(8,128)(2,1)}, bf16[2048,896]{1,0:T(8,128)(2,1)}, bf16[896,2048]{1,0:T(8,128)(2,1)}, bf16[2048,896]{1,0:T(8,128)(2,1)}) custom-call(s32[4]{0:T(128)} %pad_add_fusion.info_ref, bf16[1,2048,896]{2,1,0:T(8,128)(2,1)} %gate_ref.1, bf16[1,2048,896]{2,1,0:T(8,128)(2,1)} %up_ref.1, bf16[1,896,2048]{2,1,0:T(8,128)(2,1)} %down_ref.1), custom_call_target="tpu_custom_call" | custom-call | bytes 25690112 | tf_op jit(solution)/shard_map/stage_weights/pallas_call | solution.py:95
  29.6 3.0 %collective-permute-start = (bf16[256,512]{0,1:T(8,128)(2,1)S(1)}, bf16[256,512]{0,1:T(8,128)(2,1)S(1)}, u32[]{:S(2)}, u32[]{:S(2)}) collective-permute-start(bf16[256,512]{0,1:T(8,128)(2,1)S(1)} %get-tuple-element.47), channel_id=1, source_target_pairs={{0,4},{2,6},{4,0},{6,2},{1,5},{3,7},{5,1},{7,3},{8,12},{10,14},{12... | collective-permute-start | bytes 786440 | tf_op jit(solution)/shard_map/ppermute | solution.py:121
  32.6 0.8 collective-permute-start.1
  33.4 0.7 collective-permute-start.2
  34.1 2.4 %collective-permute-done = bf16[256,512]{0,1:T(8,128)(2,1)S(1)} collective-permute-done((bf16[256,512]{0,1:T(8,128)(2,1)S(1)}, bf16[256,512]{0,1:T(8,128)(2,1)S(1)}, u32[]{:S(2)}, u32[]{:S(2)}) %collective-permute-start) | collective-permute-done | bytes 262176 | tf_op jit(solution)/shard_map/ppermute | solution.py:121
  36.5 6.2 %collective-permute-done.1 = bf16[256,512]{0,1:T(8,128)(2,1)S(1)} collective-permute-done((bf16[256,512]{0,1:T(8,128)(2,1)S(1)}, bf16[256,512]{0,1:T(8,128)(2,1)S(1)}, u32[]{:S(2)}, u32[]{:S(2)}) %collective-permute-start.1) | collective-permute-done | bytes 262176 | tf_op jit(solution)/shard_map/ppermute | solution.py:121
  42.6 0.8 collective-permute-done.2
  43.5 2.9 %collective-permute-start.3 = (bf16[1024,512]{0,1:T(8,128)(2,1)S(1)}, bf16[1024,512]{0,1:T(8,128)(2,1)S(1)}, u32[]{:S(2)}, u32[]{:S(2)}) collective-permute-start(bf16[1024,512]{0,1:T(8,128)(2,1)S(1)} %pad_maximum_fusion), channel_id=1, source_target_pairs={{0,1},{1,0},{2,3},{3,2},{4,5},{5,4},{6,7},{7,6},{8,9},{9,8},{10,11... | collective-permute-start | bytes 3145736 | tf_op jit(solution)/shard_map/ppermute | solution.py:125
  46.4 2.3 %collective-permute-start.4 = (bf16[256,512]{0,1:T(8,128)(2,1)S(1)}, bf16[256,512]{0,1:T(8,128)(2,1)S(1)}, u32[]{:S(2)}, u32[]{:S(2)}) collective-permute-start(bf16[256,512]{0,1:T(8,128)(2,1)S(1)} %get-tuple-element.53), channel_id=1, source_target_pairs={{0,4},{2,6},{4,0},{6,2},{1,5},{3,7},{5,1},{7,3},{8,12},{10,14},{12... | collective-permute-start | bytes 786440 | tf_op jit(solution)/shard_map/ppermute | solution.py:121
  48.7 1.0 collective-permute-start.5
  49.7 0.5 collective-permute-start.6
  50.4 1.8 %copy-done.4 = bf16[2048,896]{1,0:T(8,128)(2,1)S(1)} copy-done((bf16[2048,896]{1,0:T(8,128)(2,1)S(1)}, bf16[2048,896]{1,0:T(8,128)(2,1)}, u32[]{:S(2)}) %copy-start.4) | copy-done | bytes 3670040
  52.2 2.1 %fusion.47 = f32[896,512]{1,0:T(8,128)S(1)} fusion(bf16[2048,896]{1,0:T(8,128)(2,1)S(1)} %copy-done.4, bf16[2048,512]{0,1:T(8,128)(2,1)S(1)} %constant_dynamic-update-slice_fusion), kind=kOutput, calls=%fused_computation.81 | convolution fusion | flops 1879048192 | bytes 7602176 | tf_op jit(solution)/shard_map/dot_general | solution.py:116
  54.4 2.1 %fusion.46 = f32[896,512]{1,0:T(8,128)S(1)} fusion(bf16[2048,896]{1,0:T(8,128)(2,1)S(1)} %copy-done.5, bf16[2048,512]{0,1:T(8,128)(2,1)S(1)} %constant_dynamic-update-slice_fusion), kind=kOutput, calls=%fused_computation.80 | convolution fusion | flops 1879048192 | bytes 7602176 | tf_op jit(solution)/shard_map/dot_general | solution.py:116
  56.5 3.1 %fusion.42 = (f32[896,512]{1,0:T(8,128)S(1)}, f32[896,512]{1,0:T(8,128)S(1)}, f32[896,512]{1,0:T(8,128)S(1)}, f32[896,512]{1,0:T(8,128)S(1)}) fusion(f32[896,512]{1,0:T(8,128)S(1)} %fusion.46, f32[896,512]{1,0:T(8,128)S(1)} %fusion.47, bf16[2048,896]{1,0:T(8,128)(2,1)S(1)} %copy-done, bf16[2048,512]{0,1:T(8,128)(2,1)S(1)} %constant_dynamic-update-slice_fusion), kind=kOutput, calls=%fused_computation.77 | convolution fusion | flops 1887305728 | bytes 16777216 | tf_op jit(solution)/shard_map/dot_general | solution.py:116
  59.6 1.6 %collective-permute-done.5 = bf16[256,512]{0,1:T(8,128)(2,1)S(1)} collective-permute-done((bf16[256,512]{0,1:T(8,128)(2,1)S(1)}, bf16[256,512]{0,1:T(8,128)(2,1)S(1)}, u32[]{:S(2)}, u32[]{:S(2)}) %collective-permute-start.5) | collective-permute-done | bytes 262176 | tf_op jit(solution)/shard_map/ppermute | solution.py:121
  61.2 0.6 collective-permute-done.6
  61.9 0.6 collective-permute-start.7
  62.5 1.1 fusion.7
  63.6 1.1 collective-permute-done.7
  64.8 1.6 %multiply_reduce_fusion = (f32[896]{0:T(1024)S(1)}, bf16[896,512]{1,0:T(8,128)(2,1)S(1)}, bf16[896,512]{1,0:T(8,128)(2,1)S(1)}, bf16[896,512]{1,0:T(8,128)(2,1)S(1)}) fusion(f32[896,512]{1,0:T(8,128)S(1)} %get-tuple-element.61, f32[896,512]{1,0:T(8,128)S(1)} %get-tuple-element.56, f32[896,512]{1,0:T(8,128)S(1)} %get-tuple-element.55, ...), kind=kOutput, calls=%fused_computation.7 | convolution fusion | flops 943651968 | bytes 14814720 | tf_op jit(solution)/shard_map/dot_general | solution.py:116
  68.1 0.7 collective-permute-start.8
  69.3 0.7 collective-permute-done.8
  70.4 1.0 fusion.13
  71.4 1.0 fusion.15
  72.4 1.0 add_convert_fusion
  73.8 2.3 %collective-permute-start.10 = (bf16[256,512]{1,0:T(8,128)(2,1)S(1)}, bf16[256,512]{1,0:T(8,128)(2,1)S(1)}, u32[]{:S(2)}, u32[]{:S(2)}) collective-permute-start(bf16[256,512]{1,0:T(8,128)(2,1)S(1)} %fusion.22), channel_id=1, source_target_pairs={{0,4},{2,6},{4,0},{6,2},{1,5},{3,7},{5,1},{7,3},{8,12},{10,14},{12... | collective-permute-start | bytes 786440 | tf_op jit(solution)/shard_map/ppermute | solution.py:121
  76.1 1.0 fusion.18
  77.1 1.0 fusion.20
  78.1 1.1 fusion.45
  79.2 0.5 collective-permute-start.11
  79.7 2.3 %collective-permute-start.12 = (bf16[256,512]{1,0:T(8,128)(2,1)S(1)}, bf16[256,512]{1,0:T(8,128)(2,1)S(1)}, u32[]{:S(2)}, u32[]{:S(2)}) collective-permute-start(bf16[256,512]{1,0:T(8,128)(2,1)S(1)} %get-tuple-element.71), channel_id=1, source_target_pairs={{0,6},{2,0},{4,2},{6,4},{1,7},{3,1},{5,3},{7,5},{8,14},{10,8},{12,... | collective-permute-start | bytes 786440 | tf_op jit(solution)/shard_map/ppermute | solution.py:121
  82.0 1.1 collective-permute-done.10
  83.1 5.8 %collective-permute-done.11 = bf16[256,512]{1,0:T(8,128)(2,1)S(1)} collective-permute-done((bf16[256,512]{1,0:T(8,128)(2,1)S(1)}, bf16[256,512]{1,0:T(8,128)(2,1)S(1)}, u32[]{:S(2)}, u32[]{:S(2)}) %collective-permute-start.11) | collective-permute-done | bytes 262176 | tf_op jit(solution)/shard_map/ppermute | solution.py:121
  89.2 18.2 %all_to_all.10 = bf16[32,16,256]{2,1,0:T(8,128)(2,1)S(1)} all-to-all(bf16[32,16,256]{2,1,0:T(8,128)(2,1)S(1)} %bitcast.61), channel_id=1, replica_groups=mesh['x'=4,'z'=8,'y'=4,'c'=2] {'x','z'}, dimensions={0} | all-to-all | bytes 524288 | tf_op jit(solution)/shard_map/all_to_all | solution.py:129
  107.7 2.9 %collective-permute-start.13 = (bf16[256,256]{1,0:T(8,128)(2,1)S(1)}, bf16[256,256]{1,0:T(8,128)(2,1)S(1)}, u32[]{:S(2)}, u32[]{:S(2)}) collective-permute-start(bf16[256,256]{1,0:T(8,128)(2,1)S(1)} %convolution_convert_fusion), channel_id=1, source_target_pairs={{0,4},{2,6},{4,0},{6,2},{1,5},{3,7},{5,1},{7,3},{8,12},{10,14},{12... | collective-permute-start | bytes 393224 | tf_op jit(solution)/shard_map/ppermute | solution.py:121
  110.6 0.9 collective-permute-start.14
  111.5 0.6 collective-permute-start.15
  112.1 1.1 collective-permute-done.13
  113.2 1.3 %collective-permute-done.14 = bf16[256,256]{1,0:T(8,128)(2,1)S(1)} collective-permute-done((bf16[256,256]{1,0:T(8,128)(2,1)S(1)}, bf16[256,256]{1,0:T(8,128)(2,1)S(1)}, u32[]{:S(2)}, u32[]{:S(2)}) %collective-permute-start.14) | collective-permute-done | bytes 131104 | tf_op jit(solution)/shard_map/ppermute | solution.py:121
  114.4 3.5 %collective-permute-done.15 = bf16[256,256]{1,0:T(8,128)(2,1)S(1)} collective-permute-done((bf16[256,256]{1,0:T(8,128)(2,1)S(1)}, bf16[256,256]{1,0:T(8,128)(2,1)S(1)}, u32[]{:S(2)}, u32[]{:S(2)}) %collective-permute-start.15) | collective-permute-done | bytes 131104 | tf_op jit(solution)/shard_map/ppermute | solution.py:121
  118.0 4.0 %collective-permute-start.16 = (bf16[4,256,256]{2,1,0:T(8,128)(2,1)S(1)}, bf16[4,256,256]{2,1,0:T(8,128)(2,1)S(1)}, u32[]{:S(2)}, u32[]{:S(2)}) collective-permute-start(bf16[4,256,256]{2,1,0:T(8,128)(2,1)S(1)} %pad_maximum_fusion.1), channel_id=1, source_target_pairs={{0,1},{1,0},{2,3},{3,2},{4,5},{5,4},{6,7},{7,6},{8,9},{9,8},{10,11... | collective-permute-start | bytes 1572872 | tf_op jit(solution)/shard_map/ppermute | solution.py:125
  122.1 0.6 broadcast_in_dim.7
  122.9 0.7 collective-permute-done.16
  123.7 1.0 copy-done.1
  (47 shorter events, 4.8 us)
Async XLA Ops:
  3.4 26.2 %all-to-all-start = ((bf16[32,16,512]{2,1,0:T(8,128)(2,1)}), bf16[32,16,512]{2,1,0:T(8,128)(2,1)S(1)}, u32[]{:S(2)}, u32[]{:S(2)}) async-start(bf16[32,16,512]{2,1,0:T(8,128)(2,1)} %bitcast.62), calls=%async_computation | async-start | bytes 1048576 | tf_op jit(solution)/shard_map/all_to_all | solution.py:129
  29.6 6.8 %collective-permute-start = (bf16[256,512]{0,1:T(8,128)(2,1)S(1)}, bf16[256,512]{0,1:T(8,128)(2,1)S(1)}, u32[]{:S(2)}, u32[]{:S(2)}) collective-permute-start(bf16[256,512]{0,1:T(8,128)(2,1)S(1)} %get-tuple-element.47), channel_id=1, source_target_pairs={{0,4},{2,6},{4,0},{6,2},{1,5},{3,7},{5,1},{7,3},{8,12},{10,14},{12... | collective-permute-start | bytes 786440 | tf_op jit(solution)/shard_map/ppermute | solution.py:121
  32.6 10.0 %collective-permute-start.1 = (bf16[256,512]{0,1:T(8,128)(2,1)S(1)}, bf16[256,512]{0,1:T(8,128)(2,1)S(1)}, u32[]{:S(2)}, u32[]{:S(2)}) collective-permute-start(bf16[256,512]{0,1:T(8,128)(2,1)S(1)} %get-tuple-element.47), channel_id=1, source_target_pairs={{0,6},{2,0},{4,2},{6,4},{1,7},{3,1},{5,3},{7,5},{8,14},{10,8},{12,... | collective-permute-start | bytes 786440 | tf_op jit(solution)/shard_map/ppermute | solution.py:121
  33.4 10.0 %collective-permute-start.2 = (bf16[256,512]{0,1:T(8,128)(2,1)S(1)}, bf16[256,512]{0,1:T(8,128)(2,1)S(1)}, u32[]{:S(2)}, u32[]{:S(2)}) collective-permute-start(bf16[256,512]{0,1:T(8,128)(2,1)S(1)} %get-tuple-element.47), channel_id=1, source_target_pairs={{0,2},{2,4},{4,6},{6,0},{1,3},{3,5},{5,7},{7,1},{8,10},{10,12},{12... | collective-permute-start | bytes 786440 | tf_op jit(solution)/shard_map/ppermute | solution.py:121
  43.5 6.8 %collective-permute-start.3 = (bf16[1024,512]{0,1:T(8,128)(2,1)S(1)}, bf16[1024,512]{0,1:T(8,128)(2,1)S(1)}, u32[]{:S(2)}, u32[]{:S(2)}) collective-permute-start(bf16[1024,512]{0,1:T(8,128)(2,1)S(1)} %pad_maximum_fusion), channel_id=1, source_target_pairs={{0,1},{1,0},{2,3},{3,2},{4,5},{5,4},{6,7},{7,6},{8,9},{9,8},{10,11... | collective-permute-start | bytes 3145736 | tf_op jit(solution)/shard_map/ppermute | solution.py:125
  46.4 13.2 %collective-permute-start.4 = (bf16[256,512]{0,1:T(8,128)(2,1)S(1)}, bf16[256,512]{0,1:T(8,128)(2,1)S(1)}, u32[]{:S(2)}, u32[]{:S(2)}) collective-permute-start(bf16[256,512]{0,1:T(8,128)(2,1)S(1)} %get-tuple-element.53), channel_id=1, source_target_pairs={{0,4},{2,6},{4,0},{6,2},{1,5},{3,7},{5,1},{7,3},{8,12},{10,14},{12... | collective-permute-start | bytes 786440 | tf_op jit(solution)/shard_map/ppermute | solution.py:121
  48.7 12.4 %collective-permute-start.5 = (bf16[256,512]{0,1:T(8,128)(2,1)S(1)}, bf16[256,512]{0,1:T(8,128)(2,1)S(1)}, u32[]{:S(2)}, u32[]{:S(2)}) collective-permute-start(bf16[256,512]{0,1:T(8,128)(2,1)S(1)} %get-tuple-element.53), channel_id=1, source_target_pairs={{0,6},{2,0},{4,2},{6,4},{1,7},{3,1},{5,3},{7,5},{8,14},{10,8},{12,... | collective-permute-start | bytes 786440 | tf_op jit(solution)/shard_map/ppermute | solution.py:121
  49.7 12.1 %collective-permute-start.6 = (bf16[256,512]{0,1:T(8,128)(2,1)S(1)}, bf16[256,512]{0,1:T(8,128)(2,1)S(1)}, u32[]{:S(2)}, u32[]{:S(2)}) collective-permute-start(bf16[256,512]{0,1:T(8,128)(2,1)S(1)} %get-tuple-element.53), channel_id=1, source_target_pairs={{0,2},{2,4},{4,6},{6,0},{1,3},{3,5},{5,7},{7,1},{8,10},{10,12},{12... | collective-permute-start | bytes 786440 | tf_op jit(solution)/shard_map/ppermute | solution.py:121
  50.2 2.0 %copy-start.4 = (bf16[2048,896]{1,0:T(8,128)(2,1)S(1)}, bf16[2048,896]{1,0:T(8,128)(2,1)}, u32[]{:S(2)}) copy-start(bf16[2048,896]{1,0:T(8,128)(2,1)} %get-tuple-element.40) | copy-start | bytes 11010052
  52.2 2.1 %copy-start.5 = (bf16[2048,896]{1,0:T(8,128)(2,1)S(1)}, bf16[2048,896]{1,0:T(8,128)(2,1)}, u32[]{:S(2)}) copy-start(bf16[2048,896]{1,0:T(8,128)(2,1)} %get-tuple-element.42) | copy-start | bytes 11010052
  54.3 2.1 %copy-start = (bf16[2048,896]{1,0:T(8,128)(2,1)S(1)}, bf16[2048,896]{1,0:T(8,128)(2,1)}, u32[]{:S(2)}) copy-start(bf16[2048,896]{1,0:T(8,128)(2,1)} %get-tuple-element.48) | copy-start | bytes 11010052
  56.5 6.0 %copy-start.2 = (bf16[896,2048]{1,0:T(8,128)(2,1)S(1)}, bf16[896,2048]{1,0:T(8,128)(2,1)}, u32[]{:S(2)}) copy-start(bf16[896,2048]{1,0:T(8,128)(2,1)} %get-tuple-element.41) | copy-start | bytes 11010052
  61.9 2.9 %collective-permute-start.7 = (bf16[1024,512]{0,1:T(8,128)(2,1)S(1)}, bf16[1024,512]{0,1:T(8,128)(2,1)S(1)}, u32[]{:S(2)}, u32[]{:S(2)}) collective-permute-start(bf16[1024,512]{0,1:T(8,128)(2,1)S(1)} %constant_dynamic-update-slice_fusion.5), channel_id=1, source_target_pairs={{0,1},{1,0},{2,3},{3,2},{4,5},{5,4},{6,7},{7,6},{8,9},{9,8},{10,11... | collective-permute-start | bytes 3145736 | tf_op jit(solution)/shard_map/ppermute | solution.py:125
  68.1 1.8 %collective-permute-start.8 = (bf16[256,512]{1,0:T(8,128)(2,1)S(1)}, bf16[256,512]{1,0:T(8,128)(2,1)S(1)}, u32[]{:S(2)}, u32[]{:S(2)}) collective-permute-start(bf16[256,512]{1,0:T(8,128)(2,1)S(1)} %fusion.23), channel_id=1, source_target_pairs={{0,1},{1,0},{2,3},{3,2},{4,5},{5,4},{6,7},{7,6},{8,9},{9,8},{10,11... | collective-permute-start | bytes 786440 | tf_op jit(solution)/shard_map/ppermute | solution.py:125
  73.3 4.7 %collective-permute-start.9 = (bf16[768,512]{1,0:T(8,128)(2,1)S(1)}, bf16[768,512]{1,0:T(8,128)(2,1)S(1)}, u32[]{:S(2)}, u32[]{:S(2)}) collective-permute-start(bf16[768,512]{1,0:T(8,128)(2,1)S(1)} %add_convert_fusion), channel_id=1, source_target_pairs={{0,1},{1,0},{2,3},{3,2},{4,5},{5,4},{6,7},{7,6},{8,9},{9,8},{10,11... | collective-permute-start | bytes 2359304 | tf_op jit(solution)/shard_map/ppermute | solution.py:125
  73.8 9.3 %collective-permute-start.10 = (bf16[256,512]{1,0:T(8,128)(2,1)S(1)}, bf16[256,512]{1,0:T(8,128)(2,1)S(1)}, u32[]{:S(2)}, u32[]{:S(2)}) collective-permute-start(bf16[256,512]{1,0:T(8,128)(2,1)S(1)} %fusion.22), channel_id=1, source_target_pairs={{0,4},{2,6},{4,0},{6,2},{1,5},{3,7},{5,1},{7,3},{8,12},{10,14},{12... | collective-permute-start | bytes 786440 | tf_op jit(solution)/shard_map/ppermute | solution.py:121
  79.2 28.3 %copy-start.3 = (bf16[512,256]{1,0:T(8,128)(2,1)S(1)}, bf16[512,256]{1,0:T(8,128)(2,1)}, u32[]{:S(2)}) copy-start(bf16[512,256]{1,0:T(8,128)(2,1)} %get-tuple-element.32) | copy-start | bytes 786436
  79.2 9.7 %collective-permute-start.11 = (bf16[256,512]{1,0:T(8,128)(2,1)S(1)}, bf16[256,512]{1,0:T(8,128)(2,1)S(1)}, u32[]{:S(2)}, u32[]{:S(2)}) collective-permute-start(bf16[256,512]{1,0:T(8,128)(2,1)S(1)} %get-tuple-element.70), channel_id=1, source_target_pairs={{0,2},{2,4},{4,6},{6,0},{1,3},{3,5},{5,7},{7,1},{8,10},{10,12},{12... | collective-permute-start | bytes 786440 | tf_op jit(solution)/shard_map/ppermute | solution.py:121
  79.7 9.2 %collective-permute-start.12 = (bf16[256,512]{1,0:T(8,128)(2,1)S(1)}, bf16[256,512]{1,0:T(8,128)(2,1)S(1)}, u32[]{:S(2)}, u32[]{:S(2)}) collective-permute-start(bf16[256,512]{1,0:T(8,128)(2,1)S(1)} %get-tuple-element.71), channel_id=1, source_target_pairs={{0,6},{2,0},{4,2},{6,4},{1,7},{3,1},{5,3},{7,5},{8,14},{10,8},{12,... | collective-permute-start | bytes 786440 | tf_op jit(solution)/shard_map/ppermute | solution.py:121
  107.7 5.4 %collective-permute-start.13 = (bf16[256,256]{1,0:T(8,128)(2,1)S(1)}, bf16[256,256]{1,0:T(8,128)(2,1)S(1)}, u32[]{:S(2)}, u32[]{:S(2)}) collective-permute-start(bf16[256,256]{1,0:T(8,128)(2,1)S(1)} %convolution_convert_fusion), channel_id=1, source_target_pairs={{0,4},{2,6},{4,0},{6,2},{1,5},{3,7},{5,1},{7,3},{8,12},{10,14},{12... | collective-permute-start | bytes 393224 | tf_op jit(solution)/shard_map/ppermute | solution.py:121
  110.6 3.8 %collective-permute-start.14 = (bf16[256,256]{1,0:T(8,128)(2,1)S(1)}, bf16[256,256]{1,0:T(8,128)(2,1)S(1)}, u32[]{:S(2)}, u32[]{:S(2)}) collective-permute-start(bf16[256,256]{1,0:T(8,128)(2,1)S(1)} %convolution_convert_fusion), channel_id=1, source_target_pairs={{0,6},{2,0},{4,2},{6,4},{1,7},{3,1},{5,3},{7,5},{8,14},{10,8},{12,... | collective-permute-start | bytes 393224 | tf_op jit(solution)/shard_map/ppermute | solution.py:121
  111.5 6.4 %collective-permute-start.15 = (bf16[256,256]{1,0:T(8,128)(2,1)S(1)}, bf16[256,256]{1,0:T(8,128)(2,1)S(1)}, u32[]{:S(2)}, u32[]{:S(2)}) collective-permute-start(bf16[256,256]{1,0:T(8,128)(2,1)S(1)} %convolution_convert_fusion), channel_id=1, source_target_pairs={{0,2},{2,4},{4,6},{6,0},{1,3},{3,5},{5,7},{7,1},{8,10},{10,12},{12... | collective-permute-start | bytes 393224 | tf_op jit(solution)/shard_map/ppermute | solution.py:121
  118.0 5.6 %collective-permute-start.16 = (bf16[4,256,256]{2,1,0:T(8,128)(2,1)S(1)}, bf16[4,256,256]{2,1,0:T(8,128)(2,1)S(1)}, u32[]{:S(2)}, u32[]{:S(2)}) collective-permute-start(bf16[4,256,256]{2,1,0:T(8,128)(2,1)S(1)} %pad_maximum_fusion.1), channel_id=1, source_target_pairs={{0,1},{1,0},{2,3},{3,2},{4,5},{5,4},{6,7},{7,6},{8,9},{9,8},{10,11... | collective-permute-start | bytes 1572872 | tf_op jit(solution)/shard_map/ppermute | solution.py:125
  123.7 1.0 copy-start.1

commit v5 on v4

v5 whole, which is shorter than its diff:
```python
import functools
import math

import jax
import jax.numpy as jnp
from jax import lax
from jax.experimental import pallas as pl
from jax.experimental.pallas import tpu as pltpu
from jax.sharding import Mesh, PartitionSpec as P

EXPERT = ("x", "z")
SWAP = [(0, 1), (1, 0)]
BF16 = jnp.bfloat16
F32 = jnp.float32
VMEM = 63 * 1024 * 1024


BLOCKS = ((0, 2), (1, 2), (0, 1), (0, 3), (0, 0), (1, 1), (1, 3), (1, 0))


def dispatch_kernel(route_ref, tokens_ref, cot_ref, dispatch_ref, send_ref, pieces, sems):
    count = route_ref.shape[1]
    slots, width = dispatch_ref.shape[0], send_ref.shape[1] // 2
    slot_count = slots // lax.axis_size(EXPERT)
    start = (lax.axis_index("c") * lax.axis_size("y") + lax.axis_index("y")) * width
    columns = pl.ds(pl.multiple_of(start, width), width)
    copies = [
        pltpu.make_async_copy(ref.at[:, columns], pieces.at[:, pl.ds(at * width, width)], sems.at[at])
        for at, ref in enumerate((tokens_ref, cot_ref))
    ]
    for copy in copies:
        copy.start()
    across = jnp.broadcast_to(route_ref[...], (count, count))
    down = across.T
    earlier = (down == across) & (
        lax.broadcasted_iota(jnp.int32, (count, count), 0) < lax.broadcasted_iota(jnp.int32, (count, count), 1)
    )
    place = jnp.sum(jnp.where(earlier, 1.0, 0.0), axis=0, keepdims=True).astype(jnp.int32)
    target = route_ref[...] * slot_count + place
    slot = lax.broadcasted_iota(jnp.int32, (slots, count), 0)
    dispatch = jnp.where(slot == target, 1.0, 0.0).astype(BF16)
    dispatch_ref[...] = dispatch
    for copy in copies:
        copy.wait()
    send_ref[...] = jnp.dot(dispatch, pieces[...], preferred_element_type=F32).astype(BF16)


def dispatch_rows(route, tokens, cotangent, slots, width):
    count = tokens.shape[0]
    vmem = pl.BlockSpec(memory_space=pltpu.VMEM)
    hbm = pl.BlockSpec(memory_space=pltpu.HBM)
    return pl.pallas_call(
        dispatch_kernel,
        out_shape=[jax.ShapeDtypeStruct((slots, count), BF16), jax.ShapeDtypeStruct((slots, 2 * width), BF16)],
        in_specs=[vmem, hbm, hbm],
        out_specs=[vmem, vmem],
        scratch_shapes=[pltpu.VMEM((count, 2 * width), BF16), pltpu.SemaphoreType.DMA((2,))],
        compiler_params=pltpu.CompilerParams(vmem_limit_bytes=24 * 1024 * 1024),
        name="dispatch",
    )(route.reshape(1, count), *[pltpu.with_memory_space_constraint(a, pltpu.HBM) for a in (tokens, cotangent)])


def stage_kernel(seed_ref, gate_ref, up_ref, down_ref, mats_ref, cuts_ref, sems):
    hidden = gate_ref.shape[2]
    ys = lax.axis_size("y")
    y, core = lax.axis_index("y"), lax.axis_index("c")
    width = mats_ref.shape[0] // len(BLOCKS)

    def block(other, step):
        return lax.rem(core + other, 2) * ys + lax.rem(y + step, ys)

    copies = []
    for at, (other, step) in enumerate(BLOCKS):
        source = pl.ds(pl.multiple_of(block(other, step) * width, width), width)
        target = pl.ds(at * width, width)
        for which, (from_ref, to_ref) in enumerate(
            (
                (gate_ref.at[0, source, :], mats_ref.at[target, pl.ds(0, hidden)]),
                (up_ref.at[0, source, :], mats_ref.at[target, pl.ds(hidden, hidden)]),
                (down_ref.at[0, :, source], cuts_ref.at[:, target]),
            )
        ):
            copies.append(pltpu.make_async_copy(from_ref, to_ref, sems.at[3 * at + which]))
    for copy in copies:
        copy.start()

    offset = (y * lax.axis_size("c") + core) * hidden
    col = lax.broadcasted_iota(jnp.int32, (1, hidden), 1) + offset
    base = col * jnp.int32(19349663) + seed_ref[0] * jnp.int32(83492791)
    scale = jnp.asarray(1.0 / math.sqrt(2048), BF16).astype(F32)
    count = 16

    def signs(at, first, step):
        row = lax.broadcasted_iota(jnp.int32, (count, 1), 0) + (first * width + step * count)
        mixed = row * jnp.int32(73856093) + base
        mixed = mixed ^ mixed >> 15
        mixed = mixed * jnp.int32(735632791)
        mixed = mixed ^ mixed >> 13
        mixed = mixed * jnp.int32(1274126177)
        mixed = mixed ^ mixed >> 16
        target = pl.ds(pl.multiple_of(at * width + step * count, count), count)
        mats_ref[target, 2 * hidden :] = jnp.where((mixed & 32) != 0, scale, -scale).astype(BF16)

    for at, (other, step) in enumerate(BLOCKS):
        first = block(other, step)
        lax.fori_loop(0, width // count, lambda i, _: signs(at, first, i), None, unroll=4)
    for copy in copies:
        copy.wait()


def stage_weights(seed, w_gate, w_up, w_down):
    model, hidden = w_gate.shape[1:]
    vmem = pl.BlockSpec(memory_space=pltpu.VMEM)
    hbm = pl.BlockSpec(memory_space=pltpu.HBM)
    return pl.pallas_call(
        stage_kernel,
        out_shape=[jax.ShapeDtypeStruct((model, 3 * hidden), BF16), jax.ShapeDtypeStruct((hidden, model), BF16)],
        in_specs=[pl.BlockSpec(memory_space=pltpu.SMEM), hbm, hbm, hbm],
        out_specs=[vmem, vmem],
        scratch_shapes=[pltpu.SemaphoreType.DMA((3 * len(BLOCKS),))],
        compiler_params=pltpu.CompilerParams(vmem_limit_bytes=24 * 1024 * 1024),
        cost_estimate=pl.CostEstimate(flops=0, bytes_accessed=14 * model * hidden, transcendentals=0),
        name="stage_weights",
    )(seed, *[pltpu.with_memory_space_constraint(w, pltpu.HBM) for w in (w_gate, w_up, w_down)])


def dot(a, b, ca, cb):
    return lax.dot_general(a, b, (((ca,), (cb,)), ((), ())), preferred_element_type=F32)


def shift_y(value, shift):
    count = lax.axis_size("y")
    return lax.ppermute(value, "y", [(i, (i + shift) % count) for i in range(count)])


def swap_cores(value):
    return lax.ppermute(value, "c", SWAP)


def exchange(value):
    return lax.all_to_all(value, EXPERT, split_axis=0, concat_axis=0, tiled=True)


def forward_factors(pre, lin, tangent):
    sig = jax.nn.sigmoid(pre)
    rest = 1.0 - sig
    slope = sig * (1.0 + pre * rest)
    bend = sig * rest * (2.0 + pre * (1.0 - 2.0 * sig))
    third = lin * bend * tangent
    return (lin * slope, slope * tangent, third, third * tangent)


def body(tokens, cotangent, expert_route, w_gate, w_up, w_down, sign_seeds):
    expert_count = lax.axis_size(EXPERT)
    ys, cores = lax.axis_size("y"), lax.axis_size("c")
    y, core = lax.axis_index("y"), lax.axis_index("c")
    tok_count, model_width = tokens.shape
    hidden_cols = w_gate.shape[2]
    slot_count = max(2, 2 * tok_count // expert_count)
    rows = expert_count * slot_count
    width = model_width // (ys * cores)
    half = ys * width
    barrier = lax.optimization_barrier

    def to_experts(send):
        return exchange(send.reshape(expert_count, slot_count, -1)).reshape(rows, -1)

    def neighbours(piece):
        return [shift_y(piece, -1), shift_y(piece, 1)]

    def beyond(near):
        cut = rows // 2
        return [shift_y(near[0][:, :cut], -1), shift_y(near[1][:, cut:], 1)]

    def both_cores(pieces, axis):
        own = jnp.concatenate(pieces, axis=axis)
        return own, swap_cores(own)

    dispatch, send = dispatch_rows(expert_route, tokens, cotangent, rows, width)
    send, seed = barrier((send, sign_seeds))
    mats, down = stage_weights(seed, w_gate, w_up, w_down)
    received, mats, down = barrier((to_experts(send), mats, down))
    piece = received.T
    near = neighbours(piece)
    far = beyond(near)
    near.append(piece)
    x_near = both_cores([part[:width] for part in near], 0)
    cot_near = both_cores([part[width:] for part in near], 0)
    split = 2 * width
    sums = dot(mats[split:], jnp.concatenate(x_near, axis=0), 0, 0)
    sums, cot_near, far = barrier((sums, cot_near, far))
    far = both_cores(far, 1)
    cot_sum = dot(down[:, split:], jnp.concatenate(cot_near, axis=0), 1, 0)
    sums, far, cot_sum = barrier((sums, far, cot_sum))
    x_far = jnp.concatenate([part[:width] for part in far], axis=0)
    cot_far = jnp.concatenate([part[width:] for part in far], axis=0)
    spans = [slice(at * hidden_cols, (at + 1) * hidden_cols) for at in range(3)]
    factors = forward_factors(*[sums[span] + dot(mats[:split, span], x_far, 0, 0) for span in spans])
    h = cot_sum + dot(down[:, :split], cot_far, 1, 0)
    curvature = jnp.sum(h * factors[3], axis=1)
    grads = jnp.concatenate([(h * f).astype(BF16) for f in (factors[2], factors[1], factors[0])], axis=0)

    def partial(start, count):
        return dot(mats[start * width : (start + count) * width], grads, 1, 0)

    give_far = partial(1, 1).astype(BF16)
    give_far, grads = barrier((give_far, grads))
    give_near = partial(5, 2).astype(BF16)
    swapped = swap_cores(give_far)
    swapped, give_near, grads = barrier((swapped, give_near, grads))
    sum_far = partial(0, 1) + swapped.astype(F32)
    sum_far, grads = barrier((sum_far, grads))
    sum_near = partial(2, 2) + swap_cores(give_near).astype(F32)
    sum_near, grads = barrier((sum_near, grads))
    total = partial(4, 1) + swap_cores(partial(7, 1).astype(BF16)).astype(F32)
    total = total + shift_y(sum_far.astype(BF16), 2).astype(F32)
    for at, shift in enumerate((1, 3)):
        total = total + shift_y(sum_near[at * width : (at + 1) * width].astype(BF16), shift).astype(F32)
    returned = to_experts(total.astype(BF16).T)
    combined = dot(dispatch, returned, 0, 0).astype(BF16)
    steps = (2, 1, 3, 0)
    own = jnp.stack([shift_y(combined, ys - step) for step in steps[:-1]] + [combined])
    result = jnp.zeros((tok_count, model_width), BF16)
    for blocks, of_core in ((own, core), (swap_cores(own), 1 - core)):
        for at, step in enumerate(steps):
            column = (of_core * ys + lax.rem(y + step, ys)) * width
            result = lax.dynamic_update_slice_in_dim(result, blocks[at], column, 1)
    return (result, curvature[None, :])


def solution(mesh):
    chips = Mesh(mesh.devices.reshape(4, 8, 4, 2), ("x", "z", "y", "c"))
    expert, dp = EXPERT, ("y", "c")
    in_specs = (
        P(expert, None),
        P(expert, None),
        P(expert, None),
        P(expert, None, dp),
        P(expert, None, dp),
        P(expert, dp, None),
        P(expert),
    )
    out_specs = (P(expert, None), P(expert, dp))
    return jax.shard_map(body, mesh=chips, in_specs=in_specs, out_specs=out_specs, check_vma=False)
```

time: 125 us -> 120 us (0.960)
  Pallas kernels: 15.5 us -> 6.49 us
  local copies, waits for them, and re-layouts: 4.1 us -> 9 us
  starting transfers between devices: 38.2 us -> 33.9 us
  other arithmetic: 0.98 us -> 3.24 us
  waiting for transfers between devices: 27.2 us -> 28.8 us
    ppermute x12 -> x10, starting transfers between devices: 17.7 us -> 9.26 us  [shift_y(): lax.ppermute(value, 'y', [(i, (i + shift) % count) for i in range(count)])]
    pallas_call x1, Pallas kernels: 12.7 us -> 4.4 us  [stage_weights(): pl.pallas_call(stage_kernel, out_shape=[jax.ShapeDtypeStruct((model, 3 *...]
    unnamed x19 -> x17, local copies, waits for them, and re-layouts: 2.96 us -> 7.72 us
    ppermute x5 -> x7, starting transfers between devices: 8.64 us -> 12.7 us  [swap_cores(): return lax.ppermute(value, 'c', SWAP)]
    all_to_all x1, waiting for transfers between devices: 0.31 us -> 3.2 us  [exchange(): lax.all_to_all(value, EXPERT, split_axis=0, concat_axis=0, tiled=True)]
    ppermute x5 -> x7, waiting for transfers between devices: 2.61 us -> 0.8 us  [swap_cores(): return lax.ppermute(value, 'c', SWAP)]
    convert_element_type x0 -> x1, other arithmetic: none -> 1.51 us  [body(): (h * f).astype(BF16)]
    all_to_all x1, blocking collectives: 18.2 us -> 17 us  [exchange(): lax.all_to_all(value, EXPERT, split_axis=0, concat_axis=0, tiled=True)]
  transfers between devices with their start and end apart: 18 -> 18, of which waited for: 14 -> 9; matrix products, arithmetic and copies ran while one was open for 11% -> 13% of each run, Pallas kernels for 10% -> 4%
where the time goes in v5:
time: 120 us
  starting transfers between devices  33.9 us (28%)
  waiting for transfers between devices  28.8 us (24%)
  matrix products  19.7 us (16%)
  blocking collectives  17 us (14%)
  local copies, waits for them, and re-layouts  9 us (8%)
  Pallas kernels  6.49 us (5%)
  other arithmetic  3.24 us (3%)
  between operations  1.68 us (1%)
    ppermute x10, waiting for transfers between devices, shift_y(): lax.ppermute(value, 'y', [(i, (i + shift) % count) for i in range(count)])  24.8 us
    dot_general x13, matrix products, dot(): lax.dot_general(a, b, (((ca,), (cb,)), ((), ())), preferred_element_type=...  19.7 us
    all_to_all x1, blocking collectives, exchange(): lax.all_to_all(value, EXPERT, split_axis=0, concat_axis=0, tiled=True)  17 us
    ppermute x7, starting transfers between devices, swap_cores(): return lax.ppermute(value, 'c', SWAP)  12.7 us
    all_to_all x1, starting transfers between devices, exchange(): lax.all_to_all(value, EXPERT, split_axis=0, concat_axis=0, tiled=True)  11.9 us
    ppermute x10, starting transfers between devices, shift_y(): lax.ppermute(value, 'y', [(i, (i + shift) % count) for i in range(count)])  9.26 us
    unnamed x17, local copies, waits for them, and re-layouts  7.72 us
    pallas_call x1, Pallas kernels, stage_weights(): pl.pallas_call(stage_kernel, out_shape=[jax.ShapeDtypeStruct((model, 3 *...  4.4 us
  transfers between devices with their start and end apart: 18, of which 9 were waited for; matrix products, arithmetic and copies ran while one was open for 13% of the time, Pallas kernels for 4%

profile of v5, /device:TPU:1, one launch (start us, length us, event | category | flops | bytes accessed | tf_op | source)
XLA Modules:
  0.0 119.9 jit_solution(4949717057552053684)
XLA Ops:
  0.6 0.7 copy-done.3
  1.3 2.1 %dispatch.1 = (bf16[512,256]{1,0:T(8,128)(2,1)S(1)}, bf16[512,512]{1,0:T(8,128)(2,1)}) custom-call(s32[1,256]{1,0:T(1,128)S(1)} %bitcast.37, bf16[256,2048]{1,0:T(8,128)(2,1)} %tokens_ref.1, bf16[256,2048]{1,0:T(8,128)(2,1)} %cot_ref.1), custom_call_target="tpu_custom_call" | custom-call | tf_op jit(solution)/shard_map/dispatch/pallas_call | solution.py:52
  3.4 11.9 %all-to-all-start = ((bf16[32,16,512]{2,1,0:T(8,128)(2,1)}), bf16[32,16,512]{2,1,0:T(8,128)(2,1)S(1)}, u32[]{:S(2)}, u32[]{:S(2)}) async-start(bf16[32,16,512]{2,1,0:T(8,128)(2,1)} %bitcast.1), calls=%async_computation | async-start | bytes 1048576 | tf_op jit(solution)/shard_map/all_to_all | solution.py:141
  15.9 4.4 %stage_weights.1 = (bf16[2048,2688]{1,0:T(8,128)(2,1)S(1)}, bf16[896,2048]{1,0:T(8,128)(2,1)S(1)}) custom-call(s32[1]{0:T(128)S(6)} %copy.19.seed_ref, bf16[1,2048,896]{2,1,0:T(8,128)(2,1)} %gate_ref.1, bf16[1,2048,896]{2,1,0:T(8,128)(2,1)} %up_ref.1, bf16[1,896,2048]{2,1,0:T(8,128)(2,1)} %down_ref.1), custom_call_target="tpu_custom_call" | custom-call | bytes 25690112 | tf_op jit(solution)/shard_map/stage_weights/pallas_call | solution.py:115
  20.4 4.2 %copy-done = bf16[2048,2688]{1,0:T(8,128)(2,1)} copy-done((bf16[2048,2688]{1,0:T(8,128)(2,1)}, bf16[2048,2688]{1,0:T(8,128)(2,1)S(1)}, u32[]{:S(2)}) %copy-start) | copy-done | bytes 11010072
  24.5 1.9 %copy-done.1 = bf16[896,2048]{1,0:T(8,128)(2,1)} copy-done((bf16[896,2048]{1,0:T(8,128)(2,1)}, bf16[896,2048]{1,0:T(8,128)(2,1)S(1)}, u32[]{:S(2)}) %copy-start.1) | copy-done | bytes 3670040
  26.4 3.2 %all-to-all-done = bf16[32,16,512]{2,1,0:T(8,128)(2,1)S(1)} async-done(((bf16[32,16,512]{2,1,0:T(8,128)(2,1)}), bf16[32,16,512]{2,1,0:T(8,128)(2,1)S(1)}, u32[]{:S(2)}, u32[]{:S(2)}) %all-to-all-start) | async-done | bytes 524320 | tf_op jit(solution)/shard_map/all_to_all | solution.py:141
  29.6 2.7 %collective-permute-start = (bf16[512,512]{0,1:T(8,128)(2,1)S(1)}, bf16[512,512]{0,1:T(8,128)(2,1)S(1)}, u32[]{:S(2)}, u32[]{:S(2)}) collective-permute-start(bf16[512,512]{0,1:T(8,128)(2,1)S(1)} %bitcast.38), channel_id=1, source_target_pairs={{0,6},{2,0},{4,2},{6,4},{1,7},{3,1},{5,3},{7,5},{8,14},{10,8},{12,... | collective-permute-start | bytes 1572872 | tf_op jit(solution)/shard_map/ppermute | solution.py:133
  32.4 7.7 %collective-permute-done = bf16[512,512]{0,1:T(8,128)(2,1)S(1)} collective-permute-done((bf16[512,512]{0,1:T(8,128)(2,1)S(1)}, bf16[512,512]{0,1:T(8,128)(2,1)S(1)}, u32[]{:S(2)}, u32[]{:S(2)}) %collective-permute-start) | collective-permute-done | bytes 524320 | tf_op jit(solution)/shard_map/ppermute | solution.py:133
  40.1 3.1 %collective-permute-done.1 = bf16[512,512]{0,1:T(8,128)(2,1)S(1)} collective-permute-done((bf16[512,512]{0,1:T(8,128)(2,1)S(1)}, bf16[512,512]{0,1:T(8,128)(2,1)S(1)}, u32[]{:S(2)}, u32[]{:S(2)}) %collective-permute-start.1) | collective-permute-done | bytes 524320 | tf_op jit(solution)/shard_map/ppermute | solution.py:133
  43.3 4.8 %collective-permute-start.2 = (bf16[768,512]{0,1:T(8,128)(2,1)S(1)}, bf16[768,512]{0,1:T(8,128)(2,1)S(1)}, u32[]{:S(2)}, u32[]{:S(2)}) collective-permute-start(bf16[768,512]{0,1:T(8,128)(2,1)S(1)} %pad_maximum_fusion.1), channel_id=1, source_target_pairs={{0,1},{1,0},{2,3},{3,2},{4,5},{5,4},{6,7},{7,6},{8,9},{9,8},{10,11... | collective-permute-start | bytes 2359304 | tf_op jit(solution)/shard_map/ppermute | solution.py:137
  48.5 1.5 %collective-permute-start.5 = (bf16[512,256]{0,1:T(8,128)(2,1)S(1)}, bf16[512,256]{0,1:T(8,128)(2,1)S(1)}, u32[]{:S(2)}, u32[]{:S(2)}) collective-permute-start(bf16[512,256]{0,1:T(8,128)(2,1)S(1)} %slice.141), channel_id=1, source_target_pairs={{0,2},{2,4},{4,6},{6,0},{1,3},{3,5},{5,7},{7,1},{8,10},{10,12},{12... | collective-permute-start | bytes 786440 | tf_op jit(solution)/shard_map/ppermute | solution.py:133
  50.0 8.1 %fusion = f32[2688,512]{1,0:T(8,128)S(1)} fusion(bf16[2048,2688]{1,0:T(8,128)(2,1)} %copy-done, bf16[768,512]{0,1:T(8,128)(2,1)S(1)} %collective-permute-done.2, bf16[256,512]{0,1:T(8,128)(2,1)S(1)} %get-tuple-element.72, bf16[256,512]{0,1:T(8,128)(2,1)S(1)} %get-tuple-element.70, bf16[256,512]{0,1:T(8,128)(2,1)S(1)} %get-tuple-element.68), kind=kOutput, calls=%fused_computation | convolution fusion | flops 4234149888 | bytes 15335424 | tf_op jit(solution)/shard_map/dot_general | solution.py:128
  58.2 1.2 %collective-permute-start.6 = (bf16[512,512]{0,1:T(8,128)(2,1)S(1)}, bf16[512,512]{0,1:T(8,128)(2,1)S(1)}, u32[]{:S(2)}, u32[]{:S(2)}) collective-permute-start(bf16[512,512]{0,1:T(8,128)(2,1)S(1)} %constant_dynamic-update-slice_fusion), channel_id=1, source_target_pairs={{0,1},{1,0},{2,3},{3,2},{4,5},{5,4},{6,7},{7,6},{8,9},{9,8},{10,11... | collective-permute-start | bytes 1572872 | tf_op jit(solution)/shard_map/ppermute | solution.py:137
  59.4 1.6 %fusion.4 = f32[896,512]{1,0:T(8,128)S(1)} fusion(bf16[896,2048]{1,0:T(8,128)(2,1)S(1)} %copy-done.2, bf16[768,512]{0,1:T(8,128)(2,1)S(1)} %collective-permute-done.3, bf16[768,512]{0,1:T(8,128)(2,1)S(1)} %pad_maximum_fusion.2), kind=kOutput, calls=%fused_computation.5 | convolution fusion | flops 1412431872 | bytes 6160384 | tf_op jit(solution)/shard_map/dot_general | solution.py:128
  61.0 0.1 fusion.72
  61.2 0.7 slice_add_fusion.1
  61.9 0.7 slice_add_fusion.2
  62.6 0.7 slice_add_fusion
  63.3 0.7 fusion.55
  64.0 1.2 %multiply_reduce_fusion = (f32[896]{0:T(1024)S(1)}, f32[896,512]{1,0:T(8,128)S(1)}) fusion(f32[896,512]{1,0:T(8,128)S(1)} %slice_add_fusion, f32[896,512]{1,0:T(8,128)S(1)} %slice_add_fusion.2, f32[896,512]{1,0:T(8,128)S(1)} %slice_add_fusion.1, f32[896,512]{1,0:T(8,128)S(1)} %fusion.4, f32[896,512]{1,0:T(8,128)S(1)} %fusion.55), kind=kLoop, calls=%fused_computation.16 | loop fusion | flops 7339136 | bytes 11013632 | tf_op jit(solution)/shard_map/reduce_sum | solution.py:200
  65.2 1.5 %multiply_convert_fusion.2 = (bf16[896,512]{1,0:T(8,128)(2,1)S(1)}, bf16[896,512]{1,0:T(8,128)(2,1)S(1)}, bf16[896,512]{1,0:T(8,128)(2,1)S(1)}) fusion(f32[896,512]{1,0:T(8,128)S(1)} %get-tuple-element.57, f32[896,512]{1,0:T(8,128)S(1)} %slice_add_fusion, f32[896,512]{1,0:T(8,128)S(1)} %slice_add_fusion.2, f32[896,512]{1,0:T(8,128)S(1)} %slice_add_fusion.1), kind=kLoop, calls=%fused_computation.19 | loop fusion | flops 10551296 | bytes 10092544 | tf_op jit(solution)/shard_map/convert_element_type | solution.py:201
  66.7 0.2 pad_maximum_fusion
  66.9 0.9 fusion.37
  67.8 0.4 collective-permute-start.7
  68.2 1.6 %fusion.31 = bf16[512,512]{1,0:T(8,128)(2,1)S(1)} fusion(bf16[2688,512]{1,0:T(8,128)(2,1)S(1)} %pad_maximum_fusion, bf16[2048,2688]{1,0:T(8,128)(2,1)S(1)} %bitcast.36), kind=kOutput, calls=%fused_computation.42 | convolution fusion | flops 1409548288 | bytes 6029312 | tf_op jit(solution)/shard_map/dot_general | solution.py:128
  69.9 0.3 collective-permute-start.8
  70.2 0.9 fusion.34
  71.2 1.6 %fusion.6 = f32[512,512]{1,0:T(8,128)S(1)} fusion(bf16[2688,512]{1,0:T(8,128)(2,1)S(1)} %pad_maximum_fusion, bf16[2048,2688]{1,0:T(8,128)(2,1)S(1)} %bitcast.36), kind=kOutput, calls=%fused_computation.7 | convolution fusion | flops 1409286144 | bytes 6553600 | tf_op jit(solution)/shard_map/dot_general | solution.py:128
  72.9 0.2 convert_add_fusion
  73.0 0.9 fusion.40
  73.9 0.5 collective-permute-start.9
  74.5 2.3 %collective-permute-start.11 = (bf16[256,512]{1,0:T(8,128)(2,1)S(1)}, bf16[256,512]{1,0:T(8,128)(2,1)S(1)}, u32[]{:S(2)}, u32[]{:S(2)}) collective-permute-start(bf16[256,512]{1,0:T(8,128)(2,1)S(1)} %get-tuple-element.61), channel_id=1, source_target_pairs={{0,2},{2,4},{4,6},{6,0},{1,3},{3,5},{5,7},{7,1},{8,10},{10,12},{12... | collective-permute-start | bytes 786440 | tf_op jit(solution)/shard_map/ppermute | solution.py:133
  76.8 0.7 collective-permute-start.12
  77.5 2.8 %collective-permute-done.10 = bf16[256,512]{1,0:T(8,128)(2,1)S(1)} collective-permute-done((bf16[256,512]{1,0:T(8,128)(2,1)S(1)}, bf16[256,512]{1,0:T(8,128)(2,1)S(1)}, u32[]{:S(2)}, u32[]{:S(2)}) %collective-permute-start.10) | collective-permute-done | bytes 262176 | tf_op jit(solution)/shard_map/ppermute | solution.py:133
  80.3 6.3 %collective-permute-done.11 = bf16[256,512]{1,0:T(8,128)(2,1)S(1)} collective-permute-done((bf16[256,512]{1,0:T(8,128)(2,1)S(1)}, bf16[256,512]{1,0:T(8,128)(2,1)S(1)}, u32[]{:S(2)}, u32[]{:S(2)}) %collective-permute-start.11) | collective-permute-done | bytes 262176 | tf_op jit(solution)/shard_map/ppermute | solution.py:133
  86.6 1.0 fusion.60
  87.6 0.1 copy.9
  87.7 17.0 %all_to_all.10 = bf16[32,16,256]{2,1,0:T(8,128)(2,1)S(1)} all-to-all(bf16[32,16,256]{2,1,0:T(8,128)(2,1)S(1)} %bitcast.43), channel_id=1, replica_groups=mesh['x'=4,'z'=8,'y'=4,'c'=2] {'x','z'}, dimensions={0} | all-to-all | bytes 524288 | tf_op jit(solution)/shard_map/all_to_all | solution.py:141
  104.7 0.3 convolution_convert_fusion
  105.1 1.6 %collective-permute-start.14 = (bf16[256,256]{1,0:T(8,128)(2,1)S(1)}, bf16[256,256]{1,0:T(8,128)(2,1)S(1)}, u32[]{:S(2)}, u32[]{:S(2)}) collective-permute-start(bf16[256,256]{1,0:T(8,128)(2,1)S(1)} %convolution_convert_fusion), channel_id=1, source_target_pairs={{0,6},{2,0},{4,2},{6,4},{1,7},{3,1},{5,3},{7,5},{8,14},{10,8},{12,... | collective-permute-start | bytes 393224 | tf_op jit(solution)/shard_map/ppermute | solution.py:133
  106.8 3.6 %collective-permute-done.13 = bf16[256,256]{1,0:T(8,128)(2,1)S(1)} collective-permute-done((bf16[256,256]{1,0:T(8,128)(2,1)S(1)}, bf16[256,256]{1,0:T(8,128)(2,1)S(1)}, u32[]{:S(2)}, u32[]{:S(2)}) %collective-permute-start.13) | collective-permute-done | bytes 131104 | tf_op jit(solution)/shard_map/ppermute | solution.py:133
  110.4 0.2 collective-permute-done.14
  110.6 1.2 %collective-permute-done.15 = bf16[256,256]{1,0:T(8,128)(2,1)S(1)} collective-permute-done((bf16[256,256]{1,0:T(8,128)(2,1)S(1)}, bf16[256,256]{1,0:T(8,128)(2,1)S(1)}, u32[]{:S(2)}, u32[]{:S(2)}) %collective-permute-start.15) | collective-permute-done | bytes 131104 | tf_op jit(solution)/shard_map/ppermute | solution.py:133
  111.9 5.4 %collective-permute-start.16 = (bf16[4,256,256]{2,1,0:T(8,128)(2,1)S(1)}, bf16[4,256,256]{2,1,0:T(8,128)(2,1)S(1)}, u32[]{:S(2)}, u32[]{:S(2)}) collective-permute-start(bf16[4,256,256]{2,1,0:T(8,128)(2,1)S(1)} %pad_maximum_fusion.4), channel_id=1, source_target_pairs={{0,1},{1,0},{2,3},{3,2},{4,5},{5,4},{6,7},{7,6},{8,9},{9,8},{10,11... | collective-permute-start | bytes 1572872 | tf_op jit(solution)/shard_map/ppermute | solution.py:137
  117.3 0.6 broadcast_in_dim.7
  118.0 0.7 collective-permute-done.16
  118.9 1.0 copy-done.4
  (48 shorter events, 1.3 us)
Async XLA Ops:
  0.6 0.7 copy-start.3
  3.4 26.2 %all-to-all-start = ((bf16[32,16,512]{2,1,0:T(8,128)(2,1)}), bf16[32,16,512]{2,1,0:T(8,128)(2,1)S(1)}, u32[]{:S(2)}, u32[]{:S(2)}) async-start(bf16[32,16,512]{2,1,0:T(8,128)(2,1)} %bitcast.1), calls=%async_computation | async-start | bytes 1048576 | tf_op jit(solution)/shard_map/all_to_all | solution.py:141
  20.3 4.2 %copy-start = (bf16[2048,2688]{1,0:T(8,128)(2,1)}, bf16[2048,2688]{1,0:T(8,128)(2,1)S(1)}, u32[]{:S(2)}) copy-start(bf16[2048,2688]{1,0:T(8,128)(2,1)S(1)} %get-tuple-element.35) | copy-start | bytes 33030148
  24.5 1.9 %copy-start.1 = (bf16[896,2048]{1,0:T(8,128)(2,1)}, bf16[896,2048]{1,0:T(8,128)(2,1)S(1)}, u32[]{:S(2)}) copy-start(bf16[896,2048]{1,0:T(8,128)(2,1)S(1)} %get-tuple-element.40) | copy-start | bytes 11010052
  29.6 10.4 %collective-permute-start = (bf16[512,512]{0,1:T(8,128)(2,1)S(1)}, bf16[512,512]{0,1:T(8,128)(2,1)S(1)}, u32[]{:S(2)}, u32[]{:S(2)}) collective-permute-start(bf16[512,512]{0,1:T(8,128)(2,1)S(1)} %bitcast.38), channel_id=1, source_target_pairs={{0,6},{2,0},{4,2},{6,4},{1,7},{3,1},{5,3},{7,5},{8,14},{10,8},{12,... | collective-permute-start | bytes 1572872 | tf_op jit(solution)/shard_map/ppermute | solution.py:133
  32.3 10.8 %collective-permute-start.1 = (bf16[512,512]{0,1:T(8,128)(2,1)S(1)}, bf16[512,512]{0,1:T(8,128)(2,1)S(1)}, u32[]{:S(2)}, u32[]{:S(2)}) collective-permute-start(bf16[512,512]{0,1:T(8,128)(2,1)S(1)} %bitcast.39), channel_id=1, source_target_pairs={{0,2},{2,4},{4,6},{6,0},{1,3},{3,5},{5,7},{7,1},{8,10},{10,12},{12... | collective-permute-start | bytes 1572872 | tf_op jit(solution)/shard_map/ppermute | solution.py:133
  43.3 6.7 %collective-permute-start.2 = (bf16[768,512]{0,1:T(8,128)(2,1)S(1)}, bf16[768,512]{0,1:T(8,128)(2,1)S(1)}, u32[]{:S(2)}, u32[]{:S(2)}) collective-permute-start(bf16[768,512]{0,1:T(8,128)(2,1)S(1)} %pad_maximum_fusion.1), channel_id=1, source_target_pairs={{0,1},{1,0},{2,3},{3,2},{4,5},{5,4},{6,7},{7,6},{8,9},{9,8},{10,11... | collective-permute-start | bytes 2359304 | tf_op jit(solution)/shard_map/ppermute | solution.py:137
  48.1 10.0 %collective-permute-start.3 = (bf16[768,512]{0,1:T(8,128)(2,1)S(1)}, bf16[768,512]{0,1:T(8,128)(2,1)S(1)}, u32[]{:S(2)}, u32[]{:S(2)}) collective-permute-start(bf16[768,512]{0,1:T(8,128)(2,1)S(1)} %pad_maximum_fusion.2), channel_id=1, source_target_pairs={{0,1},{1,0},{2,3},{3,2},{4,5},{5,4},{6,7},{7,6},{8,9},{9,8},{10,11... | collective-permute-start | bytes 2359304 | tf_op jit(solution)/shard_map/ppermute | solution.py:137
  48.2 12.9 %slice-start = ((s8[11010048]{0:T(1024)(128)(4,1)}), s8[4194304]{0:T(1024)(128)(4,1)S(1)}, s32[]{:S(2)}) async-start(s8[11010048]{0:T(1024)(128)(4,1)} %bitcast.35), calls=%async_computation.2 | async-start | bytes 8388608
  48.3 9.8 %collective-permute-start.4 = (bf16[512,256]{0,1:T(8,128)(2,1)S(1)}, bf16[512,256]{0,1:T(8,128)(2,1)S(1)}, u32[]{:S(2)}, u32[]{:S(2)}) collective-permute-start(bf16[512,256]{0,1:T(8,128)(2,1)S(1)} %slice.140), channel_id=1, source_target_pairs={{0,6},{2,0},{4,2},{6,4},{1,7},{3,1},{5,3},{7,5},{8,14},{10,8},{12,... | collective-permute-start | bytes 786440 | tf_op jit(solution)/shard_map/ppermute | solution.py:133
  48.4 11.0 %copy-start.2 = (bf16[896,2048]{1,0:T(8,128)(2,1)S(1)}, bf16[896,2048]{1,0:T(8,128)(2,1)}, u32[]{:S(2)}) copy-start(bf16[896,2048]{1,0:T(8,128)(2,1)} %copy-done.1) | copy-start | bytes 11010052
  48.4 12.8 %slice-start.1 = ((s8[11010048]{0:T(1024)(128)(4,1)}), s8[4194304]{0:T(1024)(128)(4,1)S(1)}, s32[]{:S(2)}) async-start(s8[11010048]{0:T(1024)(128)(4,1)} %bitcast.35), calls=%async_computation.3 | async-start | bytes 8388608
  48.4 12.8 %slice-start.2 = ((s8[11010048]{0:T(1024)(128)(4,1)}), s8[2621440]{0:T(1024)(128)(4,1)S(1)}, s32[]{:S(2)}) async-start(s8[11010048]{0:T(1024)(128)(4,1)} %bitcast.35), calls=%async_computation.4 | async-start | bytes 5242880
  48.5 9.6 %collective-permute-start.5 = (bf16[512,256]{0,1:T(8,128)(2,1)S(1)}, bf16[512,256]{0,1:T(8,128)(2,1)S(1)}, u32[]{:S(2)}, u32[]{:S(2)}) collective-permute-start(bf16[512,256]{0,1:T(8,128)(2,1)S(1)} %slice.141), channel_id=1, source_target_pairs={{0,2},{2,4},{4,6},{6,0},{1,3},{3,5},{5,7},{7,1},{8,10},{10,12},{12... | collective-permute-start | bytes 786440 | tf_op jit(solution)/shard_map/ppermute | solution.py:133
  58.2 2.9 %collective-permute-start.6 = (bf16[512,512]{0,1:T(8,128)(2,1)S(1)}, bf16[512,512]{0,1:T(8,128)(2,1)S(1)}, u32[]{:S(2)}, u32[]{:S(2)}) collective-permute-start(bf16[512,512]{0,1:T(8,128)(2,1)S(1)} %constant_dynamic-update-slice_fusion), channel_id=1, source_target_pairs={{0,1},{1,0},{2,3},{3,2},{4,5},{5,4},{6,7},{7,6},{8,9},{9,8},{10,11... | collective-permute-start | bytes 1572872 | tf_op jit(solution)/shard_map/ppermute | solution.py:137
  67.8 2.0 %collective-permute-start.7 = (bf16[256,512]{1,0:T(8,128)(2,1)S(1)}, bf16[256,512]{1,0:T(8,128)(2,1)S(1)}, u32[]{:S(2)}, u32[]{:S(2)}) collective-permute-start(bf16[256,512]{1,0:T(8,128)(2,1)S(1)} %fusion.37), channel_id=1, source_target_pairs={{0,1},{1,0},{2,3},{3,2},{4,5},{5,4},{6,7},{7,6},{8,9},{9,8},{10,11... | collective-permute-start | bytes 786440 | tf_op jit(solution)/shard_map/ppermute | solution.py:137
  69.9 3.0 %collective-permute-start.8 = (bf16[512,512]{1,0:T(8,128)(2,1)S(1)}, bf16[512,512]{1,0:T(8,128)(2,1)S(1)}, u32[]{:S(2)}, u32[]{:S(2)}) collective-permute-start(bf16[512,512]{1,0:T(8,128)(2,1)S(1)} %fusion.31), channel_id=1, source_target_pairs={{0,1},{1,0},{2,3},{3,2},{4,5},{5,4},{6,7},{7,6},{8,9},{9,8},{10,11... | collective-permute-start | bytes 1572872 | tf_op jit(solution)/shard_map/ppermute | solution.py:137
  71.1 9.2 %collective-permute-start.10 = (bf16[256,512]{1,0:T(8,128)(2,1)S(1)}, bf16[256,512]{1,0:T(8,128)(2,1)S(1)}, u32[]{:S(2)}, u32[]{:S(2)}) collective-permute-start(bf16[256,512]{1,0:T(8,128)(2,1)S(1)} %fusion.34), channel_id=1, source_target_pairs={{0,4},{2,6},{4,0},{6,2},{1,5},{3,7},{5,1},{7,3},{8,12},{10,14},{12... | collective-permute-start | bytes 786440 | tf_op jit(solution)/shard_map/ppermute | solution.py:133
  73.9 6.4 %collective-permute-start.9 = (bf16[256,512]{1,0:T(8,128)(2,1)S(1)}, bf16[256,512]{1,0:T(8,128)(2,1)S(1)}, u32[]{:S(2)}, u32[]{:S(2)}) collective-permute-start(bf16[256,512]{1,0:T(8,128)(2,1)S(1)} %fusion.40), channel_id=1, source_target_pairs={{0,1},{1,0},{2,3},{3,2},{4,5},{5,4},{6,7},{7,6},{8,9},{9,8},{10,11... | collective-permute-start | bytes 786440 | tf_op jit(solution)/shard_map/ppermute | solution.py:137
  74.5 12.1 %collective-permute-start.11 = (bf16[256,512]{1,0:T(8,128)(2,1)S(1)}, bf16[256,512]{1,0:T(8,128)(2,1)S(1)}, u32[]{:S(2)}, u32[]{:S(2)}) collective-permute-start(bf16[256,512]{1,0:T(8,128)(2,1)S(1)} %get-tuple-element.61), channel_id=1, source_target_pairs={{0,2},{2,4},{4,6},{6,0},{1,3},{3,5},{5,7},{7,1},{8,10},{10,12},{12... | collective-permute-start | bytes 786440 | tf_op jit(solution)/shard_map/ppermute | solution.py:133
  76.8 9.8 %collective-permute-start.12 = (bf16[256,512]{1,0:T(8,128)(2,1)S(1)}, bf16[256,512]{1,0:T(8,128)(2,1)S(1)}, u32[]{:S(2)}, u32[]{:S(2)}) collective-permute-start(bf16[256,512]{1,0:T(8,128)(2,1)S(1)} %get-tuple-element.62), channel_id=1, source_target_pairs={{0,6},{2,0},{4,2},{6,4},{1,7},{3,1},{5,3},{7,5},{8,14},{10,8},{12,... | collective-permute-start | bytes 786440 | tf_op jit(solution)/shard_map/ppermute | solution.py:133
  105.0 5.4 %collective-permute-start.13 = (bf16[256,256]{1,0:T(8,128)(2,1)S(1)}, bf16[256,256]{1,0:T(8,128)(2,1)S(1)}, u32[]{:S(2)}, u32[]{:S(2)}) collective-permute-start(bf16[256,256]{1,0:T(8,128)(2,1)S(1)} %convolution_convert_fusion), channel_id=1, source_target_pairs={{0,4},{2,6},{4,0},{6,2},{1,5},{3,7},{5,1},{7,3},{8,12},{10,14},{12... | collective-permute-start | bytes 393224 | tf_op jit(solution)/shard_map/ppermute | solution.py:133
  105.1 5.5 %collective-permute-start.14 = (bf16[256,256]{1,0:T(8,128)(2,1)S(1)}, bf16[256,256]{1,0:T(8,128)(2,1)S(1)}, u32[]{:S(2)}, u32[]{:S(2)}) collective-permute-start(bf16[256,256]{1,0:T(8,128)(2,1)S(1)} %convolution_convert_fusion), channel_id=1, source_target_pairs={{0,6},{2,0},{4,2},{6,4},{1,7},{3,1},{5,3},{7,5},{8,14},{10,8},{12,... | collective-permute-start | bytes 393224 | tf_op jit(solution)/shard_map/ppermute | solution.py:133
  106.7 5.1 %collective-permute-start.15 = (bf16[256,256]{1,0:T(8,128)(2,1)S(1)}, bf16[256,256]{1,0:T(8,128)(2,1)S(1)}, u32[]{:S(2)}, u32[]{:S(2)}) collective-permute-start(bf16[256,256]{1,0:T(8,128)(2,1)S(1)} %convolution_convert_fusion), channel_id=1, source_target_pairs={{0,2},{2,4},{4,6},{6,0},{1,3},{3,5},{5,7},{7,1},{8,10},{10,12},{12... | collective-permute-start | bytes 393224 | tf_op jit(solution)/shard_map/ppermute | solution.py:133
  111.9 6.9 %collective-permute-start.16 = (bf16[4,256,256]{2,1,0:T(8,128)(2,1)S(1)}, bf16[4,256,256]{2,1,0:T(8,128)(2,1)S(1)}, u32[]{:S(2)}, u32[]{:S(2)}) collective-permute-start(bf16[4,256,256]{2,1,0:T(8,128)(2,1)S(1)} %pad_maximum_fusion.4), channel_id=1, source_target_pairs={{0,1},{1,0},{2,3},{3,2},{4,5},{5,4},{6,7},{7,6},{8,9},{9,8},{10,11... | collective-permute-start | bytes 1572872 | tf_op jit(solution)/shard_map/ppermute | solution.py:137
  118.9 1.0 copy-start.4

commit v6 on v5

--- a/solution.py
+++ b/solution.py
@@ -18,8 +18,8 @@
 BLOCKS = ((0, 2), (1, 2), (0, 1), (0, 3), (0, 0), (1, 1), (1, 3), (1, 0))
 
 
-def dispatch_kernel(route_ref, tokens_ref, cot_ref, dispatch_ref, send_ref, pieces, sems):
-    count = route_ref.shape[1]
+def dispatch_kernel(route_hbm, tokens_ref, cot_ref, dispatch_ref, send_ref, route_ref, pieces, sems):
+    count = route_hbm.shape[1]
     slots, width = dispatch_ref.shape[0], send_ref.shape[1] // 2
     slot_count = slots // lax.axis_size(EXPERT)
     start = (lax.axis_index("c") * lax.axis_size("y") + lax.axis_index("y")) * width
@@ -28,8 +28,10 @@
         pltpu.make_async_copy(ref.at[:, columns], pieces.at[:, pl.ds(at * width, width)], sems.at[at])
         for at, ref in enumerate((tokens_ref, cot_ref))
     ]
-    for copy in copies:
+    copies.append(pltpu.make_async_copy(route_hbm, route_ref, sems.at[2]))
+    for copy in reversed(copies):
         copy.start()
+    copies.pop().wait()
     across = jnp.broadcast_to(route_ref[...], (count, count))
     down = across.T
     earlier = (down == across) & (
@@ -52,12 +54,16 @@
     return pl.pallas_call(
         dispatch_kernel,
         out_shape=[jax.ShapeDtypeStruct((slots, count), BF16), jax.ShapeDtypeStruct((slots, 2 * width), BF16)],
-        in_specs=[vmem, hbm, hbm],
+        in_specs=[hbm, hbm, hbm],
         out_specs=[vmem, vmem],
-        scratch_shapes=[pltpu.VMEM((count, 2 * width), BF16), pltpu.SemaphoreType.DMA((2,))],
+        scratch_shapes=[
+            pltpu.VMEM((1, count), jnp.int32),
+            pltpu.VMEM((count, 2 * width), BF16),
+            pltpu.SemaphoreType.DMA((3,)),
+        ],
         compiler_params=pltpu.CompilerParams(vmem_limit_bytes=24 * 1024 * 1024),
         name="dispatch",
-    )(route.reshape(1, count), *[pltpu.with_memory_space_constraint(a, pltpu.HBM) for a in (tokens, cotangent)])
+    )(*[pltpu.with_memory_space_constraint(a, pltpu.HBM) for a in (route.reshape(1, count), tokens, cotangent)])
 
 
 def stage_kernel(seed_ref, gate_ref, up_ref, down_ref, mats_ref, cuts_ref, sems):
@@ -177,25 +183,29 @@
         return own, swap_cores(own)
 
     dispatch, send = dispatch_rows(expert_route, tokens, cotangent, rows, width)
-    send, seed = barrier((send, sign_seeds))
+    received, seed = barrier((to_experts(send), sign_seeds))
     mats, down = stage_weights(seed, w_gate, w_up, w_down)
-    received, mats, down = barrier((to_experts(send), mats, down))
     piece = received.T
     near = neighbours(piece)
-    far = beyond(near)
-    near.append(piece)
-    x_near = both_cores([part[:width] for part in near], 0)
-    cot_near = both_cores([part[width:] for part in near], 0)
+    crossed = swap_cores(piece)
+    near, mats, down, crossed = barrier((near, mats, down, crossed))
+    x_far = beyond([part[:width] for part in near])
+    cot_far = beyond([part[width:] for part in near])
+    joint = jnp.concatenate(near, axis=0)
+    other = swap_cores(joint)
+    near = near + [piece, other[: 2 * width], other[2 * width :], crossed]
+    x_near = [part[:width] for part in near]
+    cot_near = [part[width:] for part in near]
     split = 2 * width
     sums = dot(mats[split:], jnp.concatenate(x_near, axis=0), 0, 0)
-    sums, cot_near, far = barrier((sums, cot_near, far))
-    far = both_cores(far, 1)
+    sums, cot_near, x_far = barrier((sums, cot_near, x_far))
+    x_far = jnp.concatenate(both_cores(x_far, 1), axis=0)
     cot_sum = dot(down[:, split:], jnp.concatenate(cot_near, axis=0), 1, 0)
-    sums, far, cot_sum = barrier((sums, far, cot_sum))
-    x_far = jnp.concatenate([part[:width] for part in far], axis=0)
-    cot_far = jnp.concatenate([part[width:] for part in far], axis=0)
+    sums, x_far, cot_sum, cot_far = barrier((sums, x_far, cot_sum, cot_far))
+    cot_far = jnp.concatenate(both_cores(cot_far, 1), axis=0)
     spans = [slice(at * hidden_cols, (at + 1) * hidden_cols) for at in range(3)]
     factors = forward_factors(*[sums[span] + dot(mats[:split, span], x_far, 0, 0) for span in spans])
+    factors, cot_far = barrier((factors, cot_far))
     h = cot_sum + dot(down[:, :split], cot_far, 1, 0)
     curvature = jnp.sum(h * factors[3], axis=1)
     grads = jnp.concatenate([(h * f).astype(BF16) for f in (factors[2], factors[1], factors[0])], axis=0)
@@ -205,17 +215,15 @@
 
     give_far = partial(1, 1).astype(BF16)
     give_far, grads = barrier((give_far, grads))
-    give_near = partial(5, 2).astype(BF16)
+    give_rest = partial(5, 3).astype(BF16)
     swapped = swap_cores(give_far)
-    swapped, give_near, grads = barrier((swapped, give_near, grads))
+    swapped, give_rest, grads = barrier((swapped, give_rest, grads))
     sum_far = partial(0, 1) + swapped.astype(F32)
     sum_far, grads = barrier((sum_far, grads))
-    sum_near = partial(2, 2) + swap_cores(give_near).astype(F32)
-    sum_near, grads = barrier((sum_near, grads))
-    total = partial(4, 1) + swap_cores(partial(7, 1).astype(BF16)).astype(F32)
-    total = total + shift_y(sum_far.astype(BF16), 2).astype(F32)
+    sum_rest = partial(2, 3) + swap_cores(give_rest).astype(F32)
+    total = sum_rest[2 * width :] + shift_y(sum_far.astype(BF16), 2).astype(F32)
     for at, shift in enumerate((1, 3)):
-        total = total + shift_y(sum_near[at * width : (at + 1) * width].astype(BF16), shift).astype(F32)
+        total = total + shift_y(sum_rest[at * width : (at + 1) * width].astype(BF16), shift).astype(F32)
     returned = to_experts(total.astype(BF16).T)
     combined = dot(dispatch, returned, 0, 0).astype(BF16)
     steps = (2, 1, 3, 0)

time: 120 us -> 117 us (0.975)
  blocking collectives: 17 us -> 43 us
  waiting for transfers between devices: 28.8 us -> 16.8 us
  local copies, waits for them, and re-layouts: 9 us -> 2.38 us
  starting transfers between devices: 33.9 us -> 28.5 us
  matrix products: 19.7 us -> 16.8 us
    all_to_all x1 -> x2, blocking collectives: 17 us -> 43 us  [exchange(): lax.all_to_all(value, EXPERT, split_axis=0, concat_axis=0, tiled=True)]
    all_to_all x1 -> x0, starting transfers between devices: 11.9 us -> none  [exchange(): lax.all_to_all(value, EXPERT, split_axis=0, concat_axis=0, tiled=True)]
    ppermute x10 -> x12, waiting for transfers between devices: 24.8 us -> 15.5 us  [shift_y(): lax.ppermute(value, 'y', [(i, (i + shift) % count) for i in range(count)])]
    unnamed x17 -> x10, local copies, waits for them, and re-layouts: 7.72 us -> 1.12 us
    ppermute x7, starting transfers between devices: 12.7 us -> 16.2 us  [swap_cores(): return lax.ppermute(value, 'c', SWAP)]
    all_to_all x1 -> x0, waiting for transfers between devices: 3.2 us -> none  [exchange(): lax.all_to_all(value, EXPERT, split_axis=0, concat_axis=0, tiled=True)]
    ppermute x10 -> x12, starting transfers between devices: 9.26 us -> 12.4 us  [shift_y(): lax.ppermute(value, 'y', [(i, (i + shift) % count) for i in range(count)])]
    dot_general x13 -> x11, matrix products: 19.7 us -> 16.8 us  [dot(): lax.dot_general(a, b, (((ca,), (cb,)), ((), ())), preferred_element_type=...]
  transfers between devices with their start and end apart: 18 -> 19, of which waited for: 9 -> 8; matrix products, arithmetic and copies ran while one was open for 13% -> 13% of each run, Pallas kernels for 4% -> 4%
where the time goes in v6:
time: 117 us
  blocking collectives  43 us (37%)
  starting transfers between devices  28.5 us (24%)
  waiting for transfers between devices  16.8 us (14%)
  matrix products  16.8 us (14%)
  Pallas kernels  5.71 us (5%)
  local copies, waits for them, and re-layouts  2.38 us (2%)
  other arithmetic  2.2 us (2%)
  between operations  1.72 us (1%)
    all_to_all x2, blocking collectives, exchange(): lax.all_to_all(value, EXPERT, split_axis=0, concat_axis=0, tiled=True)  43 us
    dot_general x11, matrix products, dot(): lax.dot_general(a, b, (((ca,), (cb,)), ((), ())), preferred_element_type=...  16.8 us
    ppermute x7, starting transfers between devices, swap_cores(): return lax.ppermute(value, 'c', SWAP)  16.2 us
    ppermute x12, waiting for transfers between devices, shift_y(): lax.ppermute(value, 'y', [(i, (i + shift) % count) for i in range(count)])  15.5 us
    ppermute x12, starting transfers between devices, shift_y(): lax.ppermute(value, 'y', [(i, (i + shift) % count) for i in range(count)])  12.4 us
    pallas_call x1, Pallas kernels, stage_weights(): pl.pallas_call(stage_kernel, out_shape=[jax.ShapeDtypeStruct((model, 3 *...  4.4 us
  transfers between devices with their start and end apart: 19, of which 8 were waited for; matrix products, arithmetic and copies ran while one was open for 13% of the time, Pallas kernels for 4%

profile of v6, /device:TPU:1, one launch (start us, length us, event | category | flops | bytes accessed | tf_op | source)
XLA Modules:
  0.0 117.1 jit_solution(6257379585152811266)
XLA Ops:
  0.6 1.3 %dispatch.1 = (bf16[512,256]{1,0:T(8,128)(2,1)S(1)}, bf16[512,512]{1,0:T(8,128)(2,1)S(1)}) custom-call(s32[1,256]{1,0:T(1,128)} %bitcast.50, bf16[256,2048]{1,0:T(8,128)(2,1)} %tokens_ref.1, bf16[256,2048]{1,0:T(8,128)(2,1)} %cot_ref.1), custom_call_target="tpu_custom_call" | custom-call | tf_op jit(solution)/shard_map/dispatch/pallas_call | solution.py:54
  2.0 26.0 %all_to_all.10 = bf16[32,16,512]{2,1,0:T(8,128)(2,1)S(1)} all-to-all(bf16[32,16,512]{2,1,0:T(8,128)(2,1)S(1)} %bitcast.39), channel_id=1, replica_groups=mesh['x'=4,'z'=8,'y'=4,'c'=2] {'x','z'}, dimensions={0} | all-to-all | bytes 1048576 | tf_op jit(solution)/shard_map/all_to_all | solution.py:147
  27.9 2.7 %collective-permute-start = (bf16[512,512]{0,1:T(8,128)(2,1)S(1)}, bf16[512,512]{0,1:T(8,128)(2,1)S(1)}, u32[]{:S(2)}, u32[]{:S(2)}) collective-permute-start(bf16[512,512]{0,1:T(8,128)(2,1)S(1)} %bitcast.40), channel_id=1, source_target_pairs={{0,6},{2,0},{4,2},{6,4},{1,7},{3,1},{5,3},{7,5},{8,14},{10,8},{12,... | collective-permute-start | bytes 1572872 | tf_op jit(solution)/shard_map/ppermute | solution.py:139
  30.7 3.8 %collective-permute-start.2 = (bf16[512,512]{0,1:T(8,128)(2,1)S(1)}, bf16[512,512]{0,1:T(8,128)(2,1)S(1)}, u32[]{:S(2)}, u32[]{:S(2)}) collective-permute-start(bf16[512,512]{0,1:T(8,128)(2,1)S(1)} %bitcast.42), channel_id=1, source_target_pairs={{0,1},{1,0},{2,3},{3,2},{4,5},{5,4},{6,7},{7,6},{8,9},{9,8},{10,11... | collective-permute-start | bytes 1572872 | tf_op jit(solution)/shard_map/ppermute | solution.py:143
  35.1 4.4 %stage_weights.1 = (bf16[2048,2688]{1,0:T(8,128)(2,1)S(1)}, bf16[896,2048]{1,0:T(8,128)(2,1)S(1)}) custom-call(s32[1]{0:T(128)S(6)} %copy.33.seed_ref, bf16[1,2048,896]{2,1,0:T(8,128)(2,1)} %gate_ref.1, bf16[1,2048,896]{2,1,0:T(8,128)(2,1)} %up_ref.1, bf16[1,896,2048]{2,1,0:T(8,128)(2,1)} %down_ref.1), custom_call_target="tpu_custom_call" | custom-call | bytes 25690112 | tf_op jit(solution)/shard_map/stage_weights/pallas_call | solution.py:121
  39.5 2.0 %collective-permute-done.1 = bf16[512,512]{0,1:T(8,128)(2,1)S(1)} collective-permute-done((bf16[512,512]{0,1:T(8,128)(2,1)S(1)}, bf16[512,512]{0,1:T(8,128)(2,1)S(1)}, u32[]{:S(2)}, u32[]{:S(2)}) %collective-permute-start.1) | collective-permute-done | bytes 524320 | tf_op jit(solution)/shard_map/ppermute | solution.py:139
  41.5 0.1 pad_maximum_fusion.1
  41.6 4.8 %collective-permute-start.3 = (bf16[1024,512]{0,1:T(8,128)(2,1)S(1)}, bf16[1024,512]{0,1:T(8,128)(2,1)S(1)}, u32[]{:S(2)}, u32[]{:S(2)}) collective-permute-start(bf16[1024,512]{0,1:T(8,128)(2,1)S(1)} %pad_maximum_fusion.1), channel_id=1, source_target_pairs={{0,1},{1,0},{2,3},{3,2},{4,5},{5,4},{6,7},{7,6},{8,9},{9,8},{10,11... | collective-permute-start | bytes 3145736 | tf_op jit(solution)/shard_map/ppermute | solution.py:143
  46.6 1.5 %collective-permute-start.5 = (bf16[256,256]{0,1:T(8,128)(2,1)S(1)}, bf16[256,256]{0,1:T(8,128)(2,1)S(1)}, u32[]{:S(2)}, u32[]{:S(2)}) collective-permute-start(bf16[256,256]{0,1:T(8,128)(2,1)S(1)} %get-tuple-element.91), channel_id=1, source_target_pairs={{0,2},{2,4},{4,6},{6,0},{1,3},{3,5},{5,7},{7,1},{8,10},{10,12},{12... | collective-permute-start | bytes 393224 | tf_op jit(solution)/shard_map/ppermute | solution.py:139
  48.1 1.2 %collective-permute-start.7 = (bf16[256,256]{0,1:T(8,128)(2,1)S(1)}, bf16[256,256]{0,1:T(8,128)(2,1)S(1)}, u32[]{:S(2)}, u32[]{:S(2)}) collective-permute-start(bf16[256,256]{0,1:T(8,128)(2,1)S(1)} %get-tuple-element.92), channel_id=1, source_target_pairs={{0,6},{2,0},{4,2},{6,4},{1,7},{3,1},{5,3},{7,5},{8,14},{10,8},{12,... | collective-permute-start | bytes 393224 | tf_op jit(solution)/shard_map/ppermute | solution.py:139
  49.3 0.2 collective-permute-start.8
  49.9 4.5 %fusion = f32[2688,512]{1,0:T(8,128)S(1)} fusion(bf16[1536,512]{0,1:T(8,128)(2,1)S(1)} %get-tuple-element.95, bf16[2048,2688]{1,0:T(8,128)(2,1)S(1)} %get-tuple-element.45), kind=kOutput, calls=%fused_computation | convolution fusion | flops 4227858432 | bytes 15335424 | tf_op jit(solution)/shard_map/dot_general | solution.py:134
  54.5 1.2 %collective-permute-start.6 = (bf16[256,512]{0,1:T(8,128)(2,1)S(1)}, bf16[256,512]{0,1:T(8,128)(2,1)S(1)}, u32[]{:S(2)}, u32[]{:S(2)}) collective-permute-start(bf16[256,512]{0,1:T(8,128)(2,1)S(1)} %constant_dynamic-update-slice_fusion), channel_id=1, source_target_pairs={{0,1},{1,0},{2,3},{3,2},{4,5},{5,4},{6,7},{7,6},{8,9},{9,8},{10,11... | collective-permute-start | bytes 786440 | tf_op jit(solution)/shard_map/ppermute | solution.py:143
  55.9 1.6 %fusion.6 = f32[896,512]{1,0:T(8,128)S(1)} fusion(bf16[1536,512]{0,1:T(8,128)(2,1)S(1)} %constant_dynamic-update-slice_fusion.2, bf16[896,2048]{1,0:T(8,128)(2,1)S(1)} %get-tuple-element.52), kind=kOutput, calls=%fused_computation.7 | convolution fusion | flops 1409286144 | bytes 6160384 | tf_op jit(solution)/shard_map/dot_general | solution.py:134
  57.6 0.7 slice_add_fusion.1
  58.2 0.7 slice_add_fusion.2
  59.0 0.3 collective-permute-start.9
  59.3 1.7 %fusion.52 = (f32[896,512]{1,0:T(8,128)S(1)}, f32[896,512]{1,0:T(8,128)S(1)}, f32[896,512]{1,0:T(8,128)S(1)}, f32[896,512]{1,0:T(8,128)S(1)}) fusion(f32[896,512]{1,0:T(8,128)S(1)} %slice_add_fusion.2, f32[896,512]{1,0:T(8,128)S(1)} %slice_add_fusion.1, bf16[512,512]{0,1:T(8,128)(2,1)S(1)} %pad_maximum_fusion.2, ...), kind=kOutput, calls=%fused_computation.80 | convolution fusion | flops 478478336 | bytes 14286848 | tf_op jit(solution)/shard_map/dot_general | solution.py:134
  61.1 0.7 fusion.40
  61.7 0.5 multiply_reduce_fusion
  62.3 1.0 multiply_convert_fusion.2
  63.3 0.2 pad_maximum_fusion
  63.5 0.9 fusion.25
  64.4 0.6 collective-permute-start.10
  65.0 2.4 %fusion.15 = bf16[768,512]{1,0:T(8,128)(2,1)S(1)} fusion(bf16[2688,512]{1,0:T(8,128)(2,1)S(1)} %pad_maximum_fusion, bf16[2048,2688]{1,0:T(8,128)(2,1)S(1)} %get-tuple-element.45), kind=kOutput, calls=%fused_computation.25 | convolution fusion | flops 2114322432 | bytes 7667712 | tf_op jit(solution)/shard_map/dot_general | solution.py:134
  67.5 0.9 fusion.22
  68.4 0.7 collective-permute-start.12
  69.2 0.6 collective-permute-done.11
  69.8 2.4 %fusion.62 = (bf16[768,512]{1,0:T(8,128)(2,1)S(1)}, f32[768,512]{1,0:T(8,128)S(1)}) fusion(bf16[768,512]{1,0:T(8,128)(2,1)S(1)} %collective-permute-done.11, bf16[2688,512]{1,0:T(8,128)(2,1)S(1)} %pad_maximum_fusion, bf16[2048,2688]{1,0:T(8,128)(2,1)S(1)} %get-tuple-element.45), kind=kOutput, calls=%fused_computation.89 | convolution fusion | flops 2115108864 | bytes 10027008 | tf_op jit(solution)/shard_map/dot_general | solution.py:134
  72.2 1.8 %collective-permute-start.13 = (bf16[256,512]{1,0:T(8,128)(2,1)S(1)}, bf16[256,512]{1,0:T(8,128)(2,1)S(1)}, u32[]{:S(2)}, u32[]{:S(2)}) collective-permute-start(bf16[256,512]{1,0:T(8,128)(2,1)S(1)} %get-tuple-element.88), channel_id=1, source_target_pairs={{0,2},{2,4},{4,6},{6,0},{1,3},{3,5},{5,7},{7,1},{8,10},{10,12},{12... | collective-permute-start | bytes 786440 | tf_op jit(solution)/shard_map/ppermute | solution.py:139
  74.1 0.9 collective-permute-start.14
  75.0 2.4 %collective-permute-done.12 = bf16[256,512]{1,0:T(8,128)(2,1)S(1)} collective-permute-done((bf16[256,512]{1,0:T(8,128)(2,1)S(1)}, bf16[256,512]{1,0:T(8,128)(2,1)S(1)}, u32[]{:S(2)}, u32[]{:S(2)}) %collective-permute-start.12) | collective-permute-done | bytes 262176 | tf_op jit(solution)/shard_map/ppermute | solution.py:139
  77.4 6.5 %collective-permute-done.13 = bf16[256,512]{1,0:T(8,128)(2,1)S(1)} collective-permute-done((bf16[256,512]{1,0:T(8,128)(2,1)S(1)}, bf16[256,512]{1,0:T(8,128)(2,1)S(1)}, u32[]{:S(2)}, u32[]{:S(2)}) %collective-permute-start.13) | collective-permute-done | bytes 262176 | tf_op jit(solution)/shard_map/ppermute | solution.py:139
  83.9 0.2 fusion.45
  84.1 0.1 copy.11
  84.2 17.0 %all_to_all.11 = bf16[32,16,256]{2,1,0:T(8,128)(2,1)S(1)} all-to-all(bf16[32,16,256]{2,1,0:T(8,128)(2,1)S(1)} %bitcast.46), channel_id=1, replica_groups=mesh['x'=4,'z'=8,'y'=4,'c'=2] {'x','z'}, dimensions={0} | all-to-all | bytes 524288 | tf_op jit(solution)/shard_map/all_to_all | solution.py:147
  101.2 0.3 convolution_convert_fusion
  101.5 0.7 collective-permute-start.15
  102.2 1.9 %collective-permute-start.16 = (bf16[256,256]{1,0:T(8,128)(2,1)S(1)}, bf16[256,256]{1,0:T(8,128)(2,1)S(1)}, u32[]{:S(2)}, u32[]{:S(2)}) collective-permute-start(bf16[256,256]{1,0:T(8,128)(2,1)S(1)} %convolution_convert_fusion), channel_id=1, source_target_pairs={{0,6},{2,0},{4,2},{6,4},{1,7},{3,1},{5,3},{7,5},{8,14},{10,8},{12,... | collective-permute-start | bytes 393224 | tf_op jit(solution)/shard_map/ppermute | solution.py:139
  104.1 0.5 collective-permute-start.17
  104.5 2.3 %collective-permute-done.15 = bf16[256,256]{1,0:T(8,128)(2,1)S(1)} collective-permute-done((bf16[256,256]{1,0:T(8,128)(2,1)S(1)}, bf16[256,256]{1,0:T(8,128)(2,1)S(1)}, u32[]{:S(2)}, u32[]{:S(2)}) %collective-permute-start.15) | collective-permute-done | bytes 131104 | tf_op jit(solution)/shard_map/ppermute | solution.py:139
  106.9 1.4 %collective-permute-done.16 = bf16[256,256]{1,0:T(8,128)(2,1)S(1)} collective-permute-done((bf16[256,256]{1,0:T(8,128)(2,1)S(1)}, bf16[256,256]{1,0:T(8,128)(2,1)S(1)}, u32[]{:S(2)}, u32[]{:S(2)}) %collective-permute-start.16) | collective-permute-done | bytes 131104 | tf_op jit(solution)/shard_map/ppermute | solution.py:139
  108.3 0.7 collective-permute-done.17
  109.2 5.3 %collective-permute-start.18 = (bf16[4,256,256]{2,1,0:T(8,128)(2,1)S(1)}, bf16[4,256,256]{2,1,0:T(8,128)(2,1)S(1)}, u32[]{:S(2)}, u32[]{:S(2)}) collective-permute-start(bf16[4,256,256]{2,1,0:T(8,128)(2,1)S(1)} %pad_maximum_fusion.4), channel_id=1, source_target_pairs={{0,1},{1,0},{2,3},{3,2},{4,5},{5,4},{6,7},{7,6},{8,9},{9,8},{10,11... | collective-permute-start | bytes 1572872 | tf_op jit(solution)/shard_map/ppermute | solution.py:143
  114.5 0.6 broadcast_in_dim.7
  115.1 0.1 broadcast_in_dim.6
  115.3 0.7 collective-permute-done.18
  116.1 1.0 copy-done
  (45 shorter events, 1.0 us)
Async XLA Ops:
  27.9 11.6 %collective-permute-start = (bf16[512,512]{0,1:T(8,128)(2,1)S(1)}, bf16[512,512]{0,1:T(8,128)(2,1)S(1)}, u32[]{:S(2)}, u32[]{:S(2)}) collective-permute-start(bf16[512,512]{0,1:T(8,128)(2,1)S(1)} %bitcast.40), channel_id=1, source_target_pairs={{0,6},{2,0},{4,2},{6,4},{1,7},{3,1},{5,3},{7,5},{8,14},{10,8},{12,... | collective-permute-start | bytes 1572872 | tf_op jit(solution)/shard_map/ppermute | solution.py:139
  30.7 10.8 %collective-permute-start.1 = (bf16[512,512]{0,1:T(8,128)(2,1)S(1)}, bf16[512,512]{0,1:T(8,128)(2,1)S(1)}, u32[]{:S(2)}, u32[]{:S(2)}) collective-permute-start(bf16[512,512]{0,1:T(8,128)(2,1)S(1)} %bitcast.41), channel_id=1, source_target_pairs={{0,2},{2,4},{4,6},{6,0},{1,3},{3,5},{5,7},{7,1},{8,10},{10,12},{12... | collective-permute-start | bytes 1572872 | tf_op jit(solution)/shard_map/ppermute | solution.py:139
  30.7 10.8 %collective-permute-start.2 = (bf16[512,512]{0,1:T(8,128)(2,1)S(1)}, bf16[512,512]{0,1:T(8,128)(2,1)S(1)}, u32[]{:S(2)}, u32[]{:S(2)}) collective-permute-start(bf16[512,512]{0,1:T(8,128)(2,1)S(1)} %bitcast.42), channel_id=1, source_target_pairs={{0,1},{1,0},{2,3},{3,2},{4,5},{5,4},{6,7},{7,6},{8,9},{9,8},{10,11... | collective-permute-start | bytes 1572872 | tf_op jit(solution)/shard_map/ppermute | solution.py:143
  41.6 8.1 %collective-permute-start.3 = (bf16[1024,512]{0,1:T(8,128)(2,1)S(1)}, bf16[1024,512]{0,1:T(8,128)(2,1)S(1)}, u32[]{:S(2)}, u32[]{:S(2)}) collective-permute-start(bf16[1024,512]{0,1:T(8,128)(2,1)S(1)} %pad_maximum_fusion.1), channel_id=1, source_target_pairs={{0,1},{1,0},{2,3},{3,2},{4,5},{5,4},{6,7},{7,6},{8,9},{9,8},{10,11... | collective-permute-start | bytes 3145736 | tf_op jit(solution)/shard_map/ppermute | solution.py:143
  46.5 7.9 %collective-permute-start.4 = (bf16[256,256]{0,1:T(8,128)(2,1)S(1)}, bf16[256,256]{0,1:T(8,128)(2,1)S(1)}, u32[]{:S(2)}, u32[]{:S(2)}) collective-permute-start(bf16[256,256]{0,1:T(8,128)(2,1)S(1)} %get-tuple-element.93), channel_id=1, source_target_pairs={{0,6},{2,0},{4,2},{6,4},{1,7},{3,1},{5,3},{7,5},{8,14},{10,8},{12,... | collective-permute-start | bytes 393224 | tf_op jit(solution)/shard_map/ppermute | solution.py:139
  46.6 7.8 %collective-permute-start.5 = (bf16[256,256]{0,1:T(8,128)(2,1)S(1)}, bf16[256,256]{0,1:T(8,128)(2,1)S(1)}, u32[]{:S(2)}, u32[]{:S(2)}) collective-permute-start(bf16[256,256]{0,1:T(8,128)(2,1)S(1)} %get-tuple-element.91), channel_id=1, source_target_pairs={{0,2},{2,4},{4,6},{6,0},{1,3},{3,5},{5,7},{7,1},{8,10},{10,12},{12... | collective-permute-start | bytes 393224 | tf_op jit(solution)/shard_map/ppermute | solution.py:139
  48.1 9.4 %collective-permute-start.7 = (bf16[256,256]{0,1:T(8,128)(2,1)S(1)}, bf16[256,256]{0,1:T(8,128)(2,1)S(1)}, u32[]{:S(2)}, u32[]{:S(2)}) collective-permute-start(bf16[256,256]{0,1:T(8,128)(2,1)S(1)} %get-tuple-element.92), channel_id=1, source_target_pairs={{0,6},{2,0},{4,2},{6,4},{1,7},{3,1},{5,3},{7,5},{8,14},{10,8},{12,... | collective-permute-start | bytes 393224 | tf_op jit(solution)/shard_map/ppermute | solution.py:139
  49.3 8.2 %collective-permute-start.8 = (bf16[256,256]{0,1:T(8,128)(2,1)S(1)}, bf16[256,256]{0,1:T(8,128)(2,1)S(1)}, u32[]{:S(2)}, u32[]{:S(2)}) collective-permute-start(bf16[256,256]{0,1:T(8,128)(2,1)S(1)} %get-tuple-element.90), channel_id=1, source_target_pairs={{0,2},{2,4},{4,6},{6,0},{1,3},{3,5},{5,7},{7,1},{8,10},{10,12},{12... | collective-permute-start | bytes 393224 | tf_op jit(solution)/shard_map/ppermute | solution.py:139
  54.5 3.0 %collective-permute-start.6 = (bf16[256,512]{0,1:T(8,128)(2,1)S(1)}, bf16[256,512]{0,1:T(8,128)(2,1)S(1)}, u32[]{:S(2)}, u32[]{:S(2)}) collective-permute-start(bf16[256,512]{0,1:T(8,128)(2,1)S(1)} %constant_dynamic-update-slice_fusion), channel_id=1, source_target_pairs={{0,1},{1,0},{2,3},{3,2},{4,5},{5,4},{6,7},{7,6},{8,9},{9,8},{10,11... | collective-permute-start | bytes 786440 | tf_op jit(solution)/shard_map/ppermute | solution.py:143
  59.0 2.0 %collective-permute-start.9 = (bf16[256,512]{0,1:T(8,128)(2,1)S(1)}, bf16[256,512]{0,1:T(8,128)(2,1)S(1)}, u32[]{:S(2)}, u32[]{:S(2)}) collective-permute-start(bf16[256,512]{0,1:T(8,128)(2,1)S(1)} %constant_dynamic-update-slice_fusion.8), channel_id=1, source_target_pairs={{0,1},{1,0},{2,3},{3,2},{4,5},{5,4},{6,7},{7,6},{8,9},{9,8},{10,11... | collective-permute-start | bytes 786440 | tf_op jit(solution)/shard_map/ppermute | solution.py:143
  64.4 3.0 %collective-permute-start.10 = (bf16[256,512]{1,0:T(8,128)(2,1)S(1)}, bf16[256,512]{1,0:T(8,128)(2,1)S(1)}, u32[]{:S(2)}, u32[]{:S(2)}) collective-permute-start(bf16[256,512]{1,0:T(8,128)(2,1)S(1)} %fusion.25), channel_id=1, source_target_pairs={{0,1},{1,0},{2,3},{3,2},{4,5},{5,4},{6,7},{7,6},{8,9},{9,8},{10,11... | collective-permute-start | bytes 786440 | tf_op jit(solution)/shard_map/ppermute | solution.py:143
  67.4 2.4 %collective-permute-start.11 = (bf16[768,512]{1,0:T(8,128)(2,1)S(1)}, bf16[768,512]{1,0:T(8,128)(2,1)S(1)}, u32[]{:S(2)}, u32[]{:S(2)}) collective-permute-start(bf16[768,512]{1,0:T(8,128)(2,1)S(1)} %fusion.15), channel_id=1, source_target_pairs={{0,1},{1,0},{2,3},{3,2},{4,5},{5,4},{6,7},{7,6},{8,9},{9,8},{10,11... | collective-permute-start | bytes 2359304 | tf_op jit(solution)/shard_map/ppermute | solution.py:143
  68.4 9.0 %collective-permute-start.12 = (bf16[256,512]{1,0:T(8,128)(2,1)S(1)}, bf16[256,512]{1,0:T(8,128)(2,1)S(1)}, u32[]{:S(2)}, u32[]{:S(2)}) collective-permute-start(bf16[256,512]{1,0:T(8,128)(2,1)S(1)} %fusion.22), channel_id=1, source_target_pairs={{0,4},{2,6},{4,0},{6,2},{1,5},{3,7},{5,1},{7,3},{8,12},{10,14},{12... | collective-permute-start | bytes 786440 | tf_op jit(solution)/shard_map/ppermute | solution.py:139
  72.2 11.7 %collective-permute-start.13 = (bf16[256,512]{1,0:T(8,128)(2,1)S(1)}, bf16[256,512]{1,0:T(8,128)(2,1)S(1)}, u32[]{:S(2)}, u32[]{:S(2)}) collective-permute-start(bf16[256,512]{1,0:T(8,128)(2,1)S(1)} %get-tuple-element.88), channel_id=1, source_target_pairs={{0,2},{2,4},{4,6},{6,0},{1,3},{3,5},{5,7},{7,1},{8,10},{10,12},{12... | collective-permute-start | bytes 786440 | tf_op jit(solution)/shard_map/ppermute | solution.py:139
  74.1 9.9 %collective-permute-start.14 = (bf16[256,512]{1,0:T(8,128)(2,1)S(1)}, bf16[256,512]{1,0:T(8,128)(2,1)S(1)}, u32[]{:S(2)}, u32[]{:S(2)}) collective-permute-start(bf16[256,512]{1,0:T(8,128)(2,1)S(1)} %get-tuple-element.89), channel_id=1, source_target_pairs={{0,6},{2,0},{4,2},{6,4},{1,7},{3,1},{5,3},{7,5},{8,14},{10,8},{12,... | collective-permute-start | bytes 786440 | tf_op jit(solution)/shard_map/ppermute | solution.py:139
  101.5 5.4 %collective-permute-start.15 = (bf16[256,256]{1,0:T(8,128)(2,1)S(1)}, bf16[256,256]{1,0:T(8,128)(2,1)S(1)}, u32[]{:S(2)}, u32[]{:S(2)}) collective-permute-start(bf16[256,256]{1,0:T(8,128)(2,1)S(1)} %convolution_convert_fusion), channel_id=1, source_target_pairs={{0,4},{2,6},{4,0},{6,2},{1,5},{3,7},{5,1},{7,3},{8,12},{10,14},{12... | collective-permute-start | bytes 393224 | tf_op jit(solution)/shard_map/ppermute | solution.py:139
  102.2 6.2 %collective-permute-start.16 = (bf16[256,256]{1,0:T(8,128)(2,1)S(1)}, bf16[256,256]{1,0:T(8,128)(2,1)S(1)}, u32[]{:S(2)}, u32[]{:S(2)}) collective-permute-start(bf16[256,256]{1,0:T(8,128)(2,1)S(1)} %convolution_convert_fusion), channel_id=1, source_target_pairs={{0,6},{2,0},{4,2},{6,4},{1,7},{3,1},{5,3},{7,5},{8,14},{10,8},{12,... | collective-permute-start | bytes 393224 | tf_op jit(solution)/shard_map/ppermute | solution.py:139
  104.1 5.0 %collective-permute-start.17 = (bf16[256,256]{1,0:T(8,128)(2,1)S(1)}, bf16[256,256]{1,0:T(8,128)(2,1)S(1)}, u32[]{:S(2)}, u32[]{:S(2)}) collective-permute-start(bf16[256,256]{1,0:T(8,128)(2,1)S(1)} %convolution_convert_fusion), channel_id=1, source_target_pairs={{0,2},{2,4},{4,6},{6,0},{1,3},{3,5},{5,7},{7,1},{8,10},{10,12},{12... | collective-permute-start | bytes 393224 | tf_op jit(solution)/shard_map/ppermute | solution.py:139
  109.2 6.9 %collective-permute-start.18 = (bf16[4,256,256]{2,1,0:T(8,128)(2,1)S(1)}, bf16[4,256,256]{2,1,0:T(8,128)(2,1)S(1)}, u32[]{:S(2)}, u32[]{:S(2)}) collective-permute-start(bf16[4,256,256]{2,1,0:T(8,128)(2,1)S(1)} %pad_maximum_fusion.4), channel_id=1, source_target_pairs={{0,1},{1,0},{2,3},{3,2},{4,5},{5,4},{6,7},{7,6},{8,9},{9,8},{10,11... | collective-permute-start | bytes 1572872 | tf_op jit(solution)/shard_map/ppermute | solution.py:143
  116.1 1.0 copy-start

commit v7 on v6

--- a/solution.py
+++ b/solution.py
@@ -165,7 +165,6 @@
     slot_count = max(2, 2 * tok_count // expert_count)
     rows = expert_count * slot_count
     width = model_width // (ys * cores)
-    half = ys * width
     barrier = lax.optimization_barrier
 
     def to_experts(send):
@@ -174,13 +173,8 @@
     def neighbours(piece):
         return [shift_y(piece, -1), shift_y(piece, 1)]
 
-    def beyond(near):
-        cut = rows // 2
-        return [shift_y(near[0][:, :cut], -1), shift_y(near[1][:, cut:], 1)]
-
-    def both_cores(pieces, axis):
-        own = jnp.concatenate(pieces, axis=axis)
-        return own, swap_cores(own)
+    def both_cores(own):
+        return jnp.concatenate([own, swap_cores(own)], axis=0)
 
     dispatch, send = dispatch_rows(expert_route, tokens, cotangent, rows, width)
     received, seed = barrier((to_experts(send), sign_seeds))
@@ -189,8 +183,8 @@
     near = neighbours(piece)
     crossed = swap_cores(piece)
     near, mats, down, crossed = barrier((near, mats, down, crossed))
-    x_far = beyond([part[:width] for part in near])
-    cot_far = beyond([part[width:] for part in near])
+    x_far = shift_y(near[0][:width], -1)
+    cot_far = shift_y(near[1][width:], 1)
     joint = jnp.concatenate(near, axis=0)
     other = swap_cores(joint)
     near = near + [piece, other[: 2 * width], other[2 * width :], crossed]
@@ -199,10 +193,10 @@
     split = 2 * width
     sums = dot(mats[split:], jnp.concatenate(x_near, axis=0), 0, 0)
     sums, cot_near, x_far = barrier((sums, cot_near, x_far))
-    x_far = jnp.concatenate(both_cores(x_far, 1), axis=0)
+    x_far = both_cores(x_far)
     cot_sum = dot(down[:, split:], jnp.concatenate(cot_near, axis=0), 1, 0)
     sums, x_far, cot_sum, cot_far = barrier((sums, x_far, cot_sum, cot_far))
-    cot_far = jnp.concatenate(both_cores(cot_far, 1), axis=0)
+    cot_far = both_cores(cot_far)
     spans = [slice(at * hidden_cols, (at + 1) * hidden_cols) for at in range(3)]
     factors = forward_factors(*[sums[span] + dot(mats[:split, span], x_far, 0, 0) for span in spans])
     factors, cot_far = barrier((factors, cot_far))

time: 117 us -> 116 us (level)
  starting transfers between devices: 28.5 us -> 24.6 us
  waiting for transfers between devices: 16.8 us -> 19.4 us
    ppermute x12 -> x10, starting transfers between devices: 12.4 us -> 9.18 us  [shift_y(): lax.ppermute(value, 'y', [(i, (i + shift) % count) for i in range(count)])]
    ppermute x12 -> x10, waiting for transfers between devices: 15.5 us -> 16.8 us  [shift_y(): lax.ppermute(value, 'y', [(i, (i + shift) % count) for i in range(count)])]
    ppermute x7, waiting for transfers between devices: 1.35 us -> 2.53 us  [swap_cores(): return lax.ppermute(value, 'c', SWAP)]
  transfers between devices with their start and end apart: 19 -> 17, of which waited for: 8 -> 10; matrix products, arithmetic and copies ran while one was open for 13% -> 13% of each run, Pallas kernels for 4% -> 4%
where the time goes in v7:
time: 116 us
  blocking collectives  42.9 us (37%)
  starting transfers between devices  24.6 us (21%)
  waiting for transfers between devices  19.4 us (17%)
  matrix products  16.8 us (14%)
  Pallas kernels  5.71 us (5%)
  local copies, waits for them, and re-layouts  2.31 us (2%)
  other arithmetic  2.2 us (2%)
  between operations  1.65 us (1%)
    all_to_all x2, blocking collectives, exchange(): lax.all_to_all(value, EXPERT, split_axis=0, concat_axis=0, tiled=True)  42.9 us
    ppermute x10, waiting for transfers between devices, shift_y(): lax.ppermute(value, 'y', [(i, (i + shift) % count) for i in range(count)])  16.8 us
    dot_general x11, matrix products, dot(): lax.dot_general(a, b, (((ca,), (cb,)), ((), ())), preferred_element_type=...  16.8 us
    ppermute x7, starting transfers between devices, swap_cores(): return lax.ppermute(value, 'c', SWAP)  15.5 us
    ppermute x10, starting transfers between devices, shift_y(): lax.ppermute(value, 'y', [(i, (i + shift) % count) for i in range(count)])  9.18 us
    pallas_call x1, Pallas kernels, stage_weights(): pl.pallas_call(stage_kernel, out_shape=[jax.ShapeDtypeStruct((model, 3 *...  4.4 us
    ppermute x7, waiting for transfers between devices, swap_cores(): return lax.ppermute(value, 'c', SWAP)  2.53 us
  transfers between devices with their start and end apart: 17, of which 10 were waited for; matrix products, arithmetic and copies ran while one was open for 13% of the time, Pallas kernels for 4%

profile of v7, /device:TPU:1, one launch (start us, length us, event | category | flops | bytes accessed | tf_op | source)
XLA Modules:
  0.0 115.6 jit_solution(6465603219807956875)
XLA Ops:
  0.6 1.3 %dispatch.1 = (bf16[512,256]{1,0:T(8,128)(2,1)S(1)}, bf16[512,512]{1,0:T(8,128)(2,1)S(1)}) custom-call(s32[1,256]{1,0:T(1,128)} %bitcast.50, bf16[256,2048]{1,0:T(8,128)(2,1)} %tokens_ref.1, bf16[256,2048]{1,0:T(8,128)(2,1)} %cot_ref.1), custom_call_target="tpu_custom_call" | custom-call | tf_op jit(solution)/shard_map/dispatch/pallas_call | solution.py:54
  2.0 26.0 %all_to_all.10 = bf16[32,16,512]{2,1,0:T(8,128)(2,1)S(1)} all-to-all(bf16[32,16,512]{2,1,0:T(8,128)(2,1)S(1)} %bitcast.39), channel_id=1, replica_groups=mesh['x'=4,'z'=8,'y'=4,'c'=2] {'x','z'}, dimensions={0} | all-to-all | bytes 1048576 | tf_op jit(solution)/shard_map/all_to_all | solution.py:147
  27.9 2.7 %collective-permute-start = (bf16[512,512]{0,1:T(8,128)(2,1)S(1)}, bf16[512,512]{0,1:T(8,128)(2,1)S(1)}, u32[]{:S(2)}, u32[]{:S(2)}) collective-permute-start(bf16[512,512]{0,1:T(8,128)(2,1)S(1)} %bitcast.40), channel_id=1, source_target_pairs={{0,6},{2,0},{4,2},{6,4},{1,7},{3,1},{5,3},{7,5},{8,14},{10,8},{12,... | collective-permute-start | bytes 1572872 | tf_op jit(solution)/shard_map/ppermute | solution.py:139
  30.7 3.8 %collective-permute-start.2 = (bf16[512,512]{0,1:T(8,128)(2,1)S(1)}, bf16[512,512]{0,1:T(8,128)(2,1)S(1)}, u32[]{:S(2)}, u32[]{:S(2)}) collective-permute-start(bf16[512,512]{0,1:T(8,128)(2,1)S(1)} %bitcast.42), channel_id=1, source_target_pairs={{0,1},{1,0},{2,3},{3,2},{4,5},{5,4},{6,7},{7,6},{8,9},{9,8},{10,11... | collective-permute-start | bytes 1572872 | tf_op jit(solution)/shard_map/ppermute | solution.py:143
  35.1 4.4 %stage_weights.1 = (bf16[2048,2688]{1,0:T(8,128)(2,1)S(1)}, bf16[896,2048]{1,0:T(8,128)(2,1)S(1)}) custom-call(s32[1]{0:T(128)S(6)} %copy.31.seed_ref, bf16[1,2048,896]{2,1,0:T(8,128)(2,1)} %gate_ref.1, bf16[1,2048,896]{2,1,0:T(8,128)(2,1)} %up_ref.1, bf16[1,896,2048]{2,1,0:T(8,128)(2,1)} %down_ref.1), custom_call_target="tpu_custom_call" | custom-call | bytes 25690112 | tf_op jit(solution)/shard_map/stage_weights/pallas_call | solution.py:121
  39.5 2.0 %collective-permute-done.1 = bf16[512,512]{0,1:T(8,128)(2,1)S(1)} collective-permute-done((bf16[512,512]{0,1:T(8,128)(2,1)S(1)}, bf16[512,512]{0,1:T(8,128)(2,1)S(1)}, u32[]{:S(2)}, u32[]{:S(2)}) %collective-permute-start.1) | collective-permute-done | bytes 524320 | tf_op jit(solution)/shard_map/ppermute | solution.py:139
  41.5 0.1 pad_maximum_fusion.1
  41.6 4.8 %collective-permute-start.3 = (bf16[1024,512]{0,1:T(8,128)(2,1)S(1)}, bf16[1024,512]{0,1:T(8,128)(2,1)S(1)}, u32[]{:S(2)}, u32[]{:S(2)}) collective-permute-start(bf16[1024,512]{0,1:T(8,128)(2,1)S(1)} %pad_maximum_fusion.1), channel_id=1, source_target_pairs={{0,1},{1,0},{2,3},{3,2},{4,5},{5,4},{6,7},{7,6},{8,9},{9,8},{10,11... | collective-permute-start | bytes 3145736 | tf_op jit(solution)/shard_map/ppermute | solution.py:143
  46.6 1.5 %collective-permute-start.6 = (bf16[256,512]{0,1:T(8,128)(2,1)S(1)}, bf16[256,512]{0,1:T(8,128)(2,1)S(1)}, u32[]{:S(2)}, u32[]{:S(2)}) collective-permute-start(bf16[256,512]{0,1:T(8,128)(2,1)S(1)} %get-tuple-element.51), channel_id=1, source_target_pairs={{0,2},{2,4},{4,6},{6,0},{1,3},{3,5},{5,7},{7,1},{8,10},{10,12},{12... | collective-permute-start | bytes 786440 | tf_op jit(solution)/shard_map/ppermute | solution.py:139
  48.2 0.5 collective-permute-done.3
  48.9 4.5 %fusion = f32[2688,512]{1,0:T(8,128)S(1)} fusion(bf16[1536,512]{0,1:T(8,128)(2,1)S(1)} %get-tuple-element.90, bf16[2048,2688]{1,0:T(8,128)(2,1)S(1)} %get-tuple-element.43), kind=kOutput, calls=%fused_computation | convolution fusion | flops 4227858432 | bytes 15335424 | tf_op jit(solution)/shard_map/dot_general | solution.py:134
  53.4 1.1 collective-permute-done.4
  54.5 1.1 collective-permute-start.5
  55.7 1.6 %fusion.6 = f32[896,512]{1,0:T(8,128)S(1)} fusion(bf16[1536,512]{0,1:T(8,128)(2,1)S(1)} %constant_dynamic-update-slice_fusion.1, bf16[896,2048]{1,0:T(8,128)(2,1)S(1)} %get-tuple-element.49), kind=kOutput, calls=%fused_computation.7 | convolution fusion | flops 1409286144 | bytes 6160384 | tf_op jit(solution)/shard_map/dot_general | solution.py:134
  57.4 0.7 slice_add_fusion.1
  58.1 0.7 slice_add_fusion.2
  58.8 0.1 collective-permute-start.7
  58.9 1.7 %fusion.52 = (f32[896,512]{1,0:T(8,128)S(1)}, f32[896,512]{1,0:T(8,128)S(1)}, f32[896,512]{1,0:T(8,128)S(1)}, f32[896,512]{1,0:T(8,128)S(1)}) fusion(f32[896,512]{1,0:T(8,128)S(1)} %slice_add_fusion.2, f32[896,512]{1,0:T(8,128)S(1)} %slice_add_fusion.1, bf16[512,512]{0,1:T(8,128)(2,1)S(1)} %pad_maximum_fusion.2, ...), kind=kOutput, calls=%fused_computation.76 | convolution fusion | flops 478478336 | bytes 14286848 | tf_op jit(solution)/shard_map/dot_general | solution.py:134
  60.7 0.7 fusion.40
  61.3 0.5 multiply_reduce_fusion
  61.9 1.0 multiply_convert_fusion.2
  62.9 0.2 pad_maximum_fusion
  63.1 0.9 fusion.25
  64.0 0.6 collective-permute-start.8
  64.6 2.4 %fusion.15 = bf16[768,512]{1,0:T(8,128)(2,1)S(1)} fusion(bf16[2688,512]{1,0:T(8,128)(2,1)S(1)} %pad_maximum_fusion, bf16[2048,2688]{1,0:T(8,128)(2,1)S(1)} %get-tuple-element.43), kind=kOutput, calls=%fused_computation.25 | convolution fusion | flops 2114322432 | bytes 7667712 | tf_op jit(solution)/shard_map/dot_general | solution.py:134
  67.0 0.1 collective-permute-start.9
  67.1 0.9 fusion.22
  68.0 0.1 collective-permute-start.10
  68.1 1.2 %collective-permute-done.9 = bf16[768,512]{1,0:T(8,128)(2,1)S(1)} collective-permute-done((bf16[768,512]{1,0:T(8,128)(2,1)S(1)}, bf16[768,512]{1,0:T(8,128)(2,1)S(1)}, u32[]{:S(2)}, u32[]{:S(2)}) %collective-permute-start.9) | collective-permute-done | bytes 786464 | tf_op jit(solution)/shard_map/ppermute | solution.py:143
  69.4 2.4 %fusion.60 = (bf16[768,512]{1,0:T(8,128)(2,1)S(1)}, f32[768,512]{1,0:T(8,128)S(1)}) fusion(bf16[768,512]{1,0:T(8,128)(2,1)S(1)} %collective-permute-done.9, bf16[2688,512]{1,0:T(8,128)(2,1)S(1)} %pad_maximum_fusion, bf16[2048,2688]{1,0:T(8,128)(2,1)S(1)} %get-tuple-element.43), kind=kOutput, calls=%fused_computation.83 | convolution fusion | flops 2115108864 | bytes 10027008 | tf_op jit(solution)/shard_map/dot_general | solution.py:134
  71.8 0.8 collective-permute-start.11
  72.7 2.1 %collective-permute-start.12 = (bf16[256,512]{1,0:T(8,128)(2,1)S(1)}, bf16[256,512]{1,0:T(8,128)(2,1)S(1)}, u32[]{:S(2)}, u32[]{:S(2)}) collective-permute-start(bf16[256,512]{1,0:T(8,128)(2,1)S(1)} %get-tuple-element.85), channel_id=1, source_target_pairs={{0,6},{2,0},{4,2},{6,4},{1,7},{3,1},{5,3},{7,5},{8,14},{10,8},{12,... | collective-permute-start | bytes 786440 | tf_op jit(solution)/shard_map/ppermute | solution.py:139
  74.8 2.2 %collective-permute-done.10 = bf16[256,512]{1,0:T(8,128)(2,1)S(1)} collective-permute-done((bf16[256,512]{1,0:T(8,128)(2,1)S(1)}, bf16[256,512]{1,0:T(8,128)(2,1)S(1)}, u32[]{:S(2)}, u32[]{:S(2)}) %collective-permute-start.10) | collective-permute-done | bytes 262176 | tf_op jit(solution)/shard_map/ppermute | solution.py:139
  77.0 6.5 %collective-permute-done.11 = bf16[256,512]{1,0:T(8,128)(2,1)S(1)} collective-permute-done((bf16[256,512]{1,0:T(8,128)(2,1)S(1)}, bf16[256,512]{1,0:T(8,128)(2,1)S(1)}, u32[]{:S(2)}, u32[]{:S(2)}) %collective-permute-start.11) | collective-permute-done | bytes 262176 | tf_op jit(solution)/shard_map/ppermute | solution.py:139
  83.5 0.2 fusion.45
  83.7 0.1 copy.11
  83.8 17.0 %all_to_all.11 = bf16[32,16,256]{2,1,0:T(8,128)(2,1)S(1)} all-to-all(bf16[32,16,256]{2,1,0:T(8,128)(2,1)S(1)} %bitcast.46), channel_id=1, replica_groups=mesh['x'=4,'z'=8,'y'=4,'c'=2] {'x','z'}, dimensions={0} | all-to-all | bytes 524288 | tf_op jit(solution)/shard_map/all_to_all | solution.py:147
  100.8 0.3 convolution_convert_fusion
  101.2 1.3 %collective-permute-start.14 = (bf16[256,256]{1,0:T(8,128)(2,1)S(1)}, bf16[256,256]{1,0:T(8,128)(2,1)S(1)}, u32[]{:S(2)}, u32[]{:S(2)}) collective-permute-start(bf16[256,256]{1,0:T(8,128)(2,1)S(1)} %convolution_convert_fusion), channel_id=1, source_target_pairs={{0,6},{2,0},{4,2},{6,4},{1,7},{3,1},{5,3},{7,5},{8,14},{10,8},{12,... | collective-permute-start | bytes 393224 | tf_op jit(solution)/shard_map/ppermute | solution.py:139
  102.5 0.4 collective-permute-start.15
  102.9 3.7 %collective-permute-done.13 = bf16[256,256]{1,0:T(8,128)(2,1)S(1)} collective-permute-done((bf16[256,256]{1,0:T(8,128)(2,1)S(1)}, bf16[256,256]{1,0:T(8,128)(2,1)S(1)}, u32[]{:S(2)}, u32[]{:S(2)}) %collective-permute-start.13) | collective-permute-done | bytes 131104 | tf_op jit(solution)/shard_map/ppermute | solution.py:139
  106.5 0.1 collective-permute-done.14
  106.7 1.2 %collective-permute-done.15 = bf16[256,256]{1,0:T(8,128)(2,1)S(1)} collective-permute-done((bf16[256,256]{1,0:T(8,128)(2,1)S(1)}, bf16[256,256]{1,0:T(8,128)(2,1)S(1)}, u32[]{:S(2)}, u32[]{:S(2)}) %collective-permute-start.15) | collective-permute-done | bytes 131104 | tf_op jit(solution)/shard_map/ppermute | solution.py:139
  108.0 5.0 %collective-permute-start.16 = (bf16[4,256,256]{2,1,0:T(8,128)(2,1)S(1)}, bf16[4,256,256]{2,1,0:T(8,128)(2,1)S(1)}, u32[]{:S(2)}, u32[]{:S(2)}) collective-permute-start(bf16[4,256,256]{2,1,0:T(8,128)(2,1)S(1)} %pad_maximum_fusion.4), channel_id=1, source_target_pairs={{0,1},{1,0},{2,3},{3,2},{4,5},{5,4},{6,7},{7,6},{8,9},{9,8},{10,11... | collective-permute-start | bytes 1572872 | tf_op jit(solution)/shard_map/ppermute | solution.py:143
  113.0 0.6 broadcast_in_dim.7
  113.6 0.1 broadcast_in_dim.6
  113.8 0.7 collective-permute-done.16
  114.6 1.0 copy-done
  (35 shorter events, 0.9 us)
Async XLA Ops:
  27.9 11.6 %collective-permute-start = (bf16[512,512]{0,1:T(8,128)(2,1)S(1)}, bf16[512,512]{0,1:T(8,128)(2,1)S(1)}, u32[]{:S(2)}, u32[]{:S(2)}) collective-permute-start(bf16[512,512]{0,1:T(8,128)(2,1)S(1)} %bitcast.40), channel_id=1, source_target_pairs={{0,6},{2,0},{4,2},{6,4},{1,7},{3,1},{5,3},{7,5},{8,14},{10,8},{12,... | collective-permute-start | bytes 1572872 | tf_op jit(solution)/shard_map/ppermute | solution.py:139
  30.7 10.8 %collective-permute-start.1 = (bf16[512,512]{0,1:T(8,128)(2,1)S(1)}, bf16[512,512]{0,1:T(8,128)(2,1)S(1)}, u32[]{:S(2)}, u32[]{:S(2)}) collective-permute-start(bf16[512,512]{0,1:T(8,128)(2,1)S(1)} %bitcast.41), channel_id=1, source_target_pairs={{0,2},{2,4},{4,6},{6,0},{1,3},{3,5},{5,7},{7,1},{8,10},{10,12},{12... | collective-permute-start | bytes 1572872 | tf_op jit(solution)/shard_map/ppermute | solution.py:139
  30.7 10.8 %collective-permute-start.2 = (bf16[512,512]{0,1:T(8,128)(2,1)S(1)}, bf16[512,512]{0,1:T(8,128)(2,1)S(1)}, u32[]{:S(2)}, u32[]{:S(2)}) collective-permute-start(bf16[512,512]{0,1:T(8,128)(2,1)S(1)} %bitcast.42), channel_id=1, source_target_pairs={{0,1},{1,0},{2,3},{3,2},{4,5},{5,4},{6,7},{7,6},{8,9},{9,8},{10,11... | collective-permute-start | bytes 1572872 | tf_op jit(solution)/shard_map/ppermute | solution.py:143
  41.6 7.1 %collective-permute-start.3 = (bf16[1024,512]{0,1:T(8,128)(2,1)S(1)}, bf16[1024,512]{0,1:T(8,128)(2,1)S(1)}, u32[]{:S(2)}, u32[]{:S(2)}) collective-permute-start(bf16[1024,512]{0,1:T(8,128)(2,1)S(1)} %pad_maximum_fusion.1), channel_id=1, source_target_pairs={{0,1},{1,0},{2,3},{3,2},{4,5},{5,4},{6,7},{7,6},{8,9},{9,8},{10,11... | collective-permute-start | bytes 3145736 | tf_op jit(solution)/shard_map/ppermute | solution.py:143
  46.5 8.0 %collective-permute-start.4 = (bf16[256,512]{0,1:T(8,128)(2,1)S(1)}, bf16[256,512]{0,1:T(8,128)(2,1)S(1)}, u32[]{:S(2)}, u32[]{:S(2)}) collective-permute-start(bf16[256,512]{0,1:T(8,128)(2,1)S(1)} %get-tuple-element.86), channel_id=1, source_target_pairs={{0,6},{2,0},{4,2},{6,4},{1,7},{3,1},{5,3},{7,5},{8,14},{10,8},{12,... | collective-permute-start | bytes 786440 | tf_op jit(solution)/shard_map/ppermute | solution.py:139
  46.6 10.8 %collective-permute-start.6 = (bf16[256,512]{0,1:T(8,128)(2,1)S(1)}, bf16[256,512]{0,1:T(8,128)(2,1)S(1)}, u32[]{:S(2)}, u32[]{:S(2)}) collective-permute-start(bf16[256,512]{0,1:T(8,128)(2,1)S(1)} %get-tuple-element.51), channel_id=1, source_target_pairs={{0,2},{2,4},{4,6},{6,0},{1,3},{3,5},{5,7},{7,1},{8,10},{10,12},{12... | collective-permute-start | bytes 786440 | tf_op jit(solution)/shard_map/ppermute | solution.py:139
  54.5 2.8 %collective-permute-start.5 = (bf16[256,512]{0,1:T(8,128)(2,1)S(1)}, bf16[256,512]{0,1:T(8,128)(2,1)S(1)}, u32[]{:S(2)}, u32[]{:S(2)}) collective-permute-start(bf16[256,512]{0,1:T(8,128)(2,1)S(1)} %collective-permute-done.4), channel_id=1, source_target_pairs={{0,1},{1,0},{2,3},{3,2},{4,5},{5,4},{6,7},{7,6},{8,9},{9,8},{10,11... | collective-permute-start | bytes 786440 | tf_op jit(solution)/shard_map/ppermute | solution.py:143
  58.8 1.8 %collective-permute-start.7 = (bf16[256,512]{0,1:T(8,128)(2,1)S(1)}, bf16[256,512]{0,1:T(8,128)(2,1)S(1)}, u32[]{:S(2)}, u32[]{:S(2)}) collective-permute-start(bf16[256,512]{0,1:T(8,128)(2,1)S(1)} %collective-permute-done.6), channel_id=1, source_target_pairs={{0,1},{1,0},{2,3},{3,2},{4,5},{5,4},{6,7},{7,6},{8,9},{9,8},{10,11... | collective-permute-start | bytes 786440 | tf_op jit(solution)/shard_map/ppermute | solution.py:143
  64.0 3.0 %collective-permute-start.8 = (bf16[256,512]{1,0:T(8,128)(2,1)S(1)}, bf16[256,512]{1,0:T(8,128)(2,1)S(1)}, u32[]{:S(2)}, u32[]{:S(2)}) collective-permute-start(bf16[256,512]{1,0:T(8,128)(2,1)S(1)} %fusion.25), channel_id=1, source_target_pairs={{0,1},{1,0},{2,3},{3,2},{4,5},{5,4},{6,7},{7,6},{8,9},{9,8},{10,11... | collective-permute-start | bytes 786440 | tf_op jit(solution)/shard_map/ppermute | solution.py:143
  67.0 2.4 %collective-permute-start.9 = (bf16[768,512]{1,0:T(8,128)(2,1)S(1)}, bf16[768,512]{1,0:T(8,128)(2,1)S(1)}, u32[]{:S(2)}, u32[]{:S(2)}) collective-permute-start(bf16[768,512]{1,0:T(8,128)(2,1)S(1)} %fusion.15), channel_id=1, source_target_pairs={{0,1},{1,0},{2,3},{3,2},{4,5},{5,4},{6,7},{7,6},{8,9},{9,8},{10,11... | collective-permute-start | bytes 2359304 | tf_op jit(solution)/shard_map/ppermute | solution.py:143
  68.0 9.0 %collective-permute-start.10 = (bf16[256,512]{1,0:T(8,128)(2,1)S(1)}, bf16[256,512]{1,0:T(8,128)(2,1)S(1)}, u32[]{:S(2)}, u32[]{:S(2)}) collective-permute-start(bf16[256,512]{1,0:T(8,128)(2,1)S(1)} %fusion.22), channel_id=1, source_target_pairs={{0,4},{2,6},{4,0},{6,2},{1,5},{3,7},{5,1},{7,3},{8,12},{10,14},{12... | collective-permute-start | bytes 786440 | tf_op jit(solution)/shard_map/ppermute | solution.py:139
  71.8 11.7 %collective-permute-start.11 = (bf16[256,512]{1,0:T(8,128)(2,1)S(1)}, bf16[256,512]{1,0:T(8,128)(2,1)S(1)}, u32[]{:S(2)}, u32[]{:S(2)}) collective-permute-start(bf16[256,512]{1,0:T(8,128)(2,1)S(1)} %get-tuple-element.84), channel_id=1, source_target_pairs={{0,2},{2,4},{4,6},{6,0},{1,3},{3,5},{5,7},{7,1},{8,10},{10,12},{12... | collective-permute-start | bytes 786440 | tf_op jit(solution)/shard_map/ppermute | solution.py:139
  72.7 10.8 %collective-permute-start.12 = (bf16[256,512]{1,0:T(8,128)(2,1)S(1)}, bf16[256,512]{1,0:T(8,128)(2,1)S(1)}, u32[]{:S(2)}, u32[]{:S(2)}) collective-permute-start(bf16[256,512]{1,0:T(8,128)(2,1)S(1)} %get-tuple-element.85), channel_id=1, source_target_pairs={{0,6},{2,0},{4,2},{6,4},{1,7},{3,1},{5,3},{7,5},{8,14},{10,8},{12,... | collective-permute-start | bytes 786440 | tf_op jit(solution)/shard_map/ppermute | solution.py:139
  101.1 5.4 %collective-permute-start.13 = (bf16[256,256]{1,0:T(8,128)(2,1)S(1)}, bf16[256,256]{1,0:T(8,128)(2,1)S(1)}, u32[]{:S(2)}, u32[]{:S(2)}) collective-permute-start(bf16[256,256]{1,0:T(8,128)(2,1)S(1)} %convolution_convert_fusion), channel_id=1, source_target_pairs={{0,4},{2,6},{4,0},{6,2},{1,5},{3,7},{5,1},{7,3},{8,12},{10,14},{12... | collective-permute-start | bytes 393224 | tf_op jit(solution)/shard_map/ppermute | solution.py:139
  101.2 5.5 %collective-permute-start.14 = (bf16[256,256]{1,0:T(8,128)(2,1)S(1)}, bf16[256,256]{1,0:T(8,128)(2,1)S(1)}, u32[]{:S(2)}, u32[]{:S(2)}) collective-permute-start(bf16[256,256]{1,0:T(8,128)(2,1)S(1)} %convolution_convert_fusion), channel_id=1, source_target_pairs={{0,6},{2,0},{4,2},{6,4},{1,7},{3,1},{5,3},{7,5},{8,14},{10,8},{12,... | collective-permute-start | bytes 393224 | tf_op jit(solution)/shard_map/ppermute | solution.py:139
  102.5 5.4 %collective-permute-start.15 = (bf16[256,256]{1,0:T(8,128)(2,1)S(1)}, bf16[256,256]{1,0:T(8,128)(2,1)S(1)}, u32[]{:S(2)}, u32[]{:S(2)}) collective-permute-start(bf16[256,256]{1,0:T(8,128)(2,1)S(1)} %convolution_convert_fusion), channel_id=1, source_target_pairs={{0,2},{2,4},{4,6},{6,0},{1,3},{3,5},{5,7},{7,1},{8,10},{10,12},{12... | collective-permute-start | bytes 393224 | tf_op jit(solution)/shard_map/ppermute | solution.py:139
  108.0 6.5 %collective-permute-start.16 = (bf16[4,256,256]{2,1,0:T(8,128)(2,1)S(1)}, bf16[4,256,256]{2,1,0:T(8,128)(2,1)S(1)}, u32[]{:S(2)}, u32[]{:S(2)}) collective-permute-start(bf16[4,256,256]{2,1,0:T(8,128)(2,1)S(1)} %pad_maximum_fusion.4), channel_id=1, source_target_pairs={{0,1},{1,0},{2,3},{3,2},{4,5},{5,4},{6,7},{7,6},{8,9},{9,8},{10,11... | collective-permute-start | bytes 1572872 | tf_op jit(solution)/shard_map/ppermute | solution.py:143
  114.6 1.0 copy-start

commit v8 on v7

--- a/solution.py
+++ b/solution.py
@@ -53,7 +53,7 @@
     hbm = pl.BlockSpec(memory_space=pltpu.HBM)
     return pl.pallas_call(
         dispatch_kernel,
-        out_shape=[jax.ShapeDtypeStruct((slots, count), BF16), jax.ShapeDtypeStruct((slots, 2 * width), BF16)],
+        out_shape=[jax.ShapeDtypeStruct((slots, count), BF16), pltpu.VMEM((slots, 2 * width), BF16)],
         in_specs=[hbm, hbm, hbm],
         out_specs=[vmem, vmem],
         scratch_shapes=[

time: 116 us -> 116 us (level)
  no operation moved by 1% of the time
where the time goes in v8:
time: 116 us
  blocking collectives  42.9 us (37%)
  starting transfers between devices  24.6 us (21%)
  waiting for transfers between devices  19.4 us (17%)
  matrix products  16.8 us (14%)
  Pallas kernels  5.71 us (5%)
  local copies, waits for them, and re-layouts  2.31 us (2%)
  other arithmetic  2.2 us (2%)
  between operations  1.65 us (1%)
    all_to_all x2, blocking collectives, exchange(): lax.all_to_all(value, EXPERT, split_axis=0, concat_axis=0, tiled=True)  42.9 us
    ppermute x10, waiting for transfers between devices, shift_y(): lax.ppermute(value, 'y', [(i, (i + shift) % count) for i in range(count)])  16.8 us
    dot_general x11, matrix products, dot(): lax.dot_general(a, b, (((ca,), (cb,)), ((), ())), preferred_element_type=...  16.8 us
    ppermute x7, starting transfers between devices, swap_cores(): return lax.ppermute(value, 'c', SWAP)  15.5 us
    ppermute x10, starting transfers between devices, shift_y(): lax.ppermute(value, 'y', [(i, (i + shift) % count) for i in range(count)])  9.18 us
    pallas_call x1, Pallas kernels, stage_weights(): pl.pallas_call(stage_kernel, out_shape=[jax.ShapeDtypeStruct((model, 3 *...  4.4 us
    ppermute x7, waiting for transfers between devices, swap_cores(): return lax.ppermute(value, 'c', SWAP)  2.53 us
  transfers between devices with their start and end apart: 17, of which 10 were waited for; matrix products, arithmetic and copies ran while one was open for 13% of the time, Pallas kernels for 4%

profile of v8, /device:TPU:1, one launch (start us, length us, event | category | flops | bytes accessed | tf_op | source)
XLA Modules:
  0.0 115.6 jit_solution(6465603219807956875)
XLA Ops:
  0.6 1.3 %dispatch.1 = (bf16[512,256]{1,0:T(8,128)(2,1)S(1)}, bf16[512,512]{1,0:T(8,128)(2,1)S(1)}) custom-call(s32[1,256]{1,0:T(1,128)} %bitcast.50, bf16[256,2048]{1,0:T(8,128)(2,1)} %tokens_ref.1, bf16[256,2048]{1,0:T(8,128)(2,1)} %cot_ref.1), custom_call_target="tpu_custom_call" | custom-call | tf_op jit(solution)/shard_map/dispatch/pallas_call | solution.py:54
  2.0 26.0 %all_to_all.10 = bf16[32,16,512]{2,1,0:T(8,128)(2,1)S(1)} all-to-all(bf16[32,16,512]{2,1,0:T(8,128)(2,1)S(1)} %bitcast.39), channel_id=1, replica_groups=mesh['x'=4,'z'=8,'y'=4,'c'=2] {'x','z'}, dimensions={0} | all-to-all | bytes 1048576 | tf_op jit(solution)/shard_map/all_to_all | solution.py:147
  27.9 2.7 %collective-permute-start = (bf16[512,512]{0,1:T(8,128)(2,1)S(1)}, bf16[512,512]{0,1:T(8,128)(2,1)S(1)}, u32[]{:S(2)}, u32[]{:S(2)}) collective-permute-start(bf16[512,512]{0,1:T(8,128)(2,1)S(1)} %bitcast.40), channel_id=1, source_target_pairs={{0,6},{2,0},{4,2},{6,4},{1,7},{3,1},{5,3},{7,5},{8,14},{10,8},{12,... | collective-permute-start | bytes 1572872 | tf_op jit(solution)/shard_map/ppermute | solution.py:139
  30.7 3.8 %collective-permute-start.2 = (bf16[512,512]{0,1:T(8,128)(2,1)S(1)}, bf16[512,512]{0,1:T(8,128)(2,1)S(1)}, u32[]{:S(2)}, u32[]{:S(2)}) collective-permute-start(bf16[512,512]{0,1:T(8,128)(2,1)S(1)} %bitcast.42), channel_id=1, source_target_pairs={{0,1},{1,0},{2,3},{3,2},{4,5},{5,4},{6,7},{7,6},{8,9},{9,8},{10,11... | collective-permute-start | bytes 1572872 | tf_op jit(solution)/shard_map/ppermute | solution.py:143
  35.1 4.4 %stage_weights.1 = (bf16[2048,2688]{1,0:T(8,128)(2,1)S(1)}, bf16[896,2048]{1,0:T(8,128)(2,1)S(1)}) custom-call(s32[1]{0:T(128)S(6)} %copy.31.seed_ref, bf16[1,2048,896]{2,1,0:T(8,128)(2,1)} %gate_ref.1, bf16[1,2048,896]{2,1,0:T(8,128)(2,1)} %up_ref.1, bf16[1,896,2048]{2,1,0:T(8,128)(2,1)} %down_ref.1), custom_call_target="tpu_custom_call" | custom-call | bytes 25690112 | tf_op jit(solution)/shard_map/stage_weights/pallas_call | solution.py:121
  39.5 2.0 %collective-permute-done.1 = bf16[512,512]{0,1:T(8,128)(2,1)S(1)} collective-permute-done((bf16[512,512]{0,1:T(8,128)(2,1)S(1)}, bf16[512,512]{0,1:T(8,128)(2,1)S(1)}, u32[]{:S(2)}, u32[]{:S(2)}) %collective-permute-start.1) | collective-permute-done | bytes 524320 | tf_op jit(solution)/shard_map/ppermute | solution.py:139
  41.5 0.1 pad_maximum_fusion.1
  41.6 4.8 %collective-permute-start.3 = (bf16[1024,512]{0,1:T(8,128)(2,1)S(1)}, bf16[1024,512]{0,1:T(8,128)(2,1)S(1)}, u32[]{:S(2)}, u32[]{:S(2)}) collective-permute-start(bf16[1024,512]{0,1:T(8,128)(2,1)S(1)} %pad_maximum_fusion.1), channel_id=1, source_target_pairs={{0,1},{1,0},{2,3},{3,2},{4,5},{5,4},{6,7},{7,6},{8,9},{9,8},{10,11... | collective-permute-start | bytes 3145736 | tf_op jit(solution)/shard_map/ppermute | solution.py:143
  46.6 1.5 %collective-permute-start.6 = (bf16[256,512]{0,1:T(8,128)(2,1)S(1)}, bf16[256,512]{0,1:T(8,128)(2,1)S(1)}, u32[]{:S(2)}, u32[]{:S(2)}) collective-permute-start(bf16[256,512]{0,1:T(8,128)(2,1)S(1)} %get-tuple-element.51), channel_id=1, source_target_pairs={{0,2},{2,4},{4,6},{6,0},{1,3},{3,5},{5,7},{7,1},{8,10},{10,12},{12... | collective-permute-start | bytes 786440 | tf_op jit(solution)/shard_map/ppermute | solution.py:139
  48.2 0.5 collective-permute-done.3
  48.9 4.5 %fusion = f32[2688,512]{1,0:T(8,128)S(1)} fusion(bf16[1536,512]{0,1:T(8,128)(2,1)S(1)} %get-tuple-element.90, bf16[2048,2688]{1,0:T(8,128)(2,1)S(1)} %get-tuple-element.43), kind=kOutput, calls=%fused_computation | convolution fusion | flops 4227858432 | bytes 15335424 | tf_op jit(solution)/shard_map/dot_general | solution.py:134
  53.4 1.1 collective-permute-done.4
  54.5 1.1 collective-permute-start.5
  55.7 1.6 %fusion.6 = f32[896,512]{1,0:T(8,128)S(1)} fusion(bf16[1536,512]{0,1:T(8,128)(2,1)S(1)} %constant_dynamic-update-slice_fusion.1, bf16[896,2048]{1,0:T(8,128)(2,1)S(1)} %get-tuple-element.49), kind=kOutput, calls=%fused_computation.7 | convolution fusion | flops 1409286144 | bytes 6160384 | tf_op jit(solution)/shard_map/dot_general | solution.py:134
  57.4 0.7 slice_add_fusion.1
  58.1 0.7 slice_add_fusion.2
  58.8 0.1 collective-permute-start.7
  58.9 1.7 %fusion.52 = (f32[896,512]{1,0:T(8,128)S(1)}, f32[896,512]{1,0:T(8,128)S(1)}, f32[896,512]{1,0:T(8,128)S(1)}, f32[896,512]{1,0:T(8,128)S(1)}) fusion(f32[896,512]{1,0:T(8,128)S(1)} %slice_add_fusion.2, f32[896,512]{1,0:T(8,128)S(1)} %slice_add_fusion.1, bf16[512,512]{0,1:T(8,128)(2,1)S(1)} %pad_maximum_fusion.2, ...), kind=kOutput, calls=%fused_computation.76 | convolution fusion | flops 478478336 | bytes 14286848 | tf_op jit(solution)/shard_map/dot_general | solution.py:134
  60.7 0.7 fusion.40
  61.3 0.5 multiply_reduce_fusion
  61.9 1.0 multiply_convert_fusion.2
  62.9 0.2 pad_maximum_fusion
  63.1 0.9 fusion.25
  64.0 0.6 collective-permute-start.8
  64.6 2.4 %fusion.15 = bf16[768,512]{1,0:T(8,128)(2,1)S(1)} fusion(bf16[2688,512]{1,0:T(8,128)(2,1)S(1)} %pad_maximum_fusion, bf16[2048,2688]{1,0:T(8,128)(2,1)S(1)} %get-tuple-element.43), kind=kOutput, calls=%fused_computation.25 | convolution fusion | flops 2114322432 | bytes 7667712 | tf_op jit(solution)/shard_map/dot_general | solution.py:134
  67.0 0.1 collective-permute-start.9
  67.1 0.9 fusion.22
  68.0 0.1 collective-permute-start.10
  68.1 1.2 %collective-permute-done.9 = bf16[768,512]{1,0:T(8,128)(2,1)S(1)} collective-permute-done((bf16[768,512]{1,0:T(8,128)(2,1)S(1)}, bf16[768,512]{1,0:T(8,128)(2,1)S(1)}, u32[]{:S(2)}, u32[]{:S(2)}) %collective-permute-start.9) | collective-permute-done | bytes 786464 | tf_op jit(solution)/shard_map/ppermute | solution.py:143
  69.4 2.4 %fusion.60 = (bf16[768,512]{1,0:T(8,128)(2,1)S(1)}, f32[768,512]{1,0:T(8,128)S(1)}) fusion(bf16[768,512]{1,0:T(8,128)(2,1)S(1)} %collective-permute-done.9, bf16[2688,512]{1,0:T(8,128)(2,1)S(1)} %pad_maximum_fusion, bf16[2048,2688]{1,0:T(8,128)(2,1)S(1)} %get-tuple-element.43), kind=kOutput, calls=%fused_computation.83 | convolution fusion | flops 2115108864 | bytes 10027008 | tf_op jit(solution)/shard_map/dot_general | solution.py:134
  71.8 0.8 collective-permute-start.11
  72.7 2.1 %collective-permute-start.12 = (bf16[256,512]{1,0:T(8,128)(2,1)S(1)}, bf16[256,512]{1,0:T(8,128)(2,1)S(1)}, u32[]{:S(2)}, u32[]{:S(2)}) collective-permute-start(bf16[256,512]{1,0:T(8,128)(2,1)S(1)} %get-tuple-element.85), channel_id=1, source_target_pairs={{0,6},{2,0},{4,2},{6,4},{1,7},{3,1},{5,3},{7,5},{8,14},{10,8},{12,... | collective-permute-start | bytes 786440 | tf_op jit(solution)/shard_map/ppermute | solution.py:139
  74.8 2.2 %collective-permute-done.10 = bf16[256,512]{1,0:T(8,128)(2,1)S(1)} collective-permute-done((bf16[256,512]{1,0:T(8,128)(2,1)S(1)}, bf16[256,512]{1,0:T(8,128)(2,1)S(1)}, u32[]{:S(2)}, u32[]{:S(2)}) %collective-permute-start.10) | collective-permute-done | bytes 262176 | tf_op jit(solution)/shard_map/ppermute | solution.py:139
  77.0 6.5 %collective-permute-done.11 = bf16[256,512]{1,0:T(8,128)(2,1)S(1)} collective-permute-done((bf16[256,512]{1,0:T(8,128)(2,1)S(1)}, bf16[256,512]{1,0:T(8,128)(2,1)S(1)}, u32[]{:S(2)}, u32[]{:S(2)}) %collective-permute-start.11) | collective-permute-done | bytes 262176 | tf_op jit(solution)/shard_map/ppermute | solution.py:139
  83.5 0.2 fusion.45
  83.7 0.1 copy.11
  83.8 17.0 %all_to_all.11 = bf16[32,16,256]{2,1,0:T(8,128)(2,1)S(1)} all-to-all(bf16[32,16,256]{2,1,0:T(8,128)(2,1)S(1)} %bitcast.46), channel_id=1, replica_groups=mesh['x'=4,'z'=8,'y'=4,'c'=2] {'x','z'}, dimensions={0} | all-to-all | bytes 524288 | tf_op jit(solution)/shard_map/all_to_all | solution.py:147
  100.8 0.3 convolution_convert_fusion
  101.2 1.3 %collective-permute-start.14 = (bf16[256,256]{1,0:T(8,128)(2,1)S(1)}, bf16[256,256]{1,0:T(8,128)(2,1)S(1)}, u32[]{:S(2)}, u32[]{:S(2)}) collective-permute-start(bf16[256,256]{1,0:T(8,128)(2,1)S(1)} %convolution_convert_fusion), channel_id=1, source_target_pairs={{0,6},{2,0},{4,2},{6,4},{1,7},{3,1},{5,3},{7,5},{8,14},{10,8},{12,... | collective-permute-start | bytes 393224 | tf_op jit(solution)/shard_map/ppermute | solution.py:139
  102.5 0.4 collective-permute-start.15
  102.9 3.7 %collective-permute-done.13 = bf16[256,256]{1,0:T(8,128)(2,1)S(1)} collective-permute-done((bf16[256,256]{1,0:T(8,128)(2,1)S(1)}, bf16[256,256]{1,0:T(8,128)(2,1)S(1)}, u32[]{:S(2)}, u32[]{:S(2)}) %collective-permute-start.13) | collective-permute-done | bytes 131104 | tf_op jit(solution)/shard_map/ppermute | solution.py:139
  106.5 0.1 collective-permute-done.14
  106.7 1.2 %collective-permute-done.15 = bf16[256,256]{1,0:T(8,128)(2,1)S(1)} collective-permute-done((bf16[256,256]{1,0:T(8,128)(2,1)S(1)}, bf16[256,256]{1,0:T(8,128)(2,1)S(1)}, u32[]{:S(2)}, u32[]{:S(2)}) %collective-permute-start.15) | collective-permute-done | bytes 131104 | tf_op jit(solution)/shard_map/ppermute | solution.py:139
  108.0 5.0 %collective-permute-start.16 = (bf16[4,256,256]{2,1,0:T(8,128)(2,1)S(1)}, bf16[4,256,256]{2,1,0:T(8,128)(2,1)S(1)}, u32[]{:S(2)}, u32[]{:S(2)}) collective-permute-start(bf16[4,256,256]{2,1,0:T(8,128)(2,1)S(1)} %pad_maximum_fusion.4), channel_id=1, source_target_pairs={{0,1},{1,0},{2,3},{3,2},{4,5},{5,4},{6,7},{7,6},{8,9},{9,8},{10,11... | collective-permute-start | bytes 1572872 | tf_op jit(solution)/shard_map/ppermute | solution.py:143
  113.0 0.6 broadcast_in_dim.7
  113.6 0.1 broadcast_in_dim.6
  113.8 0.7 collective-permute-done.16
  114.6 1.0 copy-done
  (35 shorter events, 0.9 us)
Async XLA Ops:
  27.9 11.6 %collective-permute-start = (bf16[512,512]{0,1:T(8,128)(2,1)S(1)}, bf16[512,512]{0,1:T(8,128)(2,1)S(1)}, u32[]{:S(2)}, u32[]{:S(2)}) collective-permute-start(bf16[512,512]{0,1:T(8,128)(2,1)S(1)} %bitcast.40), channel_id=1, source_target_pairs={{0,6},{2,0},{4,2},{6,4},{1,7},{3,1},{5,3},{7,5},{8,14},{10,8},{12,... | collective-permute-start | bytes 1572872 | tf_op jit(solution)/shard_map/ppermute | solution.py:139
  30.7 10.8 %collective-permute-start.1 = (bf16[512,512]{0,1:T(8,128)(2,1)S(1)}, bf16[512,512]{0,1:T(8,128)(2,1)S(1)}, u32[]{:S(2)}, u32[]{:S(2)}) collective-permute-start(bf16[512,512]{0,1:T(8,128)(2,1)S(1)} %bitcast.41), channel_id=1, source_target_pairs={{0,2},{2,4},{4,6},{6,0},{1,3},{3,5},{5,7},{7,1},{8,10},{10,12},{12... | collective-permute-start | bytes 1572872 | tf_op jit(solution)/shard_map/ppermute | solution.py:139
  30.7 10.8 %collective-permute-start.2 = (bf16[512,512]{0,1:T(8,128)(2,1)S(1)}, bf16[512,512]{0,1:T(8,128)(2,1)S(1)}, u32[]{:S(2)}, u32[]{:S(2)}) collective-permute-start(bf16[512,512]{0,1:T(8,128)(2,1)S(1)} %bitcast.42), channel_id=1, source_target_pairs={{0,1},{1,0},{2,3},{3,2},{4,5},{5,4},{6,7},{7,6},{8,9},{9,8},{10,11... | collective-permute-start | bytes 1572872 | tf_op jit(solution)/shard_map/ppermute | solution.py:143
  41.6 7.1 %collective-permute-start.3 = (bf16[1024,512]{0,1:T(8,128)(2,1)S(1)}, bf16[1024,512]{0,1:T(8,128)(2,1)S(1)}, u32[]{:S(2)}, u32[]{:S(2)}) collective-permute-start(bf16[1024,512]{0,1:T(8,128)(2,1)S(1)} %pad_maximum_fusion.1), channel_id=1, source_target_pairs={{0,1},{1,0},{2,3},{3,2},{4,5},{5,4},{6,7},{7,6},{8,9},{9,8},{10,11... | collective-permute-start | bytes 3145736 | tf_op jit(solution)/shard_map/ppermute | solution.py:143
  46.5 8.0 %collective-permute-start.4 = (bf16[256,512]{0,1:T(8,128)(2,1)S(1)}, bf16[256,512]{0,1:T(8,128)(2,1)S(1)}, u32[]{:S(2)}, u32[]{:S(2)}) collective-permute-start(bf16[256,512]{0,1:T(8,128)(2,1)S(1)} %get-tuple-element.86), channel_id=1, source_target_pairs={{0,6},{2,0},{4,2},{6,4},{1,7},{3,1},{5,3},{7,5},{8,14},{10,8},{12,... | collective-permute-start | bytes 786440 | tf_op jit(solution)/shard_map/ppermute | solution.py:139
  46.6 10.8 %collective-permute-start.6 = (bf16[256,512]{0,1:T(8,128)(2,1)S(1)}, bf16[256,512]{0,1:T(8,128)(2,1)S(1)}, u32[]{:S(2)}, u32[]{:S(2)}) collective-permute-start(bf16[256,512]{0,1:T(8,128)(2,1)S(1)} %get-tuple-element.51), channel_id=1, source_target_pairs={{0,2},{2,4},{4,6},{6,0},{1,3},{3,5},{5,7},{7,1},{8,10},{10,12},{12... | collective-permute-start | bytes 786440 | tf_op jit(solution)/shard_map/ppermute | solution.py:139
  54.5 2.8 %collective-permute-start.5 = (bf16[256,512]{0,1:T(8,128)(2,1)S(1)}, bf16[256,512]{0,1:T(8,128)(2,1)S(1)}, u32[]{:S(2)}, u32[]{:S(2)}) collective-permute-start(bf16[256,512]{0,1:T(8,128)(2,1)S(1)} %collective-permute-done.4), channel_id=1, source_target_pairs={{0,1},{1,0},{2,3},{3,2},{4,5},{5,4},{6,7},{7,6},{8,9},{9,8},{10,11... | collective-permute-start | bytes 786440 | tf_op jit(solution)/shard_map/ppermute | solution.py:143
  58.8 1.8 %collective-permute-start.7 = (bf16[256,512]{0,1:T(8,128)(2,1)S(1)}, bf16[256,512]{0,1:T(8,128)(2,1)S(1)}, u32[]{:S(2)}, u32[]{:S(2)}) collective-permute-start(bf16[256,512]{0,1:T(8,128)(2,1)S(1)} %collective-permute-done.6), channel_id=1, source_target_pairs={{0,1},{1,0},{2,3},{3,2},{4,5},{5,4},{6,7},{7,6},{8,9},{9,8},{10,11... | collective-permute-start | bytes 786440 | tf_op jit(solution)/shard_map/ppermute | solution.py:143
  64.0 3.0 %collective-permute-start.8 = (bf16[256,512]{1,0:T(8,128)(2,1)S(1)}, bf16[256,512]{1,0:T(8,128)(2,1)S(1)}, u32[]{:S(2)}, u32[]{:S(2)}) collective-permute-start(bf16[256,512]{1,0:T(8,128)(2,1)S(1)} %fusion.25), channel_id=1, source_target_pairs={{0,1},{1,0},{2,3},{3,2},{4,5},{5,4},{6,7},{7,6},{8,9},{9,8},{10,11... | collective-permute-start | bytes 786440 | tf_op jit(solution)/shard_map/ppermute | solution.py:143
  67.0 2.4 %collective-permute-start.9 = (bf16[768,512]{1,0:T(8,128)(2,1)S(1)}, bf16[768,512]{1,0:T(8,128)(2,1)S(1)}, u32[]{:S(2)}, u32[]{:S(2)}) collective-permute-start(bf16[768,512]{1,0:T(8,128)(2,1)S(1)} %fusion.15), channel_id=1, source_target_pairs={{0,1},{1,0},{2,3},{3,2},{4,5},{5,4},{6,7},{7,6},{8,9},{9,8},{10,11... | collective-permute-start | bytes 2359304 | tf_op jit(solution)/shard_map/ppermute | solution.py:143
  68.0 9.0 %collective-permute-start.10 = (bf16[256,512]{1,0:T(8,128)(2,1)S(1)}, bf16[256,512]{1,0:T(8,128)(2,1)S(1)}, u32[]{:S(2)}, u32[]{:S(2)}) collective-permute-start(bf16[256,512]{1,0:T(8,128)(2,1)S(1)} %fusion.22), channel_id=1, source_target_pairs={{0,4},{2,6},{4,0},{6,2},{1,5},{3,7},{5,1},{7,3},{8,12},{10,14},{12... | collective-permute-start | bytes 786440 | tf_op jit(solution)/shard_map/ppermute | solution.py:139
  71.8 11.7 %collective-permute-start.11 = (bf16[256,512]{1,0:T(8,128)(2,1)S(1)}, bf16[256,512]{1,0:T(8,128)(2,1)S(1)}, u32[]{:S(2)}, u32[]{:S(2)}) collective-permute-start(bf16[256,512]{1,0:T(8,128)(2,1)S(1)} %get-tuple-element.84), channel_id=1, source_target_pairs={{0,2},{2,4},{4,6},{6,0},{1,3},{3,5},{5,7},{7,1},{8,10},{10,12},{12... | collective-permute-start | bytes 786440 | tf_op jit(solution)/shard_map/ppermute | solution.py:139
  72.7 10.8 %collective-permute-start.12 = (bf16[256,512]{1,0:T(8,128)(2,1)S(1)}, bf16[256,512]{1,0:T(8,128)(2,1)S(1)}, u32[]{:S(2)}, u32[]{:S(2)}) collective-permute-start(bf16[256,512]{1,0:T(8,128)(2,1)S(1)} %get-tuple-element.85), channel_id=1, source_target_pairs={{0,6},{2,0},{4,2},{6,4},{1,7},{3,1},{5,3},{7,5},{8,14},{10,8},{12,... | collective-permute-start | bytes 786440 | tf_op jit(solution)/shard_map/ppermute | solution.py:139
  101.1 5.4 %collective-permute-start.13 = (bf16[256,256]{1,0:T(8,128)(2,1)S(1)}, bf16[256,256]{1,0:T(8,128)(2,1)S(1)}, u32[]{:S(2)}, u32[]{:S(2)}) collective-permute-start(bf16[256,256]{1,0:T(8,128)(2,1)S(1)} %convolution_convert_fusion), channel_id=1, source_target_pairs={{0,4},{2,6},{4,0},{6,2},{1,5},{3,7},{5,1},{7,3},{8,12},{10,14},{12... | collective-permute-start | bytes 393224 | tf_op jit(solution)/shard_map/ppermute | solution.py:139
  101.2 5.5 %collective-permute-start.14 = (bf16[256,256]{1,0:T(8,128)(2,1)S(1)}, bf16[256,256]{1,0:T(8,128)(2,1)S(1)}, u32[]{:S(2)}, u32[]{:S(2)}) collective-permute-start(bf16[256,256]{1,0:T(8,128)(2,1)S(1)} %convolution_convert_fusion), channel_id=1, source_target_pairs={{0,6},{2,0},{4,2},{6,4},{1,7},{3,1},{5,3},{7,5},{8,14},{10,8},{12,... | collective-permute-start | bytes 393224 | tf_op jit(solution)/shard_map/ppermute | solution.py:139
  102.5 5.4 %collective-permute-start.15 = (bf16[256,256]{1,0:T(8,128)(2,1)S(1)}, bf16[256,256]{1,0:T(8,128)(2,1)S(1)}, u32[]{:S(2)}, u32[]{:S(2)}) collective-permute-start(bf16[256,256]{1,0:T(8,128)(2,1)S(1)} %convolution_convert_fusion), channel_id=1, source_target_pairs={{0,2},{2,4},{4,6},{6,0},{1,3},{3,5},{5,7},{7,1},{8,10},{10,12},{12... | collective-permute-start | bytes 393224 | tf_op jit(solution)/shard_map/ppermute | solution.py:139
  108.0 6.5 %collective-permute-start.16 = (bf16[4,256,256]{2,1,0:T(8,128)(2,1)S(1)}, bf16[4,256,256]{2,1,0:T(8,128)(2,1)S(1)}, u32[]{:S(2)}, u32[]{:S(2)}) collective-permute-start(bf16[4,256,256]{2,1,0:T(8,128)(2,1)S(1)} %pad_maximum_fusion.4), channel_id=1, source_target_pairs={{0,1},{1,0},{2,3},{3,2},{4,5},{5,4},{6,7},{7,6},{8,9},{9,8},{10,11... | collective-permute-start | bytes 1572872 | tf_op jit(solution)/shard_map/ppermute | solution.py:143
  114.6 1.0 copy-start
